TPU v7x, 512 devices: a whole 4x4x16 slice. The times are simulated.
512 devices in a mesh: seq: 64 (over y, z), chan: 8 (over x, core).
Axes of the slice: x: 4, y: 4, z: 16, core: 2. Of those that a mesh axis runs over, the one named last changes fastest.
Arguments:
- x1: bfloat16 [8192, 4096], P('seq', 'chan'), may hold values from -6 to 6
- x2: bfloat16 [8192, 4096], P('seq', 'chan'), may hold values from -6 to 6
- value: bfloat16 [8192, 4096], P('seq', 'chan'), may hold values from -6 to 6
- out_grad: bfloat16 [8192, 4096], P('seq', 'chan'), may hold values from -6 to 6
- short_weight: float32 [3, 4096], P(None, 'chan'), may hold values from -3.5 to 3.5
- coef: float32 [64, 4096], P(None, 'chan'), may hold values from -0.75 to 0.75
- rate: float32 [64], replicated, may hold values from 0.2 to 273.06667, as said below
Outputs:
- layer_output: bfloat16 [8192, 4096], P('seq', 'chan')
- grad_x1: bfloat16 [8192, 4096], P('seq', 'chan')
- grad_value: bfloat16 [8192, 4096], P('seq', 'chan')
- grad_coef: float32 [64, 4096], P(None, 'chan')
- grad_rate: float32 [64], replicated
Inputs may be any that keep to these rules, and one draw needn't show every extreme that they name: `rate`: decay rates of the basis functions, per 8192 positions.
All inputs are finite; a program needn't handle non-finite values.
Results may differ from a plain program's by a relative error of at most 0.011.
Values may be sent and summed in bfloat16 or wider, within the bound.
No kernel may reach another device: no remote copies, remote signals or barrier semaphores. Data moves between devices by JAX's collectives and lax.ppermute only.
A program may use at most 64 MiB of HBM per device.

v0:
```python
import math

import jax
import jax.numpy as jnp
from jax import lax
from jax.sharding import PartitionSpec as P

highest = lax.Precision.HIGHEST


def from_behind(shard, axis, by):
    peers = lax.axis_size(axis)
    pairs = [(i, i + by) for i in range(peers) if 0 <= i + by < peers]
    return lax.ppermute(shard, axis, pairs)


def angles(index, period):
    return 2.0 * math.pi / period * (index % period).astype(jnp.float32)


def basis_pair(rate, start, count, length):
    position = start + jnp.arange(count, dtype=jnp.int32)
    index = jnp.arange(rate.shape[0], dtype=jnp.int32)
    cycles = (index // 2 + 1) * (index // 2 + 1)
    turned = position[:, None] * cycles[None, :] % length
    angle = 2.0 * math.pi / length * turned.astype(jnp.float32)
    wave = jnp.where(index[None, :] % 2 == 0, jnp.cos(angle), jnp.sin(angle))
    scaled = position.astype(jnp.float32)[:, None] / length
    envelope = jnp.sqrt(2.0 * rate / length)[None, :] * jnp.exp(-rate[None, :] * scaled)
    phi = envelope * wave
    psi = (0.5 / rate[None, :] - scaled) * phi
    return (phi, psi)


def row_tables(rows):
    every = jnp.arange(rows, dtype=jnp.int32)
    angle = angles(every[:, None] * every[None, :], rows)
    return (jnp.cos(angle), jnp.sin(angle))


def forward_transform(columns):
    shards = lax.axis_size("seq")
    place = lax.axis_index("seq")
    rows = columns.shape[0]
    slab = rows // shards
    width = columns.shape[1]
    received = lax.all_to_all(
        columns.reshape(shards, slab, width), "seq", split_axis=0, concat_axis=0, tiled=True
    )
    flat = received.reshape(shards, slab * width)
    freq_low = jnp.arange(2 * shards, dtype=jnp.int32)
    sources = jnp.arange(shards, dtype=jnp.int32)
    first = angles(freq_low[:, None] * sources[None, :], 2 * shards)
    real_a = jnp.dot(jnp.cos(first), flat, precision=highest).reshape(2 * shards, slab, width)
    imag_a = -jnp.dot(jnp.sin(first), flat, precision=highest).reshape(2 * shards, slab, width)
    local_rows = place * slab + jnp.arange(slab, dtype=jnp.int32)
    twist = angles(freq_low[:, None] * local_rows[None, :], 2 * shards * rows)
    cos_t = jnp.cos(twist)[:, :, None]
    sin_t = jnp.sin(twist)[:, :, None]
    real_b = real_a * cos_t + imag_a * sin_t
    imag_b = imag_a * cos_t - real_a * sin_t
    gathered = lax.all_to_all(
        jnp.stack([real_b, imag_b]), "seq", split_axis=1, concat_axis=2, tiled=True
    )
    cos_m, sin_m = row_tables(rows)
    real_x = jnp.einsum("fm,rmk->rfk", cos_m, gathered[0], precision=highest) + jnp.einsum(
        "fm,rmk->rfk", sin_m, gathered[1], precision=highest
    )
    imag_x = jnp.einsum("fm,rmk->rfk", cos_m, gathered[1], precision=highest) - jnp.einsum(
        "fm,rmk->rfk", sin_m, gathered[0], precision=highest
    )
    return (real_x, imag_x)


def inverse_transform(real_x, imag_x):
    shards = lax.axis_size("seq")
    place = lax.axis_index("seq")
    rows = real_x.shape[1]
    slab = rows // shards
    width = real_x.shape[2]
    total = 2 * shards * rows
    cos_m, sin_m = row_tables(rows)
    real_b = jnp.einsum("mf,rfk->rmk", cos_m, real_x, precision=highest) - jnp.einsum(
        "mf,rfk->rmk", sin_m, imag_x, precision=highest
    )
    imag_b = jnp.einsum("mf,rfk->rmk", cos_m, imag_x, precision=highest) + jnp.einsum(
        "mf,rfk->rmk", sin_m, real_x, precision=highest
    )
    freq_low = place * 2 + jnp.arange(2, dtype=jnp.int32)
    every = jnp.arange(rows, dtype=jnp.int32)
    twist = angles(freq_low[:, None] * every[None, :], total)
    cos_t = jnp.cos(twist)[:, :, None]
    sin_t = jnp.sin(twist)[:, :, None]
    real_c = real_b * cos_t - imag_b * sin_t
    imag_c = real_b * sin_t + imag_b * cos_t
    spread = lax.all_to_all(
        jnp.stack([real_c, imag_c]), "seq", split_axis=2, concat_axis=1, tiled=True
    )
    targets = jnp.arange(shards, dtype=jnp.int32)
    all_low = jnp.arange(2 * shards, dtype=jnp.int32)
    last = angles(targets[:, None] * all_low[None, :], 2 * shards)
    real_flat = spread[0].reshape(2 * shards, slab * width)
    imag_flat = spread[1].reshape(2 * shards, slab * width)
    signal = (
        jnp.dot(jnp.cos(last), real_flat, precision=highest)
        - jnp.dot(jnp.sin(last), imag_flat, precision=highest)
    ) / total
    returned = lax.all_to_all(
        signal.reshape(shards, slab, width), "seq", split_axis=0, concat_axis=1, tiled=True
    )
    return returned.reshape(rows, width)


def per_device(x1, x2, value, out_grad, short_weight, coef, rate):
    shards = lax.axis_size("seq")
    place = lax.axis_index("seq")
    rows = x1.shape[0]
    chans = x1.shape[1]
    length = rows * shards
    taps = short_weight.shape[0]
    prior = from_behind(value[rows - (taps - 1) :], "seq", 1)
    extended = jnp.concatenate([prior, value], axis=0).astype(jnp.float32)
    mixed = short_weight[0][None, :] * extended[taps - 1 : taps - 1 + rows]
    for shift_k in range(1, taps):
        mixed = (
            mixed
            + short_weight[shift_k][None, :]
            * extended[taps - 1 - shift_k : taps - 1 - shift_k + rows]
        )
    first = x1.astype(jnp.float32)
    second = x2.astype(jnp.float32)
    gated = (first * mixed).astype(jnp.bfloat16)
    grad_conv = (out_grad.astype(jnp.float32) * second).astype(jnp.bfloat16)
    phi, psi = basis_pair(rate, place * rows, rows, length)
    kernel = jnp.dot(phi, coef, precision=highest)
    columns = jnp.concatenate(
        [gated.astype(jnp.float32), grad_conv.astype(jnp.float32), kernel], axis=1
    )
    real_x, imag_x = forward_transform(columns)
    real_u, imag_u = (real_x[:, :, :chans], imag_x[:, :, :chans])
    real_d, imag_d = (real_x[:, :, chans : 2 * chans], imag_x[:, :, chans : 2 * chans])
    real_h, imag_h = (real_x[:, :, 2 * chans :], imag_x[:, :, 2 * chans :])
    real_z = real_u * real_h - imag_u * imag_h
    imag_z = real_u * imag_h + imag_u * real_h
    real_g = real_h * real_d + imag_h * imag_d
    imag_g = real_h * imag_d - imag_h * real_d
    real_f = real_u * real_d + imag_u * imag_d
    imag_f = real_u * imag_d - imag_u * real_d
    signals = inverse_transform(
        jnp.concatenate([real_z, real_g, real_f], axis=2),
        jnp.concatenate([imag_z, imag_g, imag_f], axis=2),
    )
    conv = signals[:, :chans]
    grad_gated = signals[:, chans : 2 * chans]
    grad_filter = signals[:, 2 * chans :]
    coef_part = jnp.dot(phi.T, grad_filter, precision=highest) * length ** (-0.5)
    rate_part = jnp.sum(psi * jnp.dot(grad_filter, coef.T, precision=highest), axis=0)
    grad_coef = lax.psum(coef_part, "seq")
    rate_sum = lax.psum(rate_part, ("seq", "chan"))
    grad_rate = rate_sum * (length * chans * lax.axis_size("chan")) ** (-0.5)
    out_y = (second * conv).astype(jnp.bfloat16)
    grad_x1 = (grad_gated * mixed).astype(jnp.bfloat16)
    grad_mixed = grad_gated * first
    later = from_behind(grad_mixed[: taps - 1], "seq", -1)
    tail = jnp.concatenate([grad_mixed, later], axis=0)
    back = short_weight[0][None, :] * tail[0:rows]
    for shift_k in range(1, taps):
        back = back + short_weight[shift_k][None, :] * tail[shift_k : shift_k + rows]
    grad_value = back.astype(jnp.bfloat16)
    return (out_y, grad_x1, grad_value, grad_coef, grad_rate)


def solution(mesh):
    return jax.shard_map(
        per_device,
        mesh=mesh,
        in_specs=(
            P("seq", "chan"),
            P("seq", "chan"),
            P("seq", "chan"),
            P("seq", "chan"),
            P(None, "chan"),
            P(None, "chan"),
            P(),
        ),
        out_specs=(P("seq", "chan"), P("seq", "chan"), P("seq", "chan"), P(None, "chan"), P()),
        check_vma=False,
    )
```

profile of v0, /device:TPU:24, one launch (start us, length us, event | category | flops | bytes accessed | tf_op | source)
XLA Modules:
  0.0 736.8 jit_solution(4605748889626512701)
XLA Ops:
  7.2 0.0 copy-start
  7.2 0.7 slice.79
  7.9 3.8 collective-permute-start
  11.8 1.2 broadcast_divide_fusion
  13.0 0.6 fusion.78
  13.6 0.8 fusion.155
  14.5 6.6 collective-permute-done
  21.0 0.9 maximum_convert_fusion
  22.0 1.2 fusion.24
  23.2 0.1 pad_maximum_fusion.8
  23.3 1.4 reshape.196
  24.6 12.3 %all-to-all-start = ((f32[64,2,1536]{2,1,0:T(2,128)}), f32[64,2,1536]{2,1,0:T(2,128)S(1)}, u32[]{:S(2)}, u32[]{:S(2)}) async-start(f32[64,2,1536]{2,1,0:T(2,128)} %reshape.196), calls=%async_computation | async-start | bytes 1572864 | tf_op jit(solution)/shard_map/all_to_all | solution.py:47
  36.9 0.5 copy-done.17
  37.4 0.1 fusion.91
  37.5 40.4 %all-to-all-done = f32[64,2,1536]{2,1,0:T(2,128)S(1)} async-done(((f32[64,2,1536]{2,1,0:T(2,128)}), f32[64,2,1536]{2,1,0:T(2,128)S(1)}, u32[]{:S(2)}, u32[]{:S(2)}) %all-to-all-start) | async-done | bytes 786464 | tf_op jit(solution)/shard_map/all_to_all | solution.py:47
  77.9 1.6 convolution_negate_fusion
  79.5 1.9 add_bitcast_fusion.1
  81.4 0.2 pad_maximum_fusion
  81.6 4.1 copy.26
  85.7 7.2 all-to-all-start.1
  92.9 11.9 %all-reduce.2.cloned.1.call-start = ((), (), s32[]{:S(2)}) async-start(), calls=%async_computation.4 | async-start | bytes 262144 | tf_op jit(solution)/shard_map/psum | solution.py:158
  104.8 1.3 fusion.89
  106.1 127.4 %all-to-all-done.1 = f32[2,128,2,1536]{3,2,0,1:T(2,128)S(1)} async-done(((f32[2,128,2,1536]{3,2,0,1:T(2,128)}), f32[2,128,2,1536]{3,2,0,1:T(2,128)S(1)}, u32[]{:S(2)}, u32[]{:S(2)}) %all-to-all-start.1) | async-done | bytes 3145760 | tf_op jit(solution)/shard_map/all_to_all | solution.py:62
  233.5 1.6 copy.56
  235.2 2.3 fusion.154
  237.4 0.7 copy.28
  238.2 2.8 fusion.37
  240.9 2.5 copy.29
  243.5 1.7 fusion.35
  245.2 1.7 fusion.1
  246.9 1.7 fusion.2
  248.7 0.2 multiply_add_fusion.2
  248.8 0.2 multiply_subtract_fusion.2
  249.0 1.7 fusion.5
  250.7 1.7 fusion.4
  252.4 0.0 copy-start.15
  252.4 1.7 convolution_add_fusion
  254.1 2.1 subtract_bitcast_fusion
  256.2 0.2 pad_maximum_fusion.1
  256.4 3.6 copy.32
  260.0 153.0 %all_to_all.44 = f32[2,2,128,1536]{3,1,0,2:T(2,128)S(1)} all-to-all(f32[2,2,128,1536]{3,1,0,2:T(2,128)} %copy.32), channel_id=1, replica_groups=mesh['seq'=64,'chan'=8] {'seq'}, dimensions={2} | all-to-all | bytes 6291456 | tf_op jit(solution)/shard_map/all_to_all | solution.py:96
  413.0 1.1 copy.33
  414.1 1.1 fusion.153
  415.2 0.8 copy.34
  416.0 0.3 copy.38
  416.3 1.1 fusion.68
  417.4 0.8 copy.35
  418.2 0.3 copy.39
  418.5 1.1 fusion
  419.6 0.7 reshape.198
  420.3 0.0 copy-start.2
  420.3 0.0 copy-start.3
  420.3 49.5 %all_to_all.45 = f32[64,2,1536]{2,1,0:T(2,128)S(1)} all-to-all(f32[64,2,1536]{2,1,0:T(2,128)S(1)} %reshape.198), channel_id=1, replica_groups=mesh['seq'=64,'chan'=8] {'seq'}, dimensions={0} | all-to-all | bytes 1572864 | tf_op jit(solution)/shard_map/all_to_all | solution.py:108
  469.8 0.5 reshape.199
  470.4 1.1 convolution_multiply_fusion
  471.6 0.8 convert_multiply_fusion
  472.4 1.9 collective-permute-start.1
  474.3 0.0 all-reduce.2.cloned.1.call-update
  474.3 0.5 fusion.3
  474.8 101.0 %psum.15 = f32[64]{0:T(128)S(1)} all-reduce(f32[64]{0:T(128)S(1)} %fusion.3), channel_id=1, replica_groups=mesh['seq'=64,'chan'=8] {'seq','chan'}, use_global_device_ids=true, to_apply=%region_2.3 | all-reduce | flops 64 | bytes 512 | tf_op jit(solution)/shard_map/psum | solution.py:159
  575.9 0.5 broadcast_multiply_fusion
  576.4 0.7 fusion.15
  577.1 150.9 %all-reduce.2.cloned.1.call-done = f32[64,512]{1,0:T(8,128)} async-done(((f32[64,512]{1,0:T(8,128)}), f32[64,512]{1,0:T(8,128)}) %all-reduce.2.cloned.1.call-update) | async-done | bytes 131088 | tf_op jit(solution)/shard_map/psum | solution.py:158
  728.0 1.6 copy.58
  (38 shorter events, 0.1 us)
Async XLA Ops:
  7.2 5.9 copy-start
  7.9 13.1 %collective-permute-start = (bf16[2,512]{1,0:T(2,128)(2,1)S(1)}, bf16[2,512]{1,0:T(2,128)(2,1)S(1)}, u32[]{:S(2)}, u32[]{:S(2)}) collective-permute-start(bf16[2,512]{1,0:T(2,128)(2,1)S(1)} %slice.79), channel_id=1, source_target_pairs={{0,8},{8,16},{16,24},{24,32},{32,40},{40,48},{48,56},{56,64},{64,7... | collective-permute-start | bytes 6152 | tf_op jit(solution)/shard_map/ppermute | solution.py:14
  11.8 11.5 %copy-start.6 = (f32[128]{0:T(128)}, f32[128]{0:T(128)S(1)}, u32[]{:S(2)}) copy-start(f32[128]{0:T(128)S(1)} %convert_multiply_fusion.4) | copy-start | bytes 1540
  11.8 11.5 %copy-start.8 = (s32[128]{0:T(128)}, s32[128]{0:T(128)S(1)}, u32[]{:S(2)}) copy-start(s32[128]{0:T(128)S(1)} %iota_add_fusion.1) | copy-start | bytes 1540
  11.8 11.4 %copy-start.10 = (pred[64]{0:T(512)(128)(4,1)}, pred[64]{0:T(512)(128)(4,1)S(1)}, u32[]{:S(2)}) copy-start(pred[64]{0:T(512)(128)(4,1)S(1)} %fusion.85) | copy-start | bytes 196
  11.8 11.4 %copy-start.12 = (s32[64]{0:T(128)}, s32[64]{0:T(128)S(1)}, u32[]{:S(2)}) copy-start(s32[64]{0:T(128)S(1)} %fusion.87) | copy-start | bytes 772
  13.0 10.3 %copy-start.4 = (f32[64]{0:T(128)}, f32[64]{0:T(128)S(1)}, u32[]{:S(2)}) copy-start(f32[64]{0:T(128)S(1)} %get-tuple-element.29) | copy-start | bytes 772
  24.6 53.3 %all-to-all-start = ((f32[64,2,1536]{2,1,0:T(2,128)}), f32[64,2,1536]{2,1,0:T(2,128)S(1)}, u32[]{:S(2)}, u32[]{:S(2)}) async-start(f32[64,2,1536]{2,1,0:T(2,128)} %reshape.196), calls=%async_computation | async-start | bytes 1572864 | tf_op jit(solution)/shard_map/all_to_all | solution.py:47
  36.9 0.5 copy-start.17
  85.7 147.9 %all-to-all-start.1 = ((f32[2,128,2,1536]{3,2,0,1:T(2,128)}), f32[2,128,2,1536]{3,2,0,1:T(2,128)S(1)}, u32[]{:S(2)}, u32[]{:S(2)}) async-start(f32[2,128,2,1536]{3,2,0,1:T(2,128)} %copy.26), calls=%async_computation.1 | async-start | bytes 6291456 | tf_op jit(solution)/shard_map/all_to_all | solution.py:62
  92.9 635.1 %all-reduce.2.cloned.1.call-start = ((), (), s32[]{:S(2)}) async-start(), calls=%async_computation.4 | async-start | bytes 262144 | tf_op jit(solution)/shard_map/psum | solution.py:158
  243.5 1.7 copy-start.1
  252.4 1.7 copy-start.14
  252.4 1.7 copy-start.15
  420.2 50.2 %copy-start.5 = (f32[64]{0:T(128)S(1)}, f32[64]{0:T(128)}, u32[]{:S(2)}) copy-start(f32[64]{0:T(128)} %copy-done.4) | copy-start | bytes 772
  420.2 50.2 %copy-start.7 = (f32[128]{0:T(128)S(1)}, f32[128]{0:T(128)}, u32[]{:S(2)}) copy-start(f32[128]{0:T(128)} %copy-done.6) | copy-start | bytes 1540
  420.2 50.2 %copy-start.9 = (s32[128]{0:T(128)S(1)}, s32[128]{0:T(128)}, u32[]{:S(2)}) copy-start(s32[128]{0:T(128)} %copy-done.8) | copy-start | bytes 1540
  420.3 50.2 %copy-start.11 = (pred[64]{0:T(512)(128)(4,1)S(1)}, pred[64]{0:T(512)(128)(4,1)}, u32[]{:S(2)}) copy-start(pred[64]{0:T(512)(128)(4,1)} %copy-done.10) | copy-start | bytes 196
  420.3 50.2 %copy-start.13 = (s32[64]{0:T(128)S(1)}, s32[64]{0:T(128)}, u32[]{:S(2)}) copy-start(s32[64]{0:T(128)} %copy-done.12) | copy-start | bytes 772
  420.3 51.3 %copy-start.2 = (bf16[128,512]{1,0:T(8,128)(2,1)S(1)}, bf16[128,512]{1,0:T(8,128)(2,1)}, u32[]{:S(2)}) copy-start(bf16[128,512]{1,0:T(8,128)(2,1)} %param.7) | copy-start | bytes 393220
  420.3 51.3 %copy-start.3 = (bf16[128,512]{1,0:T(8,128)(2,1)S(1)}, bf16[128,512]{1,0:T(8,128)(2,1)}, u32[]{:S(2)}) copy-start(bf16[128,512]{1,0:T(8,128)(2,1)} %param.8) | copy-start | bytes 393220
  469.8 4.5 copy-start.16
  472.4 104.0 %collective-permute-start.1 = (f32[2,512]{1,0:T(2,128)S(1)}, f32[2,512]{1,0:T(2,128)S(1)}, u32[]{:S(2)}, u32[]{:S(2)}) collective-permute-start(f32[2,512]{1,0:T(2,128)S(1)} %slice.116), channel_id=1, source_target_pairs={{8,0},{16,8},{24,16},{32,24},{40,32},{48,40},{56,48},{64,56},{72,6... | collective-permute-start | bytes 12296 | tf_op jit(solution)/shard_map/ppermute | solution.py:14
Sparse Core Ops, SparseCore 0:
  474.4 253.5 all-reduce.1
where the time goes:
time: 746 us; the launch traced here: 737 us
  waiting for transfers between devices  325 us (44%)
  blocking collectives  304 us (41%)
  starting transfers between devices  37.1 us (5%)
  local copies, waits for them, and re-layouts  25.4 us (3%)
  matrix products  22.9 us (3%)
  between operations  15 us (2%)
  other arithmetic  7.67 us (1%)
    all_to_all x1, blocking collectives, inverse_transform(): lax.all_to_all(jnp.stack([real_c, imag_c]), 'seq', split_axis=2, concat_a...  153 us
    psum x1, waiting for transfers between devices, per_device(): grad_coef = lax.psum(coef_part, 'seq')  151 us
    all_to_all x1, waiting for transfers between devices, forward_transform(): lax.all_to_all(jnp.stack([real_b, imag_b]), 'seq', split_axis=1, concat_a...  127 us
    psum x1, blocking collectives, per_device(): rate_sum = lax.psum(rate_part, ('seq', 'chan'))  101 us
    all_to_all x1, blocking collectives, inverse_transform(): lax.all_to_all(signal.reshape(shards, slab, width), 'seq', split_axis=0,...  49.5 us
    all_to_all x1, waiting for transfers between devices, forward_transform(): lax.all_to_all(columns.reshape(shards, slab, width), 'seq', split_axis=0,...  40.4 us
  transfers between devices with their start and end apart: 5, of which 4 were waited for; matrix products, arithmetic and copies ran while one was open for 1% of the time, Pallas kernels for 0%

commit v1 on v0

v1 whole, which is shorter than its diff:
```python
import math

import jax
import jax.numpy as jnp
import numpy as np
from jax import lax
from jax.experimental import pallas as pl
from jax.experimental.pallas import tpu as pltpu
from jax.sharding import PartitionSpec as P

f32 = jnp.float32
bf16 = jnp.bfloat16
highest = lax.Precision.HIGHEST
LENGTH = 8192
ROWS = 128
ORDER = 64
LANES = 128
OWN = 8
NT = (((1,), (1,)), ((), ()))
TN = (((0,), (0,)), ((), ()))

VMEM = pl.BlockSpec(memory_space=pltpu.VMEM)
SMEM = pl.BlockSpec(memory_space=pltpu.SMEM)


def wave_tables():
    index = np.arange(ORDER)
    cycles = (index // 2 + 1) ** 2
    odd = index % 2 == 1

    def turn(power):
        angle = 2.0 * math.pi / LENGTH * (power[:, None] * cycles[None, :] % LENGTH)
        return np.cos(angle), np.sin(angle)

    ahead = np.arange(ROWS)
    cos_a, sin_a = turn(ahead)
    cos_b, sin_b = turn(ROWS - ahead)
    real_b = np.where(odd, sin_b, cos_b)
    imag_b = np.where(odd, -cos_b, sin_b)
    wave = np.where(odd, sin_a, cos_a)
    cos_l, sin_l = turn(np.array([ROWS]))
    twice = [np.concatenate([t, t], axis=1).astype(np.float32) for t in (cos_a, sin_a, real_b, imag_b, wave)]
    step = np.concatenate([np.concatenate([t, t], axis=1) for t in (cos_l, sin_l)], axis=0).astype(np.float32)
    return (*twice, step)


def split(table):
    high = table.astype(bf16)
    low = (table - high.astype(f32)).astype(bf16)
    return jnp.concatenate([high, low], axis=0)


def table_kernel(
    place, rate, coef, cos_a, sin_a, real_b, imag_b, wave, step, tx, tg, mf, me, wd, small
):
    lane = lax.broadcasted_iota(jnp.int32, (ROWS, LANES), 1)
    power = lax.broadcasted_iota(jnp.int32, (ROWS, LANES), 0).astype(f32)
    left = lane < ORDER
    slope = rate[...] * (-1.0 / LENGTH)
    env_a = jnp.exp(slope * power)
    env_b = jnp.exp(slope * (ROWS - power))
    ar = env_a * cos_a[...]
    ai = env_a * sin_a[...]
    br = env_b * real_b[...]
    bi = env_b * imag_b[...]
    back = ROWS - power
    tx[...] = split(
        jnp.concatenate([br, bi, jnp.where(left, 0.0, back * br), jnp.where(left, 0.0, back * bi)], axis=1)
    )
    tg[...] = split(
        jnp.concatenate([ar, ai, jnp.where(left, ar, power * ar), jnp.where(left, ai, power * ai)], axis=1)
    )
    mf[...] = jnp.where(left, ar, ai).astype(bf16)
    me[...] = jnp.where(left, br, bi).astype(bf16)
    w = env_a * wave[...]
    wd[...] = jnp.where(left, w, power * w)
    pick = lax.broadcasted_iota(jnp.int32, (OWN, coef.shape[1]), 1) - place[0] * OWN
    pick = (pick == lax.broadcasted_iota(jnp.int32, (OWN, coef.shape[1]), 0)).astype(f32)
    own = lax.dot_general(
        pick, jnp.concatenate([coef[...], coef[...]], axis=0), NT, precision=highest, preferred_element_type=f32
    )
    scale = own * jnp.sqrt(rate[...] * (2.0 / LENGTH))
    left8 = left[:OWN]
    decay = jnp.exp(slope * ROWS)
    small[0] = scale
    small[1] = lax.dot_general(
        jnp.where(left8, scale, 0.0), w, NT, precision=highest, preferred_element_type=f32
    )
    small[2] = jnp.broadcast_to(decay * step[0:1], (OWN, LANES))
    small[3] = jnp.broadcast_to(decay * step[1:2], (OWN, LANES))
    small[4] = jnp.where(left8, scale * (0.5 / rate[...]), scale * (-1.0 / LENGTH))
    small[5] = jnp.broadcast_to(jnp.sqrt(rate[...] * (2.0 / LENGTH)) * LENGTH ** -0.5, (OWN, LANES))


def make_tables(place, rate, coef):
    consts = [jnp.asarray(t) for t in wave_tables()]
    rate2 = jnp.concatenate([rate, rate])[None, :]
    return pl.pallas_call(
        table_kernel,
        out_shape=(
            jax.ShapeDtypeStruct((2 * ROWS, 4 * LANES), bf16),
            jax.ShapeDtypeStruct((2 * ROWS, 4 * LANES), bf16),
            jax.ShapeDtypeStruct((ROWS, LANES), bf16),
            jax.ShapeDtypeStruct((ROWS, LANES), bf16),
            jax.ShapeDtypeStruct((ROWS, LANES), f32),
            jax.ShapeDtypeStruct((6, OWN, LANES), f32),
        ),
        in_specs=[SMEM] + [VMEM] * 8,
        out_specs=tuple([VMEM] * 6),
        compiler_params=pltpu.CompilerParams(vmem_limit_bytes=12 << 20),
        cost_estimate=pl.CostEstimate(flops=4_000_000, bytes_accessed=1_000_000, transcendentals=40_000),
        name="tables",
    )(place, rate2, coef, *consts)


def mix(value, prior, weight):
    row = lax.broadcasted_iota(jnp.int32, value.shape, 0)
    one = jnp.where(row == 0, prior[1:2], pltpu.roll(value, 1, 0))
    two = jnp.where(row == 0, prior[0:1], jnp.where(row == 1, prior[1:2], pltpu.roll(value, 2, 0)))
    return weight[0:1] * value + weight[1:2] * one + weight[2:3] * two


def gate_kernel(x1, x2, value, out_grad, prior, weight, sent):
    mixed = mix(value[...].astype(f32), prior[...].astype(f32), weight[...])
    gated = x1[...].astype(f32) * mixed
    grad = out_grad[...].astype(f32) * x2[...].astype(f32)
    shards = sent.shape[0]
    gated = gated.T.reshape(shards, OWN, ROWS)
    grad = grad.T.reshape(shards, OWN, ROWS)
    sent[...] = jnp.concatenate([gated, grad], axis=1).astype(bf16)


def gate(x1, x2, value, out_grad, prior, weight):
    shards = x1.shape[1] // OWN
    return pl.pallas_call(
        gate_kernel,
        out_shape=jax.ShapeDtypeStruct((shards, 2 * OWN, ROWS), bf16),
        in_specs=[VMEM] * 6,
        out_specs=VMEM,
        compiler_params=pltpu.CompilerParams(vmem_limit_bytes=12 << 20),
        name="gate",
    )(x1, x2, value, out_grad, prior, weight)


def owner_kernel(got, tx, tg, mf, me, wd, small, out, xs, gs, rs, ex, eg, sr, si, gr, gi, yc, yg):
    chunks = got.shape[0]
    rows = chunks * OWN
    both = got[...].astype(f32)
    x = both[:, :OWN].reshape(rows, ROWS)
    g = both[:, OWN:].reshape(rows, ROWS)
    xs[...] = x
    gs[...] = g
    xb = x.astype(bf16)
    gb = g.astype(bf16)
    here = lax.broadcasted_iota(jnp.int32, (ROWS, ROWS), 0)
    there = lax.broadcasted_iota(jnp.int32, (ROWS, ROWS), 1)
    mirror = (here + there == ROWS - 1).astype(bf16)
    rs[...] = jnp.dot(xb, mirror, preferred_element_type=f32)
    ex[...] = jnp.dot(
        jnp.concatenate([xb, xb], axis=1), tx[...], preferred_element_type=f32
    )
    eg[...] = jnp.dot(
        jnp.concatenate([gb, gb], axis=1), tg[...], preferred_element_type=f32
    )
    scale = small[0]
    filt = small[1]
    lr = small[2]
    li = small[3]

    a = b = c = d = jnp.zeros((OWN, LANES), f32)
    for k in range(chunks):
        at = pl.ds(k * OWN, OWN)
        sr[at] = a
        si[at] = b
        a, b = (
            lr * a - li * b + ex[at, 0:LANES],
            lr * b + li * a + ex[at, LANES : 2 * LANES],
        )
        at = pl.ds((chunks - 1 - k) * OWN, OWN)
        gr[at] = c
        gi[at] = d
        c, d = (
            lr * c - li * d + eg[at, 0:LANES],
            lr * d + li * c + eg[at, LANES : 2 * LANES],
        )

    left = lax.broadcasted_iota(jnp.int32, (OWN, LANES), 1) < ORDER

    def cube(array):
        return array.reshape(chunks, OWN, LANES)

    s_r, s_i, g_r, g_i = (cube(ref[...]) for ref in (sr, si, gr, gi))
    over = jnp.where(left, 0.0, float(ROWS))
    ahead_r = over * lr * g_r - over * li * g_i
    ahead_i = over * lr * g_i + over * li * g_r
    total = (
        s_r * (cube(eg[:, 2 * LANES : 3 * LANES]) + ahead_r)
        - s_i * (cube(eg[:, 3 * LANES : 4 * LANES]) + ahead_i)
        + g_r * cube(ex[:, 2 * LANES : 3 * LANES])
        - g_i * cube(ex[:, 3 * LANES : 4 * LANES])
    )
    total = jnp.sum(total, axis=0)
    us = jnp.where(left, scale * s_r, -scale * s_i).reshape(rows, LANES).astype(bf16)
    ug = jnp.where(left, scale * g_r, -scale * g_i).reshape(rows, LANES).astype(bf16)
    yc[...] = lax.dot_general(us, mf[...], NT, preferred_element_type=f32)
    yg[...] = lax.dot_general(ug, me[...], NT, preferred_element_type=f32)

    later = there >= here
    inside = (there < here) | (there == ROWS - 1)
    lags = []
    for ch in range(OWN):
        at = pl.ds(ch, chunks, stride=OWN)
        xc = xs[at, :].astype(bf16)
        gc = gs[at, :].astype(bf16)
        toeplitz = pltpu.roll(
            jnp.broadcast_to(filt[ch : ch + 1], (ROWS, ROWS)), 0, 1, stride=1, stride_axis=0
        )
        toeplitz = jnp.where(later, toeplitz, 0.0).astype(bf16)
        yc[at, :] += jnp.dot(xc, toeplitz, preferred_element_type=f32)
        yg[at, :] += lax.dot_general(gc, toeplitz, NT, preferred_element_type=f32)
        pairs = lax.dot_general(rs[at, :].astype(bf16), gc, TN, preferred_element_type=f32)
        pairs = pltpu.roll(pairs, 0, 1, stride=1, stride_axis=0)
        lags.append(jnp.sum(jnp.where(inside, pairs, 0.0), axis=0, keepdims=True))
    lags = pltpu.roll(jnp.concatenate(lags, axis=0), 1, 1)
    total = total + jnp.dot(lags, wd[...], precision=highest, preferred_element_type=f32)

    part = jnp.sum(total * small[4], axis=0, keepdims=True)
    part = jnp.broadcast_to(part + pltpu.roll(part, ORDER, 1), (OWN, LANES))
    moved = pltpu.roll(part, 2, 1)
    low = part - part.astype(bf16).astype(f32)
    low_moved = moved - moved.astype(bf16).astype(f32)
    row = lax.broadcasted_iota(jnp.int32, (OWN, LANES), 0)
    lane = lax.broadcasted_iota(jnp.int32, (OWN, LANES), 1)
    part = jnp.where(row == 0, part, jnp.where(row == 1, moved, jnp.where(row == 2, low, low_moved)))
    extra = jnp.where(left, total * small[5], jnp.where(row < 4, part, 0.0))
    grad = cube(yg[...])
    heads = jnp.concatenate([yg[OWN:, :], jnp.zeros((OWN, LANES), f32)], axis=0)
    heads = cube(pltpu.roll(heads, ORDER, 1))
    is_head = (lane >= ORDER) & (lane < ORDER + 2)
    extra = jnp.where(is_head, heads, extra)
    out[...] = jnp.concatenate([cube(yc[...]), grad, extra], axis=1).astype(bf16)


def owner(got, tables):
    chunks = got.shape[0]
    rows = chunks * OWN
    return pl.pallas_call(
        owner_kernel,
        out_shape=jax.ShapeDtypeStruct((chunks, 3 * OWN, ROWS), bf16),
        in_specs=[VMEM] * 7,
        out_specs=VMEM,
        scratch_shapes=[pltpu.VMEM((rows, LANES), f32)] * 3
        + [pltpu.VMEM((rows, 4 * LANES), f32)] * 2
        + [pltpu.VMEM((rows, LANES), f32)] * 6,
        compiler_params=pltpu.CompilerParams(vmem_limit_bytes=24 << 20),
        name="owner",
    )(got, *tables)


def finish_kernel(back, x1, x2, value, prior, head, weight, y, gx1, gvalue, gcoef, rates):
    shards = back.shape[0]
    wide = shards * OWN
    every = back[...].astype(f32)
    conv = every[:, :OWN].reshape(wide, ROWS).T
    grad = every[:, OWN : 2 * OWN].reshape(wide, ROWS).T
    extra = every[:, 2 * OWN :]
    turned = extra.reshape(wide, LANES).T
    gcoef[...] = turned[:ORDER]
    part = jnp.sum(extra, axis=0)
    lane = lax.broadcasted_iota(jnp.int32, (1, LANES), 1)
    most = part[0:1] + part[2:3]
    few = part[1:2] + part[3:4]
    rates[...] = jnp.broadcast_to(
        jnp.where(lane < 2, pltpu.roll(few, ORDER - 2, 1), pltpu.roll(most, ORDER, 1)), rates.shape
    )
    first = x1[...].astype(f32)
    w = weight[...]
    y[...] = (x2[...].astype(f32) * conv).astype(bf16)
    mixed = mix(value[...].astype(f32), prior[...].astype(f32), w)
    gx1[...] = (grad * mixed).astype(bf16)
    grad_mixed = grad * first
    after = turned[ORDER : ORDER + 2] * head[...].astype(f32)
    row = lax.broadcasted_iota(jnp.int32, grad_mixed.shape, 0)
    one = jnp.where(row == ROWS - 1, after[0:1], pltpu.roll(grad_mixed, ROWS - 1, 0))
    two = jnp.where(
        row == ROWS - 2,
        after[0:1],
        jnp.where(row == ROWS - 1, after[1:2], pltpu.roll(grad_mixed, ROWS - 2, 0)),
    )
    gvalue[...] = (w[0:1] * grad_mixed + w[1:2] * one + w[2:3] * two).astype(bf16)


def finish(back, x1, x2, value, prior, head, weight, peers):
    shape = jax.ShapeDtypeStruct(x1.shape, bf16)
    return pl.pallas_call(
        finish_kernel,
        out_shape=(
            shape,
            shape,
            shape,
            jax.ShapeDtypeStruct((ORDER, x1.shape[1]), f32),
            jax.ShapeDtypeStruct((peers, LANES), f32),
        ),
        in_specs=[VMEM] * 7,
        out_specs=tuple([VMEM] * 5),
        compiler_params=pltpu.CompilerParams(vmem_limit_bytes=16 << 20),
        name="finish",
    )(back, x1, x2, value, prior, head, weight)


def shift(array, by):
    peers = lax.axis_size("seq")
    pairs = [(i, i + by) for i in range(peers) if 0 <= i + by < peers]
    return lax.ppermute(array, "seq", pairs)


def per_device(x1, x2, value, out_grad, short_weight, coef, rate):
    peers = lax.axis_size("chan")
    width = x1.shape[1]
    prior = shift(value[ROWS - 2 :], 1)
    head = shift(x1[:2], -1)
    place = lax.axis_index("seq").astype(jnp.int32)[None]
    tables = make_tables(place, rate, coef)
    sent = gate(x1, x2, value, out_grad, prior, short_weight)
    got = lax.all_to_all(sent, "seq", split_axis=0, concat_axis=0, tiled=True)
    done = owner(got, tables)
    back = lax.all_to_all(done, "seq", split_axis=0, concat_axis=0, tiled=True)
    y, gx1, gvalue, gcoef, rates = finish(back, x1, x2, value, prior, head, short_weight, peers)
    rates = lax.all_to_all(rates, "chan", split_axis=0, concat_axis=0, tiled=True)
    grad_rate = jnp.sum(rates, axis=0)[:ORDER] * (LENGTH * width * peers) ** -0.5
    return (y, gx1, gvalue, gcoef, grad_rate)


def solution(mesh):
    whole = P("seq", "chan")
    return jax.shard_map(
        per_device,
        mesh=mesh,
        in_specs=(whole, whole, whole, whole, P(None, "chan"), P(None, "chan"), P()),
        out_specs=(whole, whole, whole, P(None, "chan"), P()),
        check_vma=False,
    )
```

time: 746 us -> 98.1 us (0.13); the launches traced: 737 us -> 96.6 us
  blocking collectives: 304 us -> 9.36 us
  waiting for transfers between devices: 325 us -> 46.7 us
  matrix products: 22.9 us -> 0 us
  local copies, waits for them, and re-layouts: 25.4 us -> 6.35 us
  between operations: 15 us -> 0.76 us
  starting transfers between devices: 37.1 us -> 27.8 us
    all_to_all x2 -> x1, blocking collectives: 203 us -> 9.36 us  [per_device(): lax.all_to_all(rates, 'chan', split_axis=0, concat_axis=0, tiled=True)]
    psum x1 -> x0, waiting for transfers between devices: 151 us -> none  [per_device(): grad_coef = lax.psum(coef_part, 'seq')]
    all_to_all x2, waiting for transfers between devices: 168 us -> 27.1 us  [the longest x1 17.6 us: per_device(): got = lax.all_to_all(sent, 'seq', split_axis=0, concat_axis=0, tiled=True)]
    psum x1 -> x0, blocking collectives: 101 us -> none  [per_device(): rate_sum = lax.psum(rate_part, ('seq', 'chan'))]
    dot_general x15 -> x0, matrix products: 22.9 us -> none  [the longest x1 2.76 us: forward_transform(): jnp.einsum('fm,rmk->rfk', cos_m, gathered[0], precision=highest)]
    ppermute x2, waiting for transfers between devices: 6.58 us -> 19.6 us  [shift(): return lax.ppermute(array, 'seq', pairs)]
    psum x1 -> x0, starting transfers between devices: 11.9 us -> none  [per_device(): grad_coef = lax.psum(coef_part, 'seq')]
    another operation x2 -> x0, local copies, waits for them, and re-layouts: 7.62 us -> none  [the longest x1 4.05 us: forward_transform(): jnp.stack([real_b, imag_b])]
  transfers between devices with their start and end apart: 5 -> 4, of which waited for: 4 -> 4; matrix products, arithmetic and copies ran while one was open for 1% -> 0% of each run, Pallas kernels for 0% -> 1%
where the time goes in v1:
time: 98.1 us; the launch traced here: 96.6 us
  waiting for transfers between devices  46.7 us (48%)
  starting transfers between devices  27.8 us (28%)
  blocking collectives  9.36 us (10%)
  local copies, waits for them, and re-layouts  6.35 us (6%)
  Pallas kernels  5.07 us (5%)
    ppermute x2, waiting for transfers between devices, shift(): return lax.ppermute(array, 'seq', pairs)  19.6 us
    all_to_all x1, waiting for transfers between devices, per_device(): got = lax.all_to_all(sent, 'seq', split_axis=0, concat_axis=0, tiled=True)  17.6 us
    all_to_all x1, starting transfers between devices, per_device(): got = lax.all_to_all(sent, 'seq', split_axis=0, concat_axis=0, tiled=True)  12.4 us
    all_to_all x1, waiting for transfers between devices, per_device(): back = lax.all_to_all(done, 'seq', split_axis=0, concat_axis=0, tiled=True)  9.46 us
    all_to_all x1, blocking collectives, per_device(): lax.all_to_all(rates, 'chan', split_axis=0, concat_axis=0, tiled=True)  9.36 us
    ppermute x2, starting transfers between devices, shift(): return lax.ppermute(array, 'seq', pairs)  8.68 us
    all_to_all x1, starting transfers between devices, per_device(): back = lax.all_to_all(done, 'seq', split_axis=0, concat_axis=0, tiled=True)  6.68 us
    unnamed x34, local copies, waits for them, and re-layouts  5.64 us
  transfers between devices with their start and end apart: 4, of which 4 were waited for; matrix products, arithmetic and copies ran while one was open for 0% of the time, Pallas kernels for 1%

profile of v1, /device:TPU:24, one launch (start us, length us, event | category | flops | bytes accessed | tf_op | source)
XLA Modules:
  0.0 96.6 jit_solution(16798026257454418372)
XLA Ops:
  0.6 0.7 slice.9
  1.3 3.8 %collective-permute-start = (bf16[2,512]{1,0:T(2,128)(2,1)S(1)}, bf16[2,512]{1,0:T(2,128)(2,1)S(1)}, u32[]{:S(2)}, u32[]{:S(2)}) collective-permute-start(bf16[2,512]{1,0:T(2,128)(2,1)S(1)} %slice.9), channel_id=1, source_target_pairs={{0,8},{8,16},{16,24},{24,32},{32,40},{40,48},{48,56},{56,64},{64,7... | collective-permute-start | bytes 6152 | tf_op jit(solution)/shard_map/ppermute | solution.py:314
  5.2 9.3 %collective-permute-done.prior = bf16[2,512]{1,0:T(2,128)(2,1)S(1)} collective-permute-done((bf16[2,512]{1,0:T(2,128)(2,1)S(1)}, bf16[2,512]{1,0:T(2,128)(2,1)S(1)}, u32[]{:S(2)}, u32[]{:S(2)}) %collective-permute-start) | collective-permute-done | bytes 2080 | tf_op jit(solution)/shard_map/ppermute | solution.py:314
  14.5 0.0 copy-start
  14.5 0.9 copy-done
  15.4 0.0 copy-start.2
  15.4 0.9 copy-done.2
  16.3 0.0 copy-start.4
  16.3 0.9 copy-done.4
  17.2 0.0 copy-start.6
  17.2 0.9 copy-done.6
  18.1 0.0 copy-start.13
  18.1 0.7 copy-done.13
  18.8 0.9 gate.1
  19.7 0.0 copy-start.7
  19.7 0.0 copy-start.8
  19.7 0.0 copy-start.9
  19.7 0.0 copy-start.10
  19.7 0.0 copy-start.11
  19.7 0.0 copy-start.12
  19.7 12.4 %all-to-all-start = ((bf16[64,16,128]{2,1,0:T(8,128)(2,1)}), bf16[64,16,128]{2,1,0:T(8,128)(2,1)S(1)}, u32[]{:S(2)}, u32[]{:S(2)}) async-start(bf16[64,16,128]{2,1,0:T(8,128)(2,1)} %gate.1), calls=%async_computation | async-start | bytes 524288 | tf_op jit(solution)/shard_map/all_to_all | solution.py:325
  32.1 0.0 copy-start.16
  32.2 0.6 copy-done.16
  32.8 0.1 maximum_bitcast_fusion.rate
  32.9 0.0 copy-start.15
  32.9 0.0 copy-done.7
  32.9 0.0 copy-done.8
  32.9 0.0 copy-done.9
  32.9 0.0 copy-done.10
  32.9 0.0 copy-done.11
  32.9 0.0 copy-done.12
  32.9 0.6 copy-done.15
  33.6 0.7 tables.1
  34.2 17.6 %all-to-all-done.got = bf16[64,16,128]{2,1,0:T(8,128)(2,1)S(1)} async-done(((bf16[64,16,128]{2,1,0:T(8,128)(2,1)}), bf16[64,16,128]{2,1,0:T(8,128)(2,1)S(1)}, u32[]{:S(2)}, u32[]{:S(2)}) %all-to-all-start) | async-done | bytes 262176 | tf_op jit(solution)/shard_map/all_to_all | solution.py:325
  51.9 2.4 %owner.1 = bf16[64,24,128]{2,1,0:T(8,128)(2,1)} custom-call(bf16[64,16,128]{2,1,0:T(8,128)(2,1)S(1)} %all-to-all-done.got, bf16[256,512]{1,0:T(8,128)(2,1)S(1)} %get-tuple-element.16.tx, bf16[256,512]{1,0:T(8,128)(2,1)S(1)} %get-tuple-element.17.tg, bf16[128,128]{1,0:T(8,128)(2,1)S(1)} %get-tuple-element.18.mf, bf16[128,128]{1,0:T(8,128)(2,1)S(1)} %get-tuple-element.19.me, ...), custom_call_target="tpu_custom_call" | custom-call | tf_op jit(solution)/shard_map/owner/pallas_call | solution.py:247
  54.3 0.0 copy-start.1
  54.3 0.0 copy-start.3
  54.3 0.0 copy-start.5
  54.3 0.0 copy-start.14
  54.3 6.7 %all-to-all-start.1 = ((bf16[64,24,128]{2,1,0:T(8,128)(2,1)}), bf16[64,24,128]{2,1,0:T(8,128)(2,1)S(1)}, u32[]{:S(2)}, u32[]{:S(2)}) async-start(bf16[64,24,128]{2,1,0:T(8,128)(2,1)} %owner.1), calls=%async_computation.1 | async-start | bytes 786432 | tf_op jit(solution)/shard_map/all_to_all | solution.py:327
  61.0 0.0 copy-done.1
  61.0 4.9 %collective-permute-start.1 = (bf16[2,512]{1,0:T(2,128)(2,1)S(1)}, bf16[2,512]{1,0:T(2,128)(2,1)S(1)}, u32[]{:S(2)}, u32[]{:S(2)}) collective-permute-start(bf16[2,512]{1,0:T(2,128)(2,1)S(1)} %slice.10), channel_id=1, source_target_pairs={{8,0},{16,8},{24,16},{32,24},{40,32},{48,40},{56,48},{64,56},{72,6... | collective-permute-start | bytes 6152 | tf_op jit(solution)/shard_map/ppermute | solution.py:314
  65.9 10.3 %collective-permute-done.1.head = bf16[2,512]{1,0:T(2,128)(2,1)S(1)} collective-permute-done((bf16[2,512]{1,0:T(2,128)(2,1)S(1)}, bf16[2,512]{1,0:T(2,128)(2,1)S(1)}, u32[]{:S(2)}, u32[]{:S(2)}) %collective-permute-start.1) | collective-permute-done | bytes 2080 | tf_op jit(solution)/shard_map/ppermute | solution.py:314
  76.2 9.5 %all-to-all-done.1.back = bf16[64,24,128]{2,1,0:T(8,128)(2,1)S(1)} async-done(((bf16[64,24,128]{2,1,0:T(8,128)(2,1)}), bf16[64,24,128]{2,1,0:T(8,128)(2,1)S(1)}, u32[]{:S(2)}, u32[]{:S(2)}) %all-to-all-start.1) | async-done | bytes 393248 | tf_op jit(solution)/shard_map/all_to_all | solution.py:327
  85.7 0.0 copy-done.3
  85.7 0.0 copy-done.5
  85.7 0.0 copy-done.14
  85.7 1.1 %finish.1 = (bf16[128,512]{1,0:T(8,128)(2,1)}, bf16[128,512]{1,0:T(8,128)(2,1)}, bf16[128,512]{1,0:T(8,128)(2,1)}, f32[64,512]{1,0:T(8,128)}, f32[8,128]{1,0:T(8,128)S(1)}) custom-call(bf16[64,24,128]{2,1,0:T(8,128)(2,1)S(1)} %all-to-all-done.1.back, bf16[128,512]{1,0:T(8,128)(2,1)S(1)} %copy-done.1, bf16[128,512]{1,0:T(8,128)(2,1)S(1)} %copy-done.5, ...), custom_call_target="tpu_custom_call" | custom-call | tf_op jit(solution)/shard_map/finish/pallas_call | solution.py:295
  86.7 9.4 %all_to_all.19 = f32[8,1,128]{2,1,0:T(1,128)S(1)} all-to-all(f32[8,1,128]{2,1,0:T(1,128)S(1)} %bitcast.6), channel_id=1, replica_groups=mesh['seq'=64,'chan'=8] {'chan'}, dimensions={0} | all-to-all | bytes 8192 | tf_op jit(solution)/shard_map/all_to_all | solution.py:329
  96.1 0.5 slice_multiply_fusion
  (2 shorter events, 0.0 us)
Async XLA Ops:
  1.3 13.1 %collective-permute-start = (bf16[2,512]{1,0:T(2,128)(2,1)S(1)}, bf16[2,512]{1,0:T(2,128)(2,1)S(1)}, u32[]{:S(2)}, u32[]{:S(2)}) collective-permute-start(bf16[2,512]{1,0:T(2,128)(2,1)S(1)} %slice.9), channel_id=1, source_target_pairs={{0,8},{8,16},{16,24},{24,32},{32,40},{40,48},{48,56},{56,64},{64,7... | collective-permute-start | bytes 6152 | tf_op jit(solution)/shard_map/ppermute | solution.py:314
  14.5 0.9 copy-start
  15.4 0.9 copy-start.2
  16.3 0.9 copy-start.4
  17.2 0.9 copy-start.6
  18.1 0.7 copy-start.13
  19.7 13.2 %copy-start.7 = (f32[64,512]{1,0:T(8,128)S(1)}, f32[64,512]{1,0:T(8,128)}, u32[]{:S(2)}) copy-start(f32[64,512]{1,0:T(8,128)} %coef.1) | copy-start | bytes 393220
  19.7 13.2 %copy-start.8 = (f32[128,128]{1,0:T(8,128)S(1)}, f32[128,128]{1,0:T(8,128)}, u32[]{:S(2)}) copy-start(f32[128,128]{1,0:T(8,128)} %constant.22.clone.cos_a) | copy-start | bytes 196612
  19.7 13.2 %copy-start.9 = (f32[128,128]{1,0:T(8,128)S(1)}, f32[128,128]{1,0:T(8,128)}, u32[]{:S(2)}) copy-start(f32[128,128]{1,0:T(8,128)} %constant.23.clone.sin_a) | copy-start | bytes 196612
  19.7 13.2 %copy-start.10 = (f32[128,128]{1,0:T(8,128)S(1)}, f32[128,128]{1,0:T(8,128)}, u32[]{:S(2)}) copy-start(f32[128,128]{1,0:T(8,128)} %constant.24.clone.real_b) | copy-start | bytes 196612
  19.7 13.2 %copy-start.11 = (f32[128,128]{1,0:T(8,128)S(1)}, f32[128,128]{1,0:T(8,128)}, u32[]{:S(2)}) copy-start(f32[128,128]{1,0:T(8,128)} %constant.25.clone.imag_b) | copy-start | bytes 196612
  19.7 13.2 %copy-start.12 = (f32[128,128]{1,0:T(8,128)S(1)}, f32[128,128]{1,0:T(8,128)}, u32[]{:S(2)}) copy-start(f32[128,128]{1,0:T(8,128)} %constant.26.clone.wave) | copy-start | bytes 196612
  19.7 32.2 %all-to-all-start = ((bf16[64,16,128]{2,1,0:T(8,128)(2,1)}), bf16[64,16,128]{2,1,0:T(8,128)(2,1)S(1)}, u32[]{:S(2)}, u32[]{:S(2)}) async-start(bf16[64,16,128]{2,1,0:T(8,128)(2,1)} %gate.1), calls=%async_computation | async-start | bytes 524288 | tf_op jit(solution)/shard_map/all_to_all | solution.py:325
  32.1 0.7 copy-start.16
  32.9 0.7 copy-start.15
  54.3 6.7 %copy-start.1 = (bf16[128,512]{1,0:T(8,128)(2,1)S(1)}, bf16[128,512]{1,0:T(8,128)(2,1)}, u32[]{:S(2)}) copy-start(bf16[128,512]{1,0:T(8,128)(2,1)} %x1.3) | copy-start | bytes 393220
  54.3 31.4 %copy-start.3 = (bf16[128,512]{1,0:T(8,128)(2,1)S(1)}, bf16[128,512]{1,0:T(8,128)(2,1)}, u32[]{:S(2)}) copy-start(bf16[128,512]{1,0:T(8,128)(2,1)} %value.3) | copy-start | bytes 393220
  54.3 31.4 %copy-start.5 = (bf16[128,512]{1,0:T(8,128)(2,1)S(1)}, bf16[128,512]{1,0:T(8,128)(2,1)}, u32[]{:S(2)}) copy-start(bf16[128,512]{1,0:T(8,128)(2,1)} %x2.3) | copy-start | bytes 393220
  54.3 31.4 %copy-start.14 = (f32[3,512]{1,0:T(4,128)S(1)}, f32[3,512]{1,0:T(4,128)}, u32[]{:S(2)}) copy-start(f32[3,512]{1,0:T(4,128)} %weight.3) | copy-start | bytes 18436
  54.3 31.3 %all-to-all-start.1 = ((bf16[64,24,128]{2,1,0:T(8,128)(2,1)}), bf16[64,24,128]{2,1,0:T(8,128)(2,1)S(1)}, u32[]{:S(2)}, u32[]{:S(2)}) async-start(bf16[64,24,128]{2,1,0:T(8,128)(2,1)} %owner.1), calls=%async_computation.1 | async-start | bytes 786432 | tf_op jit(solution)/shard_map/all_to_all | solution.py:327
  61.0 15.2 %collective-permute-start.1 = (bf16[2,512]{1,0:T(2,128)(2,1)S(1)}, bf16[2,512]{1,0:T(2,128)(2,1)S(1)}, u32[]{:S(2)}, u32[]{:S(2)}) collective-permute-start(bf16[2,512]{1,0:T(2,128)(2,1)S(1)} %slice.10), channel_id=1, source_target_pairs={{8,0},{16,8},{24,16},{32,24},{40,32},{48,40},{56,48},{64,56},{72,6... | collective-permute-start | bytes 6152 | tf_op jit(solution)/shard_map/ppermute | solution.py:314

commit v2 on v1

--- a/solution.py
+++ b/solution.py
@@ -16,6 +16,7 @@
 ORDER = 64
 LANES = 128
 OWN = 8
+WORDS = 2 * OWN + 2
 NT = (((1,), (1,)), ((), ()))
 TN = (((0,), (0,)), ((), ()))
 
@@ -51,7 +52,7 @@
 
 
 def table_kernel(
-    place, rate, coef, cos_a, sin_a, real_b, imag_b, wave, step, tx, tg, mf, me, wd, small
+    place, rate, coef, weight, cos_a, sin_a, real_b, imag_b, wave, step, tx, tg, mf, me, wd, small
 ):
     lane = lax.broadcasted_iota(jnp.int32, (ROWS, LANES), 1)
     power = lax.broadcasted_iota(jnp.int32, (ROWS, LANES), 0).astype(f32)
@@ -89,10 +90,18 @@
     small[2] = jnp.broadcast_to(decay * step[0:1], (OWN, LANES))
     small[3] = jnp.broadcast_to(decay * step[1:2], (OWN, LANES))
     small[4] = jnp.where(left8, scale * (0.5 / rate[...]), scale * (-1.0 / LENGTH))
+    for tap in (1, 2):
+        small[5 + tap] = lax.dot_general(
+            pick,
+            jnp.broadcast_to(weight[tap : tap + 1], (LANES, coef.shape[1])),
+            NT,
+            precision=highest,
+            preferred_element_type=f32,
+        )
     small[5] = jnp.broadcast_to(jnp.sqrt(rate[...] * (2.0 / LENGTH)) * LENGTH ** -0.5, (OWN, LANES))
 
 
-def make_tables(place, rate, coef):
+def make_tables(place, rate, coef, weight):
     consts = [jnp.asarray(t) for t in wave_tables()]
     rate2 = jnp.concatenate([rate, rate])[None, :]
     return pl.pallas_call(
@@ -103,14 +112,14 @@
             jax.ShapeDtypeStruct((ROWS, LANES), bf16),
             jax.ShapeDtypeStruct((ROWS, LANES), bf16),
             jax.ShapeDtypeStruct((ROWS, LANES), f32),
-            jax.ShapeDtypeStruct((6, OWN, LANES), f32),
+            jax.ShapeDtypeStruct((8, OWN, LANES), f32),
         ),
-        in_specs=[SMEM] + [VMEM] * 8,
+        in_specs=[SMEM] + [VMEM] * 9,
         out_specs=tuple([VMEM] * 6),
         compiler_params=pltpu.CompilerParams(vmem_limit_bytes=12 << 20),
         cost_estimate=pl.CostEstimate(flops=4_000_000, bytes_accessed=1_000_000, transcendentals=40_000),
         name="tables",
-    )(place, rate2, coef, *consts)
+    )(place, rate2, coef, weight, *consts)
 
 
 def mix(value, prior, weight):
@@ -120,33 +129,88 @@
     return weight[0:1] * value + weight[1:2] * one + weight[2:3] * two
 
 
-def gate_kernel(x1, x2, value, out_grad, prior, weight, sent):
-    mixed = mix(value[...].astype(f32), prior[...].astype(f32), weight[...])
-    gated = x1[...].astype(f32) * mixed
-    grad = out_grad[...].astype(f32) * x2[...].astype(f32)
+def gate_kernel(x1h, x2h, vh, oh, wh, sent, tail, x1, x2, v, o, w, sems):
+    copies = [
+        pltpu.make_async_copy(src, dst, sems.at[n])
+        for n, (src, dst) in enumerate(((oh, o), (x2h, x2), (vh, v), (wh, w), (x1h, x1)))
+    ]
+    for copy in copies:
+        copy.start()
+    copies[0].wait()
+    copies[1].wait()
     shards = sent.shape[0]
-    gated = gated.T.reshape(shards, OWN, ROWS)
+    grad = o[...].astype(f32) * x2[...].astype(f32)
     grad = grad.T.reshape(shards, OWN, ROWS)
-    sent[...] = jnp.concatenate([gated, grad], axis=1).astype(bf16)
-
-
-def gate(x1, x2, value, out_grad, prior, weight):
+    for copy in copies[2:]:
+        copy.wait()
+    value = v[...].astype(f32)
+    first = x1[...].astype(f32)
+    zero = jnp.zeros((2, value.shape[1]), f32)
+    gated = (first * mix(value, zero, w[...])).T.reshape(shards, OWN, ROWS)
+    flat = sent.reshape(shards, WORDS, ROWS)
+    flat[:, : 2 * OWN] = jnp.concatenate([gated, grad], axis=1).astype(bf16)
+    tail[...] = v[ROWS - 16 :]
+
+    per = LANES // OWN
+    lane = lax.broadcasted_iota(jnp.int32, (per, LANES), 1)
+    row = lax.broadcasted_iota(jnp.int32, (per, LANES), 0)
+    group = lax.rem(lane - row * OWN + LANES, LANES) // OWN
+    edges = []
+    for at in range(0, value.shape[1], LANES):
+        tile = jnp.zeros((per, LANES), f32)
+        for n, (source, where) in enumerate(((first, 0), (first, 1), (value, ROWS - 2), (value, ROWS - 1))):
+            line = source[where : where + 1, at : at + LANES]
+            line = pltpu.roll(line, n * OWN, 1) if n else line
+            tile = jnp.where(group == n, line, tile)
+        edges.append(tile)
+    edges = jnp.concatenate(edges, axis=0)
+    flat[:, 2 * OWN :] = jnp.broadcast_to(edges[:, None, :], (shards, 2, LANES)).astype(bf16)
+
+
+def gate(x1, x2, value, out_grad, weight):
     shards = x1.shape[1] // OWN
     return pl.pallas_call(
         gate_kernel,
-        out_shape=jax.ShapeDtypeStruct((shards, 2 * OWN, ROWS), bf16),
-        in_specs=[VMEM] * 6,
-        out_specs=VMEM,
-        compiler_params=pltpu.CompilerParams(vmem_limit_bytes=12 << 20),
+        out_shape=(
+            jax.ShapeDtypeStruct((shards, WORDS // 2, 2, ROWS), bf16),
+            jax.ShapeDtypeStruct((16, x1.shape[1]), bf16),
+        ),
+        in_specs=[pl.BlockSpec(memory_space=pltpu.HBM)] * 5,
+        out_specs=(VMEM, VMEM),
+        scratch_shapes=[pltpu.VMEM(x1.shape, bf16)] * 4
+        + [pltpu.VMEM(weight.shape, f32), pltpu.SemaphoreType.DMA((5,))],
+        compiler_params=pltpu.CompilerParams(vmem_limit_bytes=(64 << 20) - (64 << 10)),
         name="gate",
-    )(x1, x2, value, out_grad, prior, weight)
-
-
-def owner_kernel(got, tx, tg, mf, me, wd, small, out, xs, gs, rs, ex, eg, sr, si, gr, gi, yc, yg):
+    )(x1, x2, value, out_grad, weight)
+
+
+def owner_kernel(place, got, tx, tg, mf, me, wd, small, out, xs, gs, rs, ex, eg, sr, si, gr, gi, yc, yg):
     chunks = got.shape[0]
     rows = chunks * OWN
-    both = got[...].astype(f32)
-    x = both[:, :OWN].reshape(rows, ROWS)
+    flat = got.reshape(chunks, WORDS, ROWS)
+    both = flat[:, : 2 * OWN].astype(f32)
+    edge = flat[:, 2 * OWN :].astype(f32)[:, :1]
+    edge = jnp.broadcast_to(edge, (chunks, OWN, LANES)).reshape(rows, LANES)
+    edge = pltpu.roll(edge, lax.rem(ORDER * LANES - place[0] * OWN, LANES), 1)
+    lane3 = lax.broadcasted_iota(jnp.int32, (rows, LANES), 1)
+    row3 = lax.broadcasted_iota(jnp.int32, (rows, LANES), 0)
+    edge = jnp.where(lane3 % OWN == row3 % OWN, edge, 0.0).astype(bf16)
+    group = lax.broadcasted_iota(jnp.int32, (LANES, LANES), 0) // OWN
+    to = lax.broadcasted_iota(jnp.int32, (LANES, LANES), 1)
+    spot_x1 = ((group < 2) & (to % ORDER == group)).astype(bf16)
+    spot_v = (((group == 2) & (to == 0)) | ((group == 3) & (to == 1))).astype(bf16)
+    spot_last = ((group == 3) & (to == 0)).astype(bf16)
+    spread = jnp.dot(
+        edge, jnp.concatenate([spot_x1, spot_v, spot_last], axis=1), preferred_element_type=f32
+    )
+    x1_head = spread[:, :LANES]
+    before = (
+        small[7] * spread[:, LANES : 2 * LANES].reshape(chunks, OWN, LANES)
+        + small[6] * spread[:, 2 * LANES :].reshape(chunks, OWN, LANES)
+    )
+    before = jnp.concatenate([jnp.zeros((1, OWN, LANES), f32), before[:-1]], axis=0)
+    x = both[:, :OWN].reshape(rows, ROWS) + x1_head * before.reshape(rows, LANES)
+    x = x.astype(bf16).astype(f32)
     g = both[:, OWN:].reshape(rows, ROWS)
     xs[...] = x
     gs[...] = g
@@ -234,30 +298,30 @@
     part = jnp.where(row == 0, part, jnp.where(row == 1, moved, jnp.where(row == 2, low, low_moved)))
     extra = jnp.where(left, total * small[5], jnp.where(row < 4, part, 0.0))
     grad = cube(yg[...])
-    heads = jnp.concatenate([yg[OWN:, :], jnp.zeros((OWN, LANES), f32)], axis=0)
-    heads = cube(pltpu.roll(heads, ORDER, 1))
+    heads = cube(pltpu.roll(yg[...], ORDER, 1) * x1_head)
+    heads = jnp.concatenate([heads[1:], jnp.zeros((1, OWN, LANES), f32)], axis=0)
     is_head = (lane >= ORDER) & (lane < ORDER + 2)
     extra = jnp.where(is_head, heads, extra)
     out[...] = jnp.concatenate([cube(yc[...]), grad, extra], axis=1).astype(bf16)
 
 
-def owner(got, tables):
+def owner(place, got, tables):
     chunks = got.shape[0]
     rows = chunks * OWN
     return pl.pallas_call(
         owner_kernel,
         out_shape=jax.ShapeDtypeStruct((chunks, 3 * OWN, ROWS), bf16),
-        in_specs=[VMEM] * 7,
+        in_specs=[SMEM] + [VMEM] * 7,
         out_specs=VMEM,
         scratch_shapes=[pltpu.VMEM((rows, LANES), f32)] * 3
         + [pltpu.VMEM((rows, 4 * LANES), f32)] * 2
         + [pltpu.VMEM((rows, LANES), f32)] * 6,
         compiler_params=pltpu.CompilerParams(vmem_limit_bytes=24 << 20),
         name="owner",
-    )(got, *tables)
-
-
-def finish_kernel(back, x1, x2, value, prior, head, weight, y, gx1, gvalue, gcoef, rates):
+    )(place, got, *tables)
+
+
+def finish_kernel(back, x1, x2, value, tail, weight, y, gx1, gvalue, gcoef, rates):
     shards = back.shape[0]
     wide = shards * OWN
     every = back[...].astype(f32)
@@ -276,10 +340,10 @@
     first = x1[...].astype(f32)
     w = weight[...]
     y[...] = (x2[...].astype(f32) * conv).astype(bf16)
-    mixed = mix(value[...].astype(f32), prior[...].astype(f32), w)
+    mixed = mix(value[...].astype(f32), tail[...].astype(f32)[14:], w)
     gx1[...] = (grad * mixed).astype(bf16)
     grad_mixed = grad * first
-    after = turned[ORDER : ORDER + 2] * head[...].astype(f32)
+    after = turned[ORDER : ORDER + 2]
     row = lax.broadcasted_iota(jnp.int32, grad_mixed.shape, 0)
     one = jnp.where(row == ROWS - 1, after[0:1], pltpu.roll(grad_mixed, ROWS - 1, 0))
     two = jnp.where(
@@ -290,7 +354,7 @@
     gvalue[...] = (w[0:1] * grad_mixed + w[1:2] * one + w[2:3] * two).astype(bf16)
 
 
-def finish(back, x1, x2, value, prior, head, weight, peers):
+def finish(back, x1, x2, value, tail, weight, peers):
     shape = jax.ShapeDtypeStruct(x1.shape, bf16)
     return pl.pallas_call(
         finish_kernel,
@@ -301,11 +365,11 @@
             jax.ShapeDtypeStruct((ORDER, x1.shape[1]), f32),
             jax.ShapeDtypeStruct((peers, LANES), f32),
         ),
-        in_specs=[VMEM] * 7,
+        in_specs=[VMEM] * 6,
         out_specs=tuple([VMEM] * 5),
         compiler_params=pltpu.CompilerParams(vmem_limit_bytes=16 << 20),
         name="finish",
-    )(back, x1, x2, value, prior, head, weight)
+    )(back, x1, x2, value, tail, weight)
 
 
 def shift(array, by):
@@ -317,15 +381,14 @@
 def per_device(x1, x2, value, out_grad, short_weight, coef, rate):
     peers = lax.axis_size("chan")
     width = x1.shape[1]
-    prior = shift(value[ROWS - 2 :], 1)
-    head = shift(x1[:2], -1)
     place = lax.axis_index("seq").astype(jnp.int32)[None]
-    tables = make_tables(place, rate, coef)
-    sent = gate(x1, x2, value, out_grad, prior, short_weight)
+    tables = make_tables(place, rate, coef, short_weight)
+    sent, tail = gate(x1, x2, value, out_grad, short_weight)
+    tail = shift(tail, 1)
     got = lax.all_to_all(sent, "seq", split_axis=0, concat_axis=0, tiled=True)
-    done = owner(got, tables)
+    done = owner(place, got, tables)
     back = lax.all_to_all(done, "seq", split_axis=0, concat_axis=0, tiled=True)
-    y, gx1, gvalue, gcoef, rates = finish(back, x1, x2, value, prior, head, short_weight, peers)
+    y, gx1, gvalue, gcoef, rates = finish(back, x1, x2, value, tail, short_weight, peers)
     rates = lax.all_to_all(rates, "chan", split_axis=0, concat_axis=0, tiled=True)
     grad_rate = jnp.sum(rates, axis=0)[:ORDER] * (LENGTH * width * peers) ** -0.5
     return (y, gx1, gvalue, gcoef, grad_rate)

time: 98.1 us -> 91.4 us (0.932)
  local copies, waits for them, and re-layouts: 6.35 us -> 0.7 us
  waiting for transfers between devices: 46.7 us -> 42.7 us
  Pallas kernels: 5.07 us -> 7.14 us
  starting transfers between devices: 27.8 us -> 28.9 us
    all_to_all x1, starting transfers between devices: 12.4 us -> 18.9 us  [per_device(): got = lax.all_to_all(sent, 'seq', split_axis=0, concat_axis=0, tiled=True)]
    ppermute x2 -> x1, waiting for transfers between devices: 19.6 us -> 14.2 us  [shift(): return lax.ppermute(array, 'seq', pairs)]
    ppermute x2 -> x1, starting transfers between devices: 8.68 us -> 3.38 us  [shift(): return lax.ppermute(array, 'seq', pairs)]
    unnamed x34 -> x26, local copies, waits for them, and re-layouts: 5.64 us -> 0.7 us
    all_to_all x1, waiting for transfers between devices: 17.6 us -> 20.4 us  [per_device(): got = lax.all_to_all(sent, 'seq', split_axis=0, concat_axis=0, tiled=True)]
    pallas_call x1, Pallas kernels: 0.92 us -> 2.23 us  [gate(): pl.pallas_call(gate_kernel, out_shape=(jax.ShapeDtypeStruct((shards, WORD...]
    all_to_all x1, waiting for transfers between devices: 9.46 us -> 8.14 us  [per_device(): back = lax.all_to_all(done, 'seq', split_axis=0, concat_axis=0, tiled=True)]
  transfers between devices with their start and end apart: 4 -> 3, of which waited for: 4 -> 3; matrix products, arithmetic and copies ran while one was open for 0% -> 0% of each run, Pallas kernels for 1% -> 1%
where the time goes in v2:
time: 91.4 us; the launch traced here: 90.2 us
  waiting for transfers between devices  42.7 us (47%)
  starting transfers between devices  28.9 us (32%)
  blocking collectives  9.35 us (10%)
  Pallas kernels  7.14 us (8%)
    all_to_all x1, waiting for transfers between devices, per_device(): got = lax.all_to_all(sent, 'seq', split_axis=0, concat_axis=0, tiled=True)  20.4 us
    all_to_all x1, starting transfers between devices, per_device(): got = lax.all_to_all(sent, 'seq', split_axis=0, concat_axis=0, tiled=True)  18.9 us
    ppermute x1, waiting for transfers between devices, shift(): return lax.ppermute(array, 'seq', pairs)  14.2 us
    all_to_all x1, blocking collectives, per_device(): lax.all_to_all(rates, 'chan', split_axis=0, concat_axis=0, tiled=True)  9.35 us
    all_to_all x1, waiting for transfers between devices, per_device(): back = lax.all_to_all(done, 'seq', split_axis=0, concat_axis=0, tiled=True)  8.14 us
    all_to_all x1, starting transfers between devices, per_device(): back = lax.all_to_all(done, 'seq', split_axis=0, concat_axis=0, tiled=True)  6.72 us
    ppermute x1, starting transfers between devices, shift(): return lax.ppermute(array, 'seq', pairs)  3.38 us
    pallas_call x1, Pallas kernels, owner(): pl.pallas_call(owner_kernel, out_shape=jax.ShapeDtypeStruct((chunks, 3 *...  2.73 us
  transfers between devices with their start and end apart: 3, of which 3 were waited for; matrix products, arithmetic and copies ran while one was open for 0% of the time, Pallas kernels for 1%

profile of v2, /device:TPU:24, one launch (start us, length us, event | category | flops | bytes accessed | tf_op | source)
XLA Modules:
  0.0 90.2 jit_solution(17700935164639130907)
XLA Ops:
  0.6 2.2 %gate.1 = (bf16[64,9,2,128]{3,2,1,0:T(2,128)(2,1)}, bf16[16,512]{1,0:T(8,128)(2,1)}) custom-call(bf16[128,512]{1,0:T(8,128)(2,1)} %x1.1, bf16[128,512]{1,0:T(8,128)(2,1)} %x2.1, bf16[128,512]{1,0:T(8,128)(2,1)} %value.1, bf16[128,512]{1,0:T(8,128)(2,1)} %oh.1, f32[3,512]{1,0:T(4,128)} %weight.3), custom_call_target="tpu_custom_call" | custom-call | tf_op jit(solution)/shard_map/gate/pallas_call | solution.py:172
  2.9 0.0 copy-start.12
  2.9 0.0 copy-start.3
  2.9 0.0 copy-start.5
  2.9 0.0 copy-start.6
  2.9 0.0 copy-start.7
  2.9 0.0 copy-start.8
  2.9 0.0 copy-start.9
  3.0 18.9 %all-to-all-start = ((bf16[64,9,2,128]{3,2,1,0:T(2,128)(2,1)}), bf16[64,9,2,128]{3,2,1,0:T(2,128)(2,1)S(1)}, u32[]{:S(2)}, u32[]{:S(2)}) async-start(bf16[64,9,2,128]{3,2,1,0:T(2,128)(2,1)} %get-tuple-element.18), calls=%async_computation | async-start | bytes 589824 | tf_op jit(solution)/shard_map/all_to_all | solution.py:388
  21.8 0.0 copy-start.4
  21.8 0.0 copy-done.12
  21.8 0.1 maximum_bitcast_fusion.rate
  21.9 0.0 copy-start.10
  21.9 0.0 copy-done.3
  21.9 0.0 copy-done.5
  21.9 0.0 copy-done.6
  21.9 0.0 copy-done.7
  21.9 0.0 copy-done.8
  21.9 0.0 copy-done.9
  22.0 0.6 copy-done.4
  22.5 0.1 copy-done.10
  22.6 1.1 %tables.1 = (bf16[256,512]{1,0:T(8,128)(2,1)S(1)}, bf16[256,512]{1,0:T(8,128)(2,1)S(1)}, bf16[128,128]{1,0:T(8,128)(2,1)S(1)}, bf16[128,128]{1,0:T(8,128)(2,1)S(...) custom-call(s32[1]{0:T(128)} %bitcast.place, f32[1,128]{1,0:T(1,128)S(1)} %maximum_bitcast_fusion.rate, ...), custom_call_target="tpu_custom_call" | custom-call | flops 4000000 | bytes 1000000 | tf_op jit(solution)/shard_map/tables/pallas_call | solution.py:107
  23.7 20.4 %all-to-all-done.got = bf16[64,9,2,128]{3,2,1,0:T(2,128)(2,1)S(1)} async-done(((bf16[64,9,2,128]{3,2,1,0:T(2,128)(2,1)}), bf16[64,9,2,128]{3,2,1,0:T(2,128)(2,1)S(1)}, u32[]{:S(2)}, u32[]{:S(2)}) %all-to-all-start) | async-done | bytes 294944 | tf_op jit(solution)/shard_map/all_to_all | solution.py:388
  44.1 2.7 %owner.1 = bf16[64,24,128]{2,1,0:T(8,128)(2,1)} custom-call(s32[1]{0:T(128)} %bitcast.place, bf16[64,9,2,128]{3,2,1,0:T(2,128)(2,1)S(1)} %all-to-all-done.got, bf16[256,512]{1,0:T(8,128)(2,1)S(1)} %get-tuple-element.19.tx, bf16[256,512]{1,0:T(8,128)(2,1)S(1)} %get-tuple-element.20.tg, bf16[128,128]{1,0:T(8,128)(2,1)S(1)} %get-tuple-element.21.mf, ...), custom_call_target="tpu_custom_call" | custom-call | tf_op jit(solution)/shard_map/owner/pallas_call | solution.py:311
  46.8 0.0 copy-start.11
  46.8 0.0 copy-start
  46.8 0.0 copy-start.1
  46.8 0.0 copy-start.2
  46.8 6.7 %all-to-all-start.1 = ((bf16[64,24,128]{2,1,0:T(8,128)(2,1)}), bf16[64,24,128]{2,1,0:T(8,128)(2,1)S(1)}, u32[]{:S(2)}, u32[]{:S(2)}) async-start(bf16[64,24,128]{2,1,0:T(8,128)(2,1)} %owner.1), calls=%async_computation.1 | async-start | bytes 786432 | tf_op jit(solution)/shard_map/all_to_all | solution.py:390
  53.5 0.0 copy-done.11
  53.5 3.4 %collective-permute-start = (bf16[16,512]{1,0:T(8,128)(2,1)S(1)}, bf16[16,512]{1,0:T(8,128)(2,1)S(1)}, u32[]{:S(2)}, u32[]{:S(2)}) collective-permute-start(bf16[16,512]{1,0:T(8,128)(2,1)S(1)} %copy-done.11), channel_id=1, source_target_pairs={{0,8},{8,16},{16,24},{24,32},{32,40},{40,48},{48,56},{56,64},{64,7... | collective-permute-start | bytes 49160 | tf_op jit(solution)/shard_map/ppermute | solution.py:378
  56.9 14.2 %collective-permute-done.tail = bf16[16,512]{1,0:T(8,128)(2,1)S(1)} collective-permute-done((bf16[16,512]{1,0:T(8,128)(2,1)S(1)}, bf16[16,512]{1,0:T(8,128)(2,1)S(1)}, u32[]{:S(2)}, u32[]{:S(2)}) %collective-permute-start) | collective-permute-done | bytes 16416 | tf_op jit(solution)/shard_map/ppermute | solution.py:378
  71.1 8.1 %all-to-all-done.1.back = bf16[64,24,128]{2,1,0:T(8,128)(2,1)S(1)} async-done(((bf16[64,24,128]{2,1,0:T(8,128)(2,1)}), bf16[64,24,128]{2,1,0:T(8,128)(2,1)S(1)}, u32[]{:S(2)}, u32[]{:S(2)}) %all-to-all-start.1) | async-done | bytes 393248 | tf_op jit(solution)/shard_map/all_to_all | solution.py:390
  79.2 0.0 copy-done
  79.3 0.0 copy-done.1
  79.3 0.0 copy-done.2
  79.3 1.1 %finish.1 = (bf16[128,512]{1,0:T(8,128)(2,1)}, bf16[128,512]{1,0:T(8,128)(2,1)}, bf16[128,512]{1,0:T(8,128)(2,1)}, f32[64,512]{1,0:T(8,128)}, f32[8,128]{1,0:T(8,128)S(1)}) custom-call(bf16[64,24,128]{2,1,0:T(8,128)(2,1)S(1)} %all-to-all-done.1.back, bf16[128,512]{1,0:T(8,128)(2,1)S(1)} %copy-done, bf16[128,512]{1,0:T(8,128)(2,1)S(1)} %copy-done.1, ...), custom_call_target="tpu_custom_call" | custom-call | tf_op jit(solution)/shard_map/finish/pallas_call | solution.py:359
  80.3 9.4 %all_to_all.19 = f32[8,1,128]{2,1,0:T(1,128)S(1)} all-to-all(f32[8,1,128]{2,1,0:T(1,128)S(1)} %bitcast.6), channel_id=1, replica_groups=mesh['seq'=64,'chan'=8] {'chan'}, dimensions={0} | all-to-all | bytes 8192 | tf_op jit(solution)/shard_map/all_to_all | solution.py:392
  89.7 0.5 slice_multiply_fusion
  (1 shorter events, 0.0 us)
Async XLA Ops:
  2.9 19.0 %copy-start.12 = (f32[64]{0:T(128)S(1)}, f32[64]{0:T(128)}, u32[]{:S(2)}) copy-start(f32[64]{0:T(128)} %param.19) | copy-start | bytes 772
  2.9 19.0 %copy-start.3 = (f32[64,512]{1,0:T(8,128)S(1)}, f32[64,512]{1,0:T(8,128)}, u32[]{:S(2)}) copy-start(f32[64,512]{1,0:T(8,128)} %coef.1) | copy-start | bytes 393220
  2.9 19.0 %copy-start.5 = (f32[128,128]{1,0:T(8,128)S(1)}, f32[128,128]{1,0:T(8,128)}, u32[]{:S(2)}) copy-start(f32[128,128]{1,0:T(8,128)} %constant.26.clone.wave) | copy-start | bytes 196612
  2.9 19.0 %copy-start.6 = (f32[128,128]{1,0:T(8,128)S(1)}, f32[128,128]{1,0:T(8,128)}, u32[]{:S(2)}) copy-start(f32[128,128]{1,0:T(8,128)} %constant.25.clone.imag_b) | copy-start | bytes 196612
  2.9 19.0 %copy-start.7 = (f32[128,128]{1,0:T(8,128)S(1)}, f32[128,128]{1,0:T(8,128)}, u32[]{:S(2)}) copy-start(f32[128,128]{1,0:T(8,128)} %constant.24.clone.real_b) | copy-start | bytes 196612
  2.9 19.0 %copy-start.8 = (f32[128,128]{1,0:T(8,128)S(1)}, f32[128,128]{1,0:T(8,128)}, u32[]{:S(2)}) copy-start(f32[128,128]{1,0:T(8,128)} %constant.23.clone.sin_a) | copy-start | bytes 196612
  2.9 19.0 %copy-start.9 = (f32[128,128]{1,0:T(8,128)S(1)}, f32[128,128]{1,0:T(8,128)}, u32[]{:S(2)}) copy-start(f32[128,128]{1,0:T(8,128)} %constant.22.clone.cos_a) | copy-start | bytes 196612
  3.0 41.1 %all-to-all-start = ((bf16[64,9,2,128]{3,2,1,0:T(2,128)(2,1)}), bf16[64,9,2,128]{3,2,1,0:T(2,128)(2,1)S(1)}, u32[]{:S(2)}, u32[]{:S(2)}) async-start(bf16[64,9,2,128]{3,2,1,0:T(2,128)(2,1)} %get-tuple-element.18), calls=%async_computation | async-start | bytes 589824 | tf_op jit(solution)/shard_map/all_to_all | solution.py:388
  21.8 0.7 copy-start.4
  21.9 0.7 copy-start.10
  46.8 6.7 %copy-start.11 = (bf16[16,512]{1,0:T(8,128)(2,1)S(1)}, bf16[16,512]{1,0:T(8,128)(2,1)}, u32[]{:S(2)}) copy-start(bf16[16,512]{1,0:T(8,128)(2,1)} %get-tuple-element.25) | copy-start | bytes 49156
  46.8 32.5 %copy-start = (bf16[128,512]{1,0:T(8,128)(2,1)S(1)}, bf16[128,512]{1,0:T(8,128)(2,1)}, u32[]{:S(2)}) copy-start(bf16[128,512]{1,0:T(8,128)(2,1)} %x1.1) | copy-start | bytes 393220
  46.8 32.5 %copy-start.1 = (bf16[128,512]{1,0:T(8,128)(2,1)S(1)}, bf16[128,512]{1,0:T(8,128)(2,1)}, u32[]{:S(2)}) copy-start(bf16[128,512]{1,0:T(8,128)(2,1)} %x2.1) | copy-start | bytes 393220
  46.8 32.5 %copy-start.2 = (bf16[128,512]{1,0:T(8,128)(2,1)S(1)}, bf16[128,512]{1,0:T(8,128)(2,1)}, u32[]{:S(2)}) copy-start(bf16[128,512]{1,0:T(8,128)(2,1)} %value.1) | copy-start | bytes 393220
  46.8 32.4 %all-to-all-start.1 = ((bf16[64,24,128]{2,1,0:T(8,128)(2,1)}), bf16[64,24,128]{2,1,0:T(8,128)(2,1)S(1)}, u32[]{:S(2)}, u32[]{:S(2)}) async-start(bf16[64,24,128]{2,1,0:T(8,128)(2,1)} %owner.1), calls=%async_computation.1 | async-start | bytes 786432 | tf_op jit(solution)/shard_map/all_to_all | solution.py:390
  53.5 17.6 %collective-permute-start = (bf16[16,512]{1,0:T(8,128)(2,1)S(1)}, bf16[16,512]{1,0:T(8,128)(2,1)S(1)}, u32[]{:S(2)}, u32[]{:S(2)}) collective-permute-start(bf16[16,512]{1,0:T(8,128)(2,1)S(1)} %copy-done.11), channel_id=1, source_target_pairs={{0,8},{8,16},{16,24},{24,32},{32,40},{40,48},{48,56},{56,64},{64,7... | collective-permute-start | bytes 49160 | tf_op jit(solution)/shard_map/ppermute | solution.py:378

commit v3 on v2

--- a/solution.py
+++ b/solution.py
@@ -1,3 +1,4 @@
+import functools
 import math
 
 import jax
@@ -184,7 +185,9 @@
     )(x1, x2, value, out_grad, weight)
 
 
-def owner_kernel(place, got, tx, tg, mf, me, wd, small, out, xs, gs, rs, ex, eg, sr, si, gr, gi, yc, yg):
+def owner_kernel(
+    place, got, tx, tg, wd, small, part_out, coef_out, us, ug, xb_out, head_out, gs, rs, ex, eg, sr, si, gr, gi
+):
     chunks = got.shape[0]
     rows = chunks * OWN
     flat = got.reshape(chunks, WORDS, ROWS)
@@ -210,11 +213,11 @@
     )
     before = jnp.concatenate([jnp.zeros((1, OWN, LANES), f32), before[:-1]], axis=0)
     x = both[:, :OWN].reshape(rows, ROWS) + x1_head * before.reshape(rows, LANES)
-    x = x.astype(bf16).astype(f32)
     g = both[:, OWN:].reshape(rows, ROWS)
-    xs[...] = x
     gs[...] = g
     xb = x.astype(bf16)
+    xb_out[...] = xb
+    head_out[...] = x1_head
     gb = g.astype(bf16)
     here = lax.broadcasted_iota(jnp.int32, (ROWS, ROWS), 0)
     there = lax.broadcasted_iota(jnp.int32, (ROWS, ROWS), 1)
@@ -227,7 +230,6 @@
         jnp.concatenate([gb, gb], axis=1), tg[...], preferred_element_type=f32
     )
     scale = small[0]
-    filt = small[1]
     lr = small[2]
     li = small[3]
 
@@ -264,64 +266,105 @@
         - g_i * cube(ex[:, 3 * LANES : 4 * LANES])
     )
     total = jnp.sum(total, axis=0)
-    us = jnp.where(left, scale * s_r, -scale * s_i).reshape(rows, LANES).astype(bf16)
-    ug = jnp.where(left, scale * g_r, -scale * g_i).reshape(rows, LANES).astype(bf16)
-    yc[...] = lax.dot_general(us, mf[...], NT, preferred_element_type=f32)
-    yg[...] = lax.dot_general(ug, me[...], NT, preferred_element_type=f32)
-
-    later = there >= here
+    us[...] = jnp.where(left, scale * s_r, -scale * s_i).reshape(rows, LANES).astype(bf16)
+    ug[...] = jnp.where(left, scale * g_r, -scale * g_i).reshape(rows, LANES).astype(bf16)
+
     inside = (there < here) | (there == ROWS - 1)
     lags = []
     for ch in range(OWN):
         at = pl.ds(ch, chunks, stride=OWN)
-        xc = xs[at, :].astype(bf16)
-        gc = gs[at, :].astype(bf16)
+        pairs = lax.dot_general(
+            rs[at, :].astype(bf16), gs[at, :].astype(bf16), TN, preferred_element_type=f32
+        )
+        pairs = pltpu.roll(pairs, 0, 1, stride=1, stride_axis=0)
+        lags.append(jnp.sum(jnp.where(inside, pairs, 0.0), axis=0, keepdims=True))
+    lags = pltpu.roll(jnp.concatenate(lags, axis=0), 1, 1)
+    total = total + jnp.dot(lags, wd[...], precision=highest, preferred_element_type=f32)
+    coef_out[...] = total * small[5]
+    part = jnp.sum(total * small[4], axis=0, keepdims=True)
+    part_out[...] = jnp.broadcast_to(part + pltpu.roll(part, ORDER, 1), part_out.shape)
+
+
+def owner(place, got, tables, peers):
+    chunks = got.shape[0]
+    rows = chunks * OWN
+    tx, tg, mf, me, wd, small = tables
+    flat = jax.ShapeDtypeStruct((rows, LANES), bf16)
+    return pl.pallas_call(
+        owner_kernel,
+        out_shape=(
+            jax.ShapeDtypeStruct((peers, LANES), f32),
+            jax.ShapeDtypeStruct((OWN, LANES), f32),
+            flat,
+            flat,
+            flat,
+            jax.ShapeDtypeStruct((rows, LANES), f32),
+        ),
+        in_specs=[SMEM] + [VMEM] * 5,
+        out_specs=tuple([VMEM] * 6),
+        scratch_shapes=[pltpu.VMEM((rows, LANES), f32)] * 2
+        + [pltpu.VMEM((rows, 4 * LANES), f32)] * 2
+        + [pltpu.VMEM((rows, LANES), f32)] * 4,
+        compiler_params=pltpu.CompilerParams(vmem_limit_bytes=24 << 20),
+        name="owner",
+    )(place, got, tx, tg, wd, small)
+
+
+def emit_kernel(got, parts, coef, us, ug, xb, head, mf, me, small, out, xs, gs, yc, yg):
+    chunks = got.shape[0]
+    rows = chunks * OWN
+
+    def cube(array):
+        return array.reshape(chunks, OWN, LANES)
+
+    xs[...] = xb[...].astype(f32)
+    gs[...] = got.reshape(chunks, WORDS, ROWS)[:, : 2 * OWN].astype(f32)[:, OWN:].reshape(rows, ROWS)
+    yc[...] = lax.dot_general(us[...], mf[...], NT, preferred_element_type=f32)
+    yg[...] = lax.dot_general(ug[...], me[...], NT, preferred_element_type=f32)
+    here = lax.broadcasted_iota(jnp.int32, (ROWS, ROWS), 0)
+    there = lax.broadcasted_iota(jnp.int32, (ROWS, ROWS), 1)
+    later = there >= here
+    filt = small[1]
+    for ch in range(OWN):
+        at = pl.ds(ch, chunks, stride=OWN)
         toeplitz = pltpu.roll(
             jnp.broadcast_to(filt[ch : ch + 1], (ROWS, ROWS)), 0, 1, stride=1, stride_axis=0
         )
         toeplitz = jnp.where(later, toeplitz, 0.0).astype(bf16)
-        yc[at, :] += jnp.dot(xc, toeplitz, preferred_element_type=f32)
-        yg[at, :] += lax.dot_general(gc, toeplitz, NT, preferred_element_type=f32)
-        pairs = lax.dot_general(rs[at, :].astype(bf16), gc, TN, preferred_element_type=f32)
-        pairs = pltpu.roll(pairs, 0, 1, stride=1, stride_axis=0)
-        lags.append(jnp.sum(jnp.where(inside, pairs, 0.0), axis=0, keepdims=True))
-    lags = pltpu.roll(jnp.concatenate(lags, axis=0), 1, 1)
-    total = total + jnp.dot(lags, wd[...], precision=highest, preferred_element_type=f32)
-
-    part = jnp.sum(total * small[4], axis=0, keepdims=True)
-    part = jnp.broadcast_to(part + pltpu.roll(part, ORDER, 1), (OWN, LANES))
+        yc[at, :] += jnp.dot(xs[at, :].astype(bf16), toeplitz, preferred_element_type=f32)
+        yg[at, :] += lax.dot_general(gs[at, :].astype(bf16), toeplitz, NT, preferred_element_type=f32)
+
+    row = lax.broadcasted_iota(jnp.int32, (OWN, LANES), 0)
+    lane = lax.broadcasted_iota(jnp.int32, (OWN, LANES), 1)
+    part = jnp.broadcast_to(jnp.sum(parts[...], axis=0, keepdims=True), (OWN, LANES))
     moved = pltpu.roll(part, 2, 1)
     low = part - part.astype(bf16).astype(f32)
     low_moved = moved - moved.astype(bf16).astype(f32)
-    row = lax.broadcasted_iota(jnp.int32, (OWN, LANES), 0)
-    lane = lax.broadcasted_iota(jnp.int32, (OWN, LANES), 1)
     part = jnp.where(row == 0, part, jnp.where(row == 1, moved, jnp.where(row == 2, low, low_moved)))
-    extra = jnp.where(left, total * small[5], jnp.where(row < 4, part, 0.0))
-    grad = cube(yg[...])
-    heads = cube(pltpu.roll(yg[...], ORDER, 1) * x1_head)
+    extra = jnp.where(lane < ORDER, coef[...], jnp.where(row < 4, part, 0.0))
+    heads = cube(pltpu.roll(yg[...], ORDER, 1) * head[...])
     heads = jnp.concatenate([heads[1:], jnp.zeros((1, OWN, LANES), f32)], axis=0)
     is_head = (lane >= ORDER) & (lane < ORDER + 2)
     extra = jnp.where(is_head, heads, extra)
-    out[...] = jnp.concatenate([cube(yc[...]), grad, extra], axis=1).astype(bf16)
-
-
-def owner(place, got, tables):
+    out[...] = jnp.concatenate([cube(yc[...]), cube(yg[...]), extra], axis=1).astype(bf16)
+
+
+def emit(got, parts, made, tables):
     chunks = got.shape[0]
     rows = chunks * OWN
+    tx, tg, mf, me, wd, small = tables
     return pl.pallas_call(
-        owner_kernel,
+        emit_kernel,
         out_shape=jax.ShapeDtypeStruct((chunks, 3 * OWN, ROWS), bf16),
-        in_specs=[SMEM] + [VMEM] * 7,
+        in_specs=[VMEM] * 10,
         out_specs=VMEM,
-        scratch_shapes=[pltpu.VMEM((rows, LANES), f32)] * 3
-        + [pltpu.VMEM((rows, 4 * LANES), f32)] * 2
-        + [pltpu.VMEM((rows, LANES), f32)] * 6,
+        scratch_shapes=[pltpu.VMEM((rows, LANES), f32)] * 4,
         compiler_params=pltpu.CompilerParams(vmem_limit_bytes=24 << 20),
-        name="owner",
-    )(place, got, *tables)
-
-
-def finish_kernel(back, x1, x2, value, tail, weight, y, gx1, gvalue, gcoef, rates):
+        name="emit",
+    )(got, parts, *made, mf, me, small)
+
+
+def finish_kernel(peers, back, x1, x2, value, tail, weight, y, gx1, gvalue, gcoef, grate):
     shards = back.shape[0]
     wide = shards * OWN
     every = back[...].astype(f32)
@@ -334,9 +377,8 @@
     lane = lax.broadcasted_iota(jnp.int32, (1, LANES), 1)
     most = part[0:1] + part[2:3]
     few = part[1:2] + part[3:4]
-    rates[...] = jnp.broadcast_to(
-        jnp.where(lane < 2, pltpu.roll(few, ORDER - 2, 1), pltpu.roll(most, ORDER, 1)), rates.shape
-    )
+    rates = jnp.where(lane < 2, pltpu.roll(few, ORDER - 2, 1), pltpu.roll(most, ORDER, 1))
+    grate[...] = rates[:, :ORDER] * (LENGTH * wide * peers) ** -0.5
     first = x1[...].astype(f32)
     w = weight[...]
     y[...] = (x2[...].astype(f32) * conv).astype(bf16)
@@ -357,13 +399,13 @@
 def finish(back, x1, x2, value, tail, weight, peers):
     shape = jax.ShapeDtypeStruct(x1.shape, bf16)
     return pl.pallas_call(
-        finish_kernel,
+        functools.partial(finish_kernel, peers),
         out_shape=(
             shape,
             shape,
             shape,
             jax.ShapeDtypeStruct((ORDER, x1.shape[1]), f32),
-            jax.ShapeDtypeStruct((peers, LANES), f32),
+            jax.ShapeDtypeStruct((1, ORDER), f32),
         ),
         in_specs=[VMEM] * 6,
         out_specs=tuple([VMEM] * 5),
@@ -380,18 +422,17 @@
 
 def per_device(x1, x2, value, out_grad, short_weight, coef, rate):
     peers = lax.axis_size("chan")
-    width = x1.shape[1]
     place = lax.axis_index("seq").astype(jnp.int32)[None]
     tables = make_tables(place, rate, coef, short_weight)
     sent, tail = gate(x1, x2, value, out_grad, short_weight)
     tail = shift(tail, 1)
     got = lax.all_to_all(sent, "seq", split_axis=0, concat_axis=0, tiled=True)
-    done = owner(place, got, tables)
+    part, *made = owner(place, got, tables, peers)
+    parts = lax.all_to_all(part, "chan", split_axis=0, concat_axis=0, tiled=True)
+    done = emit(got, parts, made, tables)
     back = lax.all_to_all(done, "seq", split_axis=0, concat_axis=0, tiled=True)
-    y, gx1, gvalue, gcoef, rates = finish(back, x1, x2, value, tail, short_weight, peers)
-    rates = lax.all_to_all(rates, "chan", split_axis=0, concat_axis=0, tiled=True)
-    grad_rate = jnp.sum(rates, axis=0)[:ORDER] * (LENGTH * width * peers) ** -0.5
-    return (y, gx1, gvalue, gcoef, grad_rate)
+    y, gx1, gvalue, gcoef, grate = finish(back, x1, x2, value, tail, short_weight, peers)
+    return (y, gx1, gvalue, gcoef, grate.reshape(ORDER))
 
 
 def solution(mesh):

time: 91.4 us -> 90.8 us (level)
    pallas_call x2 -> x3, Pallas kernels: 3.81 us -> 3.95 us  [the longest x1 1.43 us: emit(): pl.pallas_call(emit_kernel, out_shape=jax.ShapeDtypeStruct((chunks, 3 * O...]
where the time goes in v3:
time: 90.8 us; the launch traced here: 90.4 us
  waiting for transfers between devices  43.3 us (48%)
  starting transfers between devices  28.9 us (32%)
  blocking collectives  9.38 us (10%)
  Pallas kernels  7.29 us (8%)
    all_to_all x1, waiting for transfers between devices, per_device(): got = lax.all_to_all(sent, 'seq', split_axis=0, concat_axis=0, tiled=True)  20.4 us
    all_to_all x1, starting transfers between devices, per_device(): got = lax.all_to_all(sent, 'seq', split_axis=0, concat_axis=0, tiled=True)  18.9 us
    ppermute x1, waiting for transfers between devices, shift(): return lax.ppermute(array, 'seq', pairs)  15 us
    all_to_all x1, blocking collectives, per_device(): lax.all_to_all(part, 'chan', split_axis=0, concat_axis=0, tiled=True)  9.38 us
    all_to_all x1, waiting for transfers between devices, per_device(): back = lax.all_to_all(done, 'seq', split_axis=0, concat_axis=0, tiled=True)  7.91 us
    all_to_all x1, starting transfers between devices, per_device(): back = lax.all_to_all(done, 'seq', split_axis=0, concat_axis=0, tiled=True)  6.71 us
    ppermute x1, starting transfers between devices, shift(): return lax.ppermute(array, 'seq', pairs)  3.38 us
    pallas_call x1, Pallas kernels, gate(): pl.pallas_call(gate_kernel, out_shape=(jax.ShapeDtypeStruct((shards, WORD...  2.23 us
  transfers between devices with their start and end apart: 3, of which 3 were waited for; matrix products, arithmetic and copies ran while one was open for 0% of the time, Pallas kernels for 1%

profile of v3, /device:TPU:24, one launch (start us, length us, event | category | flops | bytes accessed | tf_op | source)
XLA Modules:
  0.0 90.4 jit_solution(14892958494695158471)
XLA Ops:
  0.6 2.2 %gate.1 = (bf16[64,9,2,128]{3,2,1,0:T(2,128)(2,1)}, bf16[16,512]{1,0:T(8,128)(2,1)}) custom-call(bf16[128,512]{1,0:T(8,128)(2,1)} %x1.1, bf16[128,512]{1,0:T(8,128)(2,1)} %x2.1, bf16[128,512]{1,0:T(8,128)(2,1)} %value.1, bf16[128,512]{1,0:T(8,128)(2,1)} %oh.1, f32[3,512]{1,0:T(4,128)} %weight.3), custom_call_target="tpu_custom_call" | custom-call | tf_op jit(solution)/shard_map/gate/pallas_call | solution.py:173
  2.9 0.0 copy-start.12
  2.9 0.0 copy-start.3
  2.9 0.0 copy-start.5
  2.9 0.0 copy-start.6
  2.9 0.0 copy-start.7
  2.9 0.0 copy-start.8
  2.9 0.0 copy-start.9
  3.0 18.9 %all-to-all-start = ((bf16[64,9,2,128]{3,2,1,0:T(2,128)(2,1)}), bf16[64,9,2,128]{3,2,1,0:T(2,128)(2,1)S(1)}, u32[]{:S(2)}, u32[]{:S(2)}) async-start(bf16[64,9,2,128]{3,2,1,0:T(2,128)(2,1)} %get-tuple-element.24), calls=%async_computation | async-start | bytes 589824 | tf_op jit(solution)/shard_map/all_to_all | solution.py:429
  21.8 0.0 copy-start.4
  21.8 0.0 copy-done.12
  21.8 0.1 maximum_bitcast_fusion.rate
  21.9 0.0 copy-start.10
  21.9 0.0 copy-done.3
  21.9 0.0 copy-done.5
  21.9 0.0 copy-done.6
  21.9 0.0 copy-done.7
  21.9 0.0 copy-done.8
  22.0 0.0 copy-done.9
  22.0 0.6 copy-done.4
  22.5 0.1 copy-done.10
  22.6 1.1 %tables.1 = (bf16[256,512]{1,0:T(8,128)(2,1)S(1)}, bf16[256,512]{1,0:T(8,128)(2,1)S(1)}, bf16[128,128]{1,0:T(8,128)(2,1)S(1)}, bf16[128,128]{1,0:T(8,128)(2,1)S(...) custom-call(s32[1]{0:T(128)} %bitcast.place, f32[1,128]{1,0:T(1,128)S(1)} %maximum_bitcast_fusion.rate, ...), custom_call_target="tpu_custom_call" | custom-call | flops 4000000 | bytes 1000000 | tf_op jit(solution)/shard_map/tables/pallas_call | solution.py:108
  23.7 20.4 %all-to-all-done.got = bf16[64,9,2,128]{3,2,1,0:T(2,128)(2,1)S(1)} async-done(((bf16[64,9,2,128]{3,2,1,0:T(2,128)(2,1)}), bf16[64,9,2,128]{3,2,1,0:T(2,128)(2,1)S(1)}, u32[]{:S(2)}, u32[]{:S(2)}) %all-to-all-start) | async-done | bytes 294944 | tf_op jit(solution)/shard_map/all_to_all | solution.py:429
  44.1 1.4 %owner.1 = (f32[8,128]{1,0:T(8,128)S(1)}, f32[8,128]{1,0:T(8,128)S(1)}, bf16[512,128]{1,0:T(8,128)(2,1)S(1)}, bf16[512,128]{1,0:T(8,128)(2,1)S(1)}, bf16[512,128...) custom-call(s32[1]{0:T(128)} %bitcast.place, bf16[64,9,2,128]{3,2,1,0:T(2,128)(2,1)S(1)} %all-to-all-done.got, ...), custom_call_target="tpu_custom_call" | custom-call | tf_op jit(solution)/shard_map/owner/pallas_call | solution.py:293
  45.5 9.4 %all_to_all.21 = f32[8,1,128]{2,1,0:T(1,128)S(1)} all-to-all(f32[8,1,128]{2,1,0:T(1,128)S(1)} %bitcast.9), channel_id=1, replica_groups=mesh['seq'=64,'chan'=8] {'chan'}, dimensions={0} | all-to-all | bytes 8192 | tf_op jit(solution)/shard_map/all_to_all | solution.py:431
  54.9 1.4 %emit.1 = bf16[64,24,128]{2,1,0:T(8,128)(2,1)} custom-call(bf16[64,9,2,128]{3,2,1,0:T(2,128)(2,1)S(1)} %all-to-all-done.got, f32[8,128]{1,0:T(8,128)S(1)} %bitcast.8, f32[8,128]{1,0:T(8,128)S(1)} %get-tuple-element.30.coef, bf16[512,128]{1,0:T(8,128)(2,1)S(1)} %get-tuple-element.31.us, bf16[512,128]{1,0:T(8,128)(2,1)S(1)} %get-tuple-element.32.ug, ...), custom_call_target="tpu_custom_call" | custom-call | tf_op jit(solution)/shard_map/emit/pallas_call | solution.py:356
  56.3 0.0 copy-start.11
  56.3 0.0 copy-start
  56.3 0.0 copy-start.1
  56.3 0.0 copy-start.2
  56.3 6.7 %all-to-all-start.2 = ((bf16[64,24,128]{2,1,0:T(8,128)(2,1)}), bf16[64,24,128]{2,1,0:T(8,128)(2,1)S(1)}, u32[]{:S(2)}, u32[]{:S(2)}) async-start(bf16[64,24,128]{2,1,0:T(8,128)(2,1)} %emit.1), calls=%async_computation.2 | async-start | bytes 786432 | tf_op jit(solution)/shard_map/all_to_all | solution.py:433
  63.0 0.0 copy-done.11
  63.0 3.4 %collective-permute-start = (bf16[16,512]{1,0:T(8,128)(2,1)S(1)}, bf16[16,512]{1,0:T(8,128)(2,1)S(1)}, u32[]{:S(2)}, u32[]{:S(2)}) collective-permute-start(bf16[16,512]{1,0:T(8,128)(2,1)S(1)} %copy-done.11), channel_id=1, source_target_pairs={{0,8},{8,16},{16,24},{24,32},{32,40},{40,48},{48,56},{56,64},{64,7... | collective-permute-start | bytes 49160 | tf_op jit(solution)/shard_map/ppermute | solution.py:420
  66.4 15.0 %collective-permute-done.tail = bf16[16,512]{1,0:T(8,128)(2,1)S(1)} collective-permute-done((bf16[16,512]{1,0:T(8,128)(2,1)S(1)}, bf16[16,512]{1,0:T(8,128)(2,1)S(1)}, u32[]{:S(2)}, u32[]{:S(2)}) %collective-permute-start) | collective-permute-done | bytes 16416 | tf_op jit(solution)/shard_map/ppermute | solution.py:420
  81.4 7.9 %all-to-all-done.2.back = bf16[64,24,128]{2,1,0:T(8,128)(2,1)S(1)} async-done(((bf16[64,24,128]{2,1,0:T(8,128)(2,1)}), bf16[64,24,128]{2,1,0:T(8,128)(2,1)S(1)}, u32[]{:S(2)}, u32[]{:S(2)}) %all-to-all-start.2) | async-done | bytes 393248 | tf_op jit(solution)/shard_map/all_to_all | solution.py:433
  89.3 0.0 copy-done
  89.3 0.0 copy-done.1
  89.4 0.0 copy-done.2
  89.4 1.1 %finish.1 = (bf16[128,512]{1,0:T(8,128)(2,1)}, bf16[128,512]{1,0:T(8,128)(2,1)}, bf16[128,512]{1,0:T(8,128)(2,1)}, f32[64,512]{1,0:T(8,128)}, f32[1,64]{1,0:T(1,128)}) custom-call(bf16[64,24,128]{2,1,0:T(8,128)(2,1)S(1)} %all-to-all-done.2.back, bf16[128,512]{1,0:T(8,128)(2,1)S(1)} %copy-done, bf16[128,512]{1,0:T(8,128)(2,1)S(1)} %copy-done.1, ...), custom_call_target="tpu_custom_call" | custom-call | tf_op jit(solution)/shard_map/finish/pallas_call | solution.py:401
Async XLA Ops:
  2.9 19.0 %copy-start.12 = (f32[64]{0:T(128)S(1)}, f32[64]{0:T(128)}, u32[]{:S(2)}) copy-start(f32[64]{0:T(128)} %param.19) | copy-start | bytes 772
  2.9 19.0 %copy-start.3 = (f32[64,512]{1,0:T(8,128)S(1)}, f32[64,512]{1,0:T(8,128)}, u32[]{:S(2)}) copy-start(f32[64,512]{1,0:T(8,128)} %coef.1) | copy-start | bytes 393220
  2.9 19.0 %copy-start.5 = (f32[128,128]{1,0:T(8,128)S(1)}, f32[128,128]{1,0:T(8,128)}, u32[]{:S(2)}) copy-start(f32[128,128]{1,0:T(8,128)} %constant.22.clone.wave) | copy-start | bytes 196612
  2.9 19.0 %copy-start.6 = (f32[128,128]{1,0:T(8,128)S(1)}, f32[128,128]{1,0:T(8,128)}, u32[]{:S(2)}) copy-start(f32[128,128]{1,0:T(8,128)} %constant.21.clone.imag_b) | copy-start | bytes 196612
  2.9 19.0 %copy-start.7 = (f32[128,128]{1,0:T(8,128)S(1)}, f32[128,128]{1,0:T(8,128)}, u32[]{:S(2)}) copy-start(f32[128,128]{1,0:T(8,128)} %constant.20.clone.real_b) | copy-start | bytes 196612
  2.9 19.0 %copy-start.8 = (f32[128,128]{1,0:T(8,128)S(1)}, f32[128,128]{1,0:T(8,128)}, u32[]{:S(2)}) copy-start(f32[128,128]{1,0:T(8,128)} %constant.19.clone.sin_a) | copy-start | bytes 196612
  2.9 19.0 %copy-start.9 = (f32[128,128]{1,0:T(8,128)S(1)}, f32[128,128]{1,0:T(8,128)}, u32[]{:S(2)}) copy-start(f32[128,128]{1,0:T(8,128)} %constant.18.clone.cos_a) | copy-start | bytes 196612
  3.0 41.1 %all-to-all-start = ((bf16[64,9,2,128]{3,2,1,0:T(2,128)(2,1)}), bf16[64,9,2,128]{3,2,1,0:T(2,128)(2,1)S(1)}, u32[]{:S(2)}, u32[]{:S(2)}) async-start(bf16[64,9,2,128]{3,2,1,0:T(2,128)(2,1)} %get-tuple-element.24), calls=%async_computation | async-start | bytes 589824 | tf_op jit(solution)/shard_map/all_to_all | solution.py:429
  21.8 0.7 copy-start.4
  21.9 0.7 copy-start.10
  56.3 6.7 %copy-start.11 = (bf16[16,512]{1,0:T(8,128)(2,1)S(1)}, bf16[16,512]{1,0:T(8,128)(2,1)}, u32[]{:S(2)}) copy-start(bf16[16,512]{1,0:T(8,128)(2,1)} %get-tuple-element.37) | copy-start | bytes 49156
  56.3 33.0 %copy-start = (bf16[128,512]{1,0:T(8,128)(2,1)S(1)}, bf16[128,512]{1,0:T(8,128)(2,1)}, u32[]{:S(2)}) copy-start(bf16[128,512]{1,0:T(8,128)(2,1)} %x1.1) | copy-start | bytes 393220
  56.3 33.0 %copy-start.1 = (bf16[128,512]{1,0:T(8,128)(2,1)S(1)}, bf16[128,512]{1,0:T(8,128)(2,1)}, u32[]{:S(2)}) copy-start(bf16[128,512]{1,0:T(8,128)(2,1)} %x2.1) | copy-start | bytes 393220
  56.3 33.0 %copy-start.2 = (bf16[128,512]{1,0:T(8,128)(2,1)S(1)}, bf16[128,512]{1,0:T(8,128)(2,1)}, u32[]{:S(2)}) copy-start(bf16[128,512]{1,0:T(8,128)(2,1)} %value.1) | copy-start | bytes 393220
  56.3 33.0 %all-to-all-start.2 = ((bf16[64,24,128]{2,1,0:T(8,128)(2,1)}), bf16[64,24,128]{2,1,0:T(8,128)(2,1)S(1)}, u32[]{:S(2)}, u32[]{:S(2)}) async-start(bf16[64,24,128]{2,1,0:T(8,128)(2,1)} %emit.1), calls=%async_computation.2 | async-start | bytes 786432 | tf_op jit(solution)/shard_map/all_to_all | solution.py:433
  63.0 18.4 %collective-permute-start = (bf16[16,512]{1,0:T(8,128)(2,1)S(1)}, bf16[16,512]{1,0:T(8,128)(2,1)S(1)}, u32[]{:S(2)}, u32[]{:S(2)}) collective-permute-start(bf16[16,512]{1,0:T(8,128)(2,1)S(1)} %copy-done.11), channel_id=1, source_target_pairs={{0,8},{8,16},{16,24},{24,32},{32,40},{40,48},{48,56},{56,64},{64,7... | collective-permute-start | bytes 49160 | tf_op jit(solution)/shard_map/ppermute | solution.py:420

commit v4 on v3

--- a/solution.py
+++ b/solution.py
@@ -18,6 +18,7 @@
 LANES = 128
 OWN = 8
 WORDS = 2 * OWN + 2
+BACK = 2 * OWN + 6
 NT = (((1,), (1,)), ((), ()))
 TN = (((0,), (0,)), ((), ()))
 
@@ -334,19 +335,29 @@
         yc[at, :] += jnp.dot(xs[at, :].astype(bf16), toeplitz, preferred_element_type=f32)
         yg[at, :] += lax.dot_general(gs[at, :].astype(bf16), toeplitz, NT, preferred_element_type=f32)
 
+    flat = out.reshape(chunks, BACK, ROWS)
+    flat[:, : 2 * OWN] = jnp.concatenate([cube(yc[...]), cube(yg[...])], axis=1).astype(bf16)
+    lane = lax.broadcasted_iota(jnp.int32, (OWN, LANES), 1)
     row = lax.broadcasted_iota(jnp.int32, (OWN, LANES), 0)
-    lane = lax.broadcasted_iota(jnp.int32, (OWN, LANES), 1)
-    part = jnp.broadcast_to(jnp.sum(parts[...], axis=0, keepdims=True), (OWN, LANES))
-    moved = pltpu.roll(part, 2, 1)
+    both = jnp.where(lane < ORDER, coef[...], pltpu.roll(pltpu.roll(coef[...], ORDER, 1), OWN // 2, 0))
+    flat[:, 2 * OWN : 2 * OWN + 4] = jnp.broadcast_to(both[: OWN // 2], (chunks, OWN // 2, LANES)).astype(bf16)
+    heads = (pltpu.roll(yg[...], ORDER, 1) * head[...]).astype(bf16)
+    heads = cube(jnp.dot(heads, head_spots(False), preferred_element_type=f32))
+    heads = jnp.sum(jnp.where((lane - ORDER) // 2 == row, heads, 0.0), axis=1, keepdims=True)
+    heads = jnp.concatenate([heads[1:], jnp.zeros((1, 1, LANES), f32)], axis=0)
+    part = jnp.sum(parts[...], axis=0, keepdims=True)
     low = part - part.astype(bf16).astype(f32)
-    low_moved = moved - moved.astype(bf16).astype(f32)
-    part = jnp.where(row == 0, part, jnp.where(row == 1, moved, jnp.where(row == 2, low, low_moved)))
-    extra = jnp.where(lane < ORDER, coef[...], jnp.where(row < 4, part, 0.0))
-    heads = cube(pltpu.roll(yg[...], ORDER, 1) * head[...])
-    heads = jnp.concatenate([heads[1:], jnp.zeros((1, OWN, LANES), f32)], axis=0)
-    is_head = (lane >= ORDER) & (lane < ORDER + 2)
-    extra = jnp.where(is_head, heads, extra)
-    out[...] = jnp.concatenate([cube(yc[...]), cube(yg[...]), extra], axis=1).astype(bf16)
+    left = lane[:1] < ORDER
+    high = jnp.where(left, part, heads)
+    low = jnp.broadcast_to(jnp.where(left, low, 0.0), (chunks, 1, LANES))
+    flat[:, 2 * OWN + 4 :] = jnp.concatenate([high, low], axis=1).astype(bf16)
+
+
+def head_spots(turned):
+    few = lax.broadcasted_iota(jnp.int32, (LANES, LANES), 1 if turned else 0)
+    many = lax.broadcasted_iota(jnp.int32, (LANES, LANES), 0 if turned else 1)
+    hit = (few // 2 == ORDER // 2) & (many >= ORDER) & (many < ORDER + 2 * OWN) & (few % 2 == many % 2)
+    return hit.astype(bf16)
 
 
 def emit(got, parts, made, tables):
@@ -355,7 +366,7 @@
     tx, tg, mf, me, wd, small = tables
     return pl.pallas_call(
         emit_kernel,
-        out_shape=jax.ShapeDtypeStruct((chunks, 3 * OWN, ROWS), bf16),
+        out_shape=jax.ShapeDtypeStruct((chunks, BACK // 2, 2, ROWS), bf16),
         in_specs=[VMEM] * 10,
         out_specs=VMEM,
         scratch_shapes=[pltpu.VMEM((rows, LANES), f32)] * 4,
@@ -367,18 +378,22 @@
 def finish_kernel(peers, back, x1, x2, value, tail, weight, y, gx1, gvalue, gcoef, grate):
     shards = back.shape[0]
     wide = shards * OWN
-    every = back[...].astype(f32)
-    conv = every[:, :OWN].reshape(wide, ROWS).T
-    grad = every[:, OWN : 2 * OWN].reshape(wide, ROWS).T
-    extra = every[:, 2 * OWN :]
-    turned = extra.reshape(wide, LANES).T
+    every = back.reshape(shards, BACK, ROWS)
+    both = every[:, : 2 * OWN].astype(f32)
+    conv = both[:, :OWN].reshape(wide, ROWS).T
+    grad = both[:, OWN:].reshape(wide, ROWS).T
+    both = every[:, 2 * OWN : 2 * OWN + 4].astype(f32)
+    both = jnp.concatenate([both, pltpu.roll(both, ORDER, 2)], axis=1).reshape(wide, LANES)
+    rest = every[:, 2 * OWN + 4 :].astype(f32)
+    rates = jnp.sum(jnp.sum(rest, axis=0), axis=0, keepdims=True)
+    grate[...] = rates[:, :ORDER] * (LENGTH * wide * peers) ** -0.5
+    lane = lax.broadcasted_iota(jnp.int32, (shards, OWN, LANES), 2)
+    row = lax.broadcasted_iota(jnp.int32, (shards, OWN, LANES), 1)
+    heads = jnp.where((lane - ORDER) // 2 == row, jnp.broadcast_to(rest[:, :1], lane.shape), 0.0)
+    heads = jnp.dot(heads.reshape(wide, LANES).astype(bf16), head_spots(True), preferred_element_type=f32)
+    lane = lax.broadcasted_iota(jnp.int32, (wide, LANES), 1)
+    turned = jnp.where(lane < ORDER, both, heads).T
     gcoef[...] = turned[:ORDER]
-    part = jnp.sum(extra, axis=0)
-    lane = lax.broadcasted_iota(jnp.int32, (1, LANES), 1)
-    most = part[0:1] + part[2:3]
-    few = part[1:2] + part[3:4]
-    rates = jnp.where(lane < 2, pltpu.roll(few, ORDER - 2, 1), pltpu.roll(most, ORDER, 1))
-    grate[...] = rates[:, :ORDER] * (LENGTH * wide * peers) ** -0.5
     first = x1[...].astype(f32)
     w = weight[...]
     y[...] = (x2[...].astype(f32) * conv).astype(bf16)

time: 90.8 us -> 90 us (level)
  waiting for transfers between devices: 43.3 us -> 42 us
    ppermute x1, waiting for transfers between devices: 15 us -> 13.5 us  [shift(): return lax.ppermute(array, 'seq', pairs)]
where the time goes in v4:
time: 90 us; the launch traced here: 89.7 us
  waiting for transfers between devices  42 us (47%)
  starting transfers between devices  28.9 us (32%)
  blocking collectives  9.38 us (10%)
  Pallas kernels  7.78 us (9%)
    all_to_all x1, waiting for transfers between devices, per_device(): got = lax.all_to_all(sent, 'seq', split_axis=0, concat_axis=0, tiled=True)  20.4 us
    all_to_all x1, starting transfers between devices, per_device(): got = lax.all_to_all(sent, 'seq', split_axis=0, concat_axis=0, tiled=True)  18.9 us
    ppermute x1, waiting for transfers between devices, shift(): return lax.ppermute(array, 'seq', pairs)  13.5 us
    all_to_all x1, blocking collectives, per_device(): lax.all_to_all(part, 'chan', split_axis=0, concat_axis=0, tiled=True)  9.38 us
    all_to_all x1, waiting for transfers between devices, per_device(): back = lax.all_to_all(done, 'seq', split_axis=0, concat_axis=0, tiled=True)  8.18 us
    all_to_all x1, starting transfers between devices, per_device(): back = lax.all_to_all(done, 'seq', split_axis=0, concat_axis=0, tiled=True)  6.71 us
    ppermute x1, starting transfers between devices, shift(): return lax.ppermute(array, 'seq', pairs)  3.38 us
    pallas_call x1, Pallas kernels, gate(): pl.pallas_call(gate_kernel, out_shape=(jax.ShapeDtypeStruct((shards, WORD...  2.23 us
  transfers between devices with their start and end apart: 3, of which 3 were waited for; matrix products, arithmetic and copies ran while one was open for 0% of the time, Pallas kernels for 1%

profile of v4, /device:TPU:24, one launch (start us, length us, event | category | flops | bytes accessed | tf_op | source)
XLA Modules:
  0.0 89.7 jit_solution(13086107221849868338)
XLA Ops:
  0.6 2.2 %gate.1 = (bf16[64,9,2,128]{3,2,1,0:T(2,128)(2,1)}, bf16[16,512]{1,0:T(8,128)(2,1)}) custom-call(bf16[128,512]{1,0:T(8,128)(2,1)} %x1.1, bf16[128,512]{1,0:T(8,128)(2,1)} %x2.1, bf16[128,512]{1,0:T(8,128)(2,1)} %value.1, bf16[128,512]{1,0:T(8,128)(2,1)} %oh.1, f32[3,512]{1,0:T(4,128)} %weight.3), custom_call_target="tpu_custom_call" | custom-call | tf_op jit(solution)/shard_map/gate/pallas_call | solution.py:174
  2.9 0.0 copy-start.12
  2.9 0.0 copy-start.3
  2.9 0.0 copy-start.5
  2.9 0.0 copy-start.6
  2.9 0.0 copy-start.7
  2.9 0.0 copy-start.8
  2.9 0.0 copy-start.9
  3.0 18.9 %all-to-all-start = ((bf16[64,9,2,128]{3,2,1,0:T(2,128)(2,1)}), bf16[64,9,2,128]{3,2,1,0:T(2,128)(2,1)S(1)}, u32[]{:S(2)}, u32[]{:S(2)}) async-start(bf16[64,9,2,128]{3,2,1,0:T(2,128)(2,1)} %get-tuple-element.24), calls=%async_computation | async-start | bytes 589824 | tf_op jit(solution)/shard_map/all_to_all | solution.py:444
  21.8 0.0 copy-start.4
  21.8 0.0 copy-done.12
  21.8 0.1 maximum_bitcast_fusion.rate
  21.9 0.0 copy-start.10
  21.9 0.0 copy-done.3
  21.9 0.0 copy-done.5
  21.9 0.0 copy-done.6
  21.9 0.0 copy-done.7
  21.9 0.0 copy-done.8
  22.0 0.0 copy-done.9
  22.0 0.6 copy-done.4
  22.5 0.1 copy-done.10
  22.6 1.1 %tables.1 = (bf16[256,512]{1,0:T(8,128)(2,1)S(1)}, bf16[256,512]{1,0:T(8,128)(2,1)S(1)}, bf16[128,128]{1,0:T(8,128)(2,1)S(1)}, bf16[128,128]{1,0:T(8,128)(2,1)S(...) custom-call(s32[1]{0:T(128)} %bitcast.place, f32[1,128]{1,0:T(1,128)S(1)} %maximum_bitcast_fusion.rate, ...), custom_call_target="tpu_custom_call" | custom-call | flops 4000000 | bytes 1000000 | tf_op jit(solution)/shard_map/tables/pallas_call | solution.py:109
  23.7 20.4 %all-to-all-done.got = bf16[64,9,2,128]{3,2,1,0:T(2,128)(2,1)S(1)} async-done(((bf16[64,9,2,128]{3,2,1,0:T(2,128)(2,1)}), bf16[64,9,2,128]{3,2,1,0:T(2,128)(2,1)S(1)}, u32[]{:S(2)}, u32[]{:S(2)}) %all-to-all-start) | async-done | bytes 294944 | tf_op jit(solution)/shard_map/all_to_all | solution.py:444
  44.1 1.4 %owner.1 = (f32[8,128]{1,0:T(8,128)S(1)}, f32[8,128]{1,0:T(8,128)S(1)}, bf16[512,128]{1,0:T(8,128)(2,1)S(1)}, bf16[512,128]{1,0:T(8,128)(2,1)S(1)}, bf16[512,128...) custom-call(s32[1]{0:T(128)} %bitcast.place, bf16[64,9,2,128]{3,2,1,0:T(2,128)(2,1)S(1)} %all-to-all-done.got, ...), custom_call_target="tpu_custom_call" | custom-call | tf_op jit(solution)/shard_map/owner/pallas_call | solution.py:294
  45.5 9.4 %all_to_all.21 = f32[8,1,128]{2,1,0:T(1,128)S(1)} all-to-all(f32[8,1,128]{2,1,0:T(1,128)S(1)} %bitcast.9), channel_id=1, replica_groups=mesh['seq'=64,'chan'=8] {'chan'}, dimensions={0} | all-to-all | bytes 8192 | tf_op jit(solution)/shard_map/all_to_all | solution.py:446
  54.9 1.7 %emit.1 = bf16[64,11,2,128]{3,2,1,0:T(2,128)(2,1)} custom-call(bf16[64,9,2,128]{3,2,1,0:T(2,128)(2,1)S(1)} %all-to-all-done.got, f32[8,128]{1,0:T(8,128)S(1)} %bitcast.8, f32[8,128]{1,0:T(8,128)S(1)} %get-tuple-element.30.coef, bf16[512,128]{1,0:T(8,128)(2,1)S(1)} %get-tuple-element.31.us, bf16[512,128]{1,0:T(8,128)(2,1)S(1)} %get-tuple-element.32.ug, ...), custom_call_target="tpu_custom_call" | custom-call | tf_op jit(solution)/shard_map/emit/pallas_call | solution.py:367
  56.6 0.0 copy-start.11
  56.6 0.0 copy-start
  56.6 0.0 copy-start.1
  56.6 0.0 copy-start.2
  56.6 6.7 %all-to-all-start.2 = ((bf16[64,11,2,128]{3,2,1,0:T(2,128)(2,1)}), bf16[64,11,2,128]{3,2,1,0:T(2,128)(2,1)S(1)}, u32[]{:S(2)}, u32[]{:S(2)}) async-start(bf16[64,11,2,128]{3,2,1,0:T(2,128)(2,1)} %emit.1), calls=%async_computation.2 | async-start | bytes 720896 | tf_op jit(solution)/shard_map/all_to_all | solution.py:448
  63.3 0.0 copy-done.11
  63.3 3.4 %collective-permute-start = (bf16[16,512]{1,0:T(8,128)(2,1)S(1)}, bf16[16,512]{1,0:T(8,128)(2,1)S(1)}, u32[]{:S(2)}, u32[]{:S(2)}) collective-permute-start(bf16[16,512]{1,0:T(8,128)(2,1)S(1)} %copy-done.11), channel_id=1, source_target_pairs={{0,8},{8,16},{16,24},{24,32},{32,40},{40,48},{48,56},{56,64},{64,7... | collective-permute-start | bytes 49160 | tf_op jit(solution)/shard_map/ppermute | solution.py:435
  66.7 13.5 %collective-permute-done.tail = bf16[16,512]{1,0:T(8,128)(2,1)S(1)} collective-permute-done((bf16[16,512]{1,0:T(8,128)(2,1)S(1)}, bf16[16,512]{1,0:T(8,128)(2,1)S(1)}, u32[]{:S(2)}, u32[]{:S(2)}) %collective-permute-start) | collective-permute-done | bytes 16416 | tf_op jit(solution)/shard_map/ppermute | solution.py:435
  80.2 8.2 %all-to-all-done.2.back = bf16[64,11,2,128]{3,2,1,0:T(2,128)(2,1)S(1)} async-done(((bf16[64,11,2,128]{3,2,1,0:T(2,128)(2,1)}), bf16[64,11,2,128]{3,2,1,0:T(2,128)(2,1)S(1)}, u32[]{:S(2)}, u32[]{:S(2)}) %all-to-all-start.2) | async-done | bytes 360480 | tf_op jit(solution)/shard_map/all_to_all | solution.py:448
  88.4 0.0 copy-done
  88.4 0.0 copy-done.1
  88.4 0.0 copy-done.2
  88.4 1.3 %finish.1 = (bf16[128,512]{1,0:T(8,128)(2,1)}, bf16[128,512]{1,0:T(8,128)(2,1)}, bf16[128,512]{1,0:T(8,128)(2,1)}, f32[64,512]{1,0:T(8,128)}, f32[1,64]{1,0:T(1,128)}) custom-call(bf16[64,11,2,128]{3,2,1,0:T(2,128)(2,1)S(1)} %all-to-all-done.2.back, bf16[128,512]{1,0:T(8,128)(2,1)S(1)} %copy-done, bf16[128,512]{1,0:T(8,128)(2,1)S(1)} %copy-done.1, ...), custom_call_target="tpu_custom_call" | custom-call | tf_op jit(solution)/shard_map/finish/pallas_call | solution.py:416
Async XLA Ops:
  2.9 19.0 %copy-start.12 = (f32[64]{0:T(128)S(1)}, f32[64]{0:T(128)}, u32[]{:S(2)}) copy-start(f32[64]{0:T(128)} %param.19) | copy-start | bytes 772
  2.9 19.0 %copy-start.3 = (f32[64,512]{1,0:T(8,128)S(1)}, f32[64,512]{1,0:T(8,128)}, u32[]{:S(2)}) copy-start(f32[64,512]{1,0:T(8,128)} %coef.1) | copy-start | bytes 393220
  2.9 19.0 %copy-start.5 = (f32[128,128]{1,0:T(8,128)S(1)}, f32[128,128]{1,0:T(8,128)}, u32[]{:S(2)}) copy-start(f32[128,128]{1,0:T(8,128)} %constant.22.clone.wave) | copy-start | bytes 196612
  2.9 19.0 %copy-start.6 = (f32[128,128]{1,0:T(8,128)S(1)}, f32[128,128]{1,0:T(8,128)}, u32[]{:S(2)}) copy-start(f32[128,128]{1,0:T(8,128)} %constant.21.clone.imag_b) | copy-start | bytes 196612
  2.9 19.0 %copy-start.7 = (f32[128,128]{1,0:T(8,128)S(1)}, f32[128,128]{1,0:T(8,128)}, u32[]{:S(2)}) copy-start(f32[128,128]{1,0:T(8,128)} %constant.20.clone.real_b) | copy-start | bytes 196612
  2.9 19.0 %copy-start.8 = (f32[128,128]{1,0:T(8,128)S(1)}, f32[128,128]{1,0:T(8,128)}, u32[]{:S(2)}) copy-start(f32[128,128]{1,0:T(8,128)} %constant.19.clone.sin_a) | copy-start | bytes 196612
  2.9 19.0 %copy-start.9 = (f32[128,128]{1,0:T(8,128)S(1)}, f32[128,128]{1,0:T(8,128)}, u32[]{:S(2)}) copy-start(f32[128,128]{1,0:T(8,128)} %constant.18.clone.cos_a) | copy-start | bytes 196612
  3.0 41.1 %all-to-all-start = ((bf16[64,9,2,128]{3,2,1,0:T(2,128)(2,1)}), bf16[64,9,2,128]{3,2,1,0:T(2,128)(2,1)S(1)}, u32[]{:S(2)}, u32[]{:S(2)}) async-start(bf16[64,9,2,128]{3,2,1,0:T(2,128)(2,1)} %get-tuple-element.24), calls=%async_computation | async-start | bytes 589824 | tf_op jit(solution)/shard_map/all_to_all | solution.py:444
  21.8 0.7 copy-start.4
  21.9 0.7 copy-start.10
  56.6 6.7 %copy-start.11 = (bf16[16,512]{1,0:T(8,128)(2,1)S(1)}, bf16[16,512]{1,0:T(8,128)(2,1)}, u32[]{:S(2)}) copy-start(bf16[16,512]{1,0:T(8,128)(2,1)} %get-tuple-element.37) | copy-start | bytes 49156
  56.6 31.8 %copy-start = (bf16[128,512]{1,0:T(8,128)(2,1)S(1)}, bf16[128,512]{1,0:T(8,128)(2,1)}, u32[]{:S(2)}) copy-start(bf16[128,512]{1,0:T(8,128)(2,1)} %x1.1) | copy-start | bytes 393220
  56.6 31.8 %copy-start.1 = (bf16[128,512]{1,0:T(8,128)(2,1)S(1)}, bf16[128,512]{1,0:T(8,128)(2,1)}, u32[]{:S(2)}) copy-start(bf16[128,512]{1,0:T(8,128)(2,1)} %x2.1) | copy-start | bytes 393220
  56.6 31.8 %copy-start.2 = (bf16[128,512]{1,0:T(8,128)(2,1)S(1)}, bf16[128,512]{1,0:T(8,128)(2,1)}, u32[]{:S(2)}) copy-start(bf16[128,512]{1,0:T(8,128)(2,1)} %value.1) | copy-start | bytes 393220
  56.6 31.8 %all-to-all-start.2 = ((bf16[64,11,2,128]{3,2,1,0:T(2,128)(2,1)}), bf16[64,11,2,128]{3,2,1,0:T(2,128)(2,1)S(1)}, u32[]{:S(2)}, u32[]{:S(2)}) async-start(bf16[64,11,2,128]{3,2,1,0:T(2,128)(2,1)} %emit.1), calls=%async_computation.2 | async-start | bytes 720896 | tf_op jit(solution)/shard_map/all_to_all | solution.py:448
  63.3 16.9 %collective-permute-start = (bf16[16,512]{1,0:T(8,128)(2,1)S(1)}, bf16[16,512]{1,0:T(8,128)(2,1)S(1)}, u32[]{:S(2)}, u32[]{:S(2)}) collective-permute-start(bf16[16,512]{1,0:T(8,128)(2,1)S(1)} %copy-done.11), channel_id=1, source_target_pairs={{0,8},{8,16},{16,24},{24,32},{32,40},{40,48},{48,56},{56,64},{64,7... | collective-permute-start | bytes 49160 | tf_op jit(solution)/shard_map/ppermute | solution.py:435

commit v5 on v4

--- a/solution.py
+++ b/solution.py
@@ -131,7 +131,7 @@
     return weight[0:1] * value + weight[1:2] * one + weight[2:3] * two
 
 
-def gate_kernel(x1h, x2h, vh, oh, wh, sent, tail, x1, x2, v, o, w, sems):
+def gate_kernel(x1h, x2h, vh, oh, wh, sent, x1, x2, v, o, w, sems):
     copies = [
         pltpu.make_async_copy(src, dst, sems.at[n])
         for n, (src, dst) in enumerate(((oh, o), (x2h, x2), (vh, v), (wh, w), (x1h, x1)))
@@ -151,7 +151,6 @@
     gated = (first * mix(value, zero, w[...])).T.reshape(shards, OWN, ROWS)
     flat = sent.reshape(shards, WORDS, ROWS)
     flat[:, : 2 * OWN] = jnp.concatenate([gated, grad], axis=1).astype(bf16)
-    tail[...] = v[ROWS - 16 :]
 
     per = LANES // OWN
     lane = lax.broadcasted_iota(jnp.int32, (per, LANES), 1)
@@ -173,12 +172,9 @@
     shards = x1.shape[1] // OWN
     return pl.pallas_call(
         gate_kernel,
-        out_shape=(
-            jax.ShapeDtypeStruct((shards, WORDS // 2, 2, ROWS), bf16),
-            jax.ShapeDtypeStruct((16, x1.shape[1]), bf16),
-        ),
+        out_shape=jax.ShapeDtypeStruct((shards, WORDS // 2, 2, ROWS), bf16),
         in_specs=[pl.BlockSpec(memory_space=pltpu.HBM)] * 5,
-        out_specs=(VMEM, VMEM),
+        out_specs=VMEM,
         scratch_shapes=[pltpu.VMEM(x1.shape, bf16)] * 4
         + [pltpu.VMEM(weight.shape, f32), pltpu.SemaphoreType.DMA((5,))],
         compiler_params=pltpu.CompilerParams(vmem_limit_bytes=(64 << 20) - (64 << 10)),
@@ -218,7 +214,7 @@
     gs[...] = g
     xb = x.astype(bf16)
     xb_out[...] = xb
-    head_out[...] = x1_head
+    head_out[...] = jnp.where(lane3 < ORDER, spread[:, LANES : 2 * LANES], x1_head)
     gb = g.astype(bf16)
     here = lax.broadcasted_iota(jnp.int32, (ROWS, ROWS), 0)
     there = lax.broadcasted_iota(jnp.int32, (ROWS, ROWS), 1)
@@ -341,22 +337,28 @@
     row = lax.broadcasted_iota(jnp.int32, (OWN, LANES), 0)
     both = jnp.where(lane < ORDER, coef[...], pltpu.roll(pltpu.roll(coef[...], ORDER, 1), OWN // 2, 0))
     flat[:, 2 * OWN : 2 * OWN + 4] = jnp.broadcast_to(both[: OWN // 2], (chunks, OWN // 2, LANES)).astype(bf16)
-    heads = (pltpu.roll(yg[...], ORDER, 1) * head[...]).astype(bf16)
-    heads = cube(jnp.dot(heads, head_spots(False), preferred_element_type=f32))
-    heads = jnp.sum(jnp.where((lane - ORDER) // 2 == row, heads, 0.0), axis=1, keepdims=True)
-    heads = jnp.concatenate([heads[1:], jnp.zeros((1, 1, LANES), f32)], axis=0)
+    lane2 = lax.broadcasted_iota(jnp.int32, (rows, LANES), 1)
+    ends = jnp.where(lane2 < ORDER, head[...], pltpu.roll(yg[...], ORDER, 1) * head[...]).astype(bf16)
+    ends = cube(jnp.dot(ends, end_spots(False), preferred_element_type=f32))
+    ends = jnp.sum(jnp.where(lane % ORDER // 2 == row, ends, 0.0), axis=1, keepdims=True)
+    none = jnp.zeros((1, 1, LANES), f32)
     part = jnp.sum(parts[...], axis=0, keepdims=True)
     low = part - part.astype(bf16).astype(f32)
     left = lane[:1] < ORDER
-    high = jnp.where(left, part, heads)
-    low = jnp.broadcast_to(jnp.where(left, low, 0.0), (chunks, 1, LANES))
+    high = jnp.where(left, part, jnp.concatenate([ends[1:], none], axis=0))
+    ends = pltpu.roll(jnp.concatenate([none, ends[:-1]], axis=0), ORDER, 2)
+    low = jnp.where(left, low, ends)
     flat[:, 2 * OWN + 4 :] = jnp.concatenate([high, low], axis=1).astype(bf16)
 
 
-def head_spots(turned):
+def end_spots(turned):
     few = lax.broadcasted_iota(jnp.int32, (LANES, LANES), 1 if turned else 0)
     many = lax.broadcasted_iota(jnp.int32, (LANES, LANES), 0 if turned else 1)
-    hit = (few // 2 == ORDER // 2) & (many >= ORDER) & (many < ORDER + 2 * OWN) & (few % 2 == many % 2)
+    hit = (many % ORDER < 2 * OWN) & (few % 2 == many % 2)
+    if turned:
+        hit &= few // 2 == jnp.where(many < ORDER, ORDER // 2 + 1, ORDER // 2)
+    else:
+        hit &= few // 2 == many // ORDER * (ORDER // 2)
     return hit.astype(bf16)
 
 
@@ -375,7 +377,7 @@
     )(got, parts, *made, mf, me, small)
 
 
-def finish_kernel(peers, back, x1, x2, value, tail, weight, y, gx1, gvalue, gcoef, grate):
+def finish_kernel(peers, back, x1, x2, value, weight, y, gx1, gvalue, gcoef, grate):
     shards = back.shape[0]
     wide = shards * OWN
     every = back.reshape(shards, BACK, ROWS)
@@ -389,15 +391,16 @@
     grate[...] = rates[:, :ORDER] * (LENGTH * wide * peers) ** -0.5
     lane = lax.broadcasted_iota(jnp.int32, (shards, OWN, LANES), 2)
     row = lax.broadcasted_iota(jnp.int32, (shards, OWN, LANES), 1)
-    heads = jnp.where((lane - ORDER) // 2 == row, jnp.broadcast_to(rest[:, :1], lane.shape), 0.0)
-    heads = jnp.dot(heads.reshape(wide, LANES).astype(bf16), head_spots(True), preferred_element_type=f32)
+    ends = jnp.where(lane[:, :1] < ORDER, pltpu.roll(rest[:, 1:], ORDER, 2), rest[:, :1])
+    ends = jnp.where(lane % ORDER // 2 == row, jnp.broadcast_to(ends, lane.shape), 0.0)
+    ends = jnp.dot(ends.reshape(wide, LANES).astype(bf16), end_spots(True), preferred_element_type=f32)
     lane = lax.broadcasted_iota(jnp.int32, (wide, LANES), 1)
-    turned = jnp.where(lane < ORDER, both, heads).T
+    turned = jnp.where(lane < ORDER, both, ends).T
     gcoef[...] = turned[:ORDER]
     first = x1[...].astype(f32)
     w = weight[...]
     y[...] = (x2[...].astype(f32) * conv).astype(bf16)
-    mixed = mix(value[...].astype(f32), tail[...].astype(f32)[14:], w)
+    mixed = mix(value[...].astype(f32), turned[ORDER + 2 : ORDER + 4], w)
     gx1[...] = (grad * mixed).astype(bf16)
     grad_mixed = grad * first
     after = turned[ORDER : ORDER + 2]
@@ -411,7 +414,7 @@
     gvalue[...] = (w[0:1] * grad_mixed + w[1:2] * one + w[2:3] * two).astype(bf16)
 
 
-def finish(back, x1, x2, value, tail, weight, peers):
+def finish(back, x1, x2, value, weight, peers):
     shape = jax.ShapeDtypeStruct(x1.shape, bf16)
     return pl.pallas_call(
         functools.partial(finish_kernel, peers),
@@ -422,31 +425,24 @@
             jax.ShapeDtypeStruct((ORDER, x1.shape[1]), f32),
             jax.ShapeDtypeStruct((1, ORDER), f32),
         ),
-        in_specs=[VMEM] * 6,
+        in_specs=[VMEM] * 5,
         out_specs=tuple([VMEM] * 5),
         compiler_params=pltpu.CompilerParams(vmem_limit_bytes=16 << 20),
         name="finish",
-    )(back, x1, x2, value, tail, weight)
-
-
-def shift(array, by):
-    peers = lax.axis_size("seq")
-    pairs = [(i, i + by) for i in range(peers) if 0 <= i + by < peers]
-    return lax.ppermute(array, "seq", pairs)
+    )(back, x1, x2, value, weight)
 
 
 def per_device(x1, x2, value, out_grad, short_weight, coef, rate):
     peers = lax.axis_size("chan")
     place = lax.axis_index("seq").astype(jnp.int32)[None]
     tables = make_tables(place, rate, coef, short_weight)
-    sent, tail = gate(x1, x2, value, out_grad, short_weight)
-    tail = shift(tail, 1)
+    sent = gate(x1, x2, value, out_grad, short_weight)
     got = lax.all_to_all(sent, "seq", split_axis=0, concat_axis=0, tiled=True)
     part, *made = owner(place, got, tables, peers)
     parts = lax.all_to_all(part, "chan", split_axis=0, concat_axis=0, tiled=True)
     done = emit(got, parts, made, tables)
     back = lax.all_to_all(done, "seq", split_axis=0, concat_axis=0, tiled=True)
-    y, gx1, gvalue, gcoef, grate = finish(back, x1, x2, value, tail, short_weight, peers)
+    y, gx1, gvalue, gcoef, grate = finish(back, x1, x2, value, short_weight, peers)
     return (y, gx1, gvalue, gcoef, grate.reshape(ORDER))
 
 

time: 90 us -> 88.9 us (0.988)
  blocking collectives: 9.38 us -> 40.7 us
  waiting for transfers between devices: 42 us -> 20.4 us
  starting transfers between devices: 28.9 us -> 18.9 us
    all_to_all x0 -> x1, blocking collectives: none -> 31.4 us  [per_device(): back = lax.all_to_all(done, 'seq', split_axis=0, concat_axis=0, tiled=True)]
    ppermute x1 -> x0, waiting for transfers between devices: 13.5 us -> none  [shift(): return lax.ppermute(array, 'seq', pairs)]
    all_to_all x1 -> x0, waiting for transfers between devices: 8.18 us -> none  [per_device(): back = lax.all_to_all(done, 'seq', split_axis=0, concat_axis=0, tiled=True)]
    all_to_all x1 -> x0, starting transfers between devices: 6.71 us -> none  [per_device(): back = lax.all_to_all(done, 'seq', split_axis=0, concat_axis=0, tiled=True)]
    ppermute x1 -> x0, starting transfers between devices: 3.38 us -> none  [shift(): return lax.ppermute(array, 'seq', pairs)]
  transfers between devices with their start and end apart: 3 -> 1, of which waited for: 3 -> 1; matrix products, arithmetic and copies ran while one was open for 0% -> 0% of each run, Pallas kernels for 1% -> 1%
where the time goes in v5:
time: 88.9 us; the launch traced here: 88.6 us
  blocking collectives  40.7 us (46%)
  waiting for transfers between devices  20.4 us (23%)
  starting transfers between devices  18.9 us (21%)
  Pallas kernels  7.08 us (8%)
    all_to_all x1, blocking collectives, per_device(): back = lax.all_to_all(done, 'seq', split_axis=0, concat_axis=0, tiled=True)  31.4 us
    all_to_all x1, waiting for transfers between devices, per_device(): got = lax.all_to_all(sent, 'seq', split_axis=0, concat_axis=0, tiled=True)  20.4 us
    all_to_all x1, starting transfers between devices, per_device(): got = lax.all_to_all(sent, 'seq', split_axis=0, concat_axis=0, tiled=True)  18.9 us
    all_to_all x1, blocking collectives, per_device(): lax.all_to_all(part, 'chan', split_axis=0, concat_axis=0, tiled=True)  9.38 us
    pallas_call x1, Pallas kernels, gate(): pl.pallas_call(gate_kernel, out_shape=jax.ShapeDtypeStruct((shards, WORDS...  2.23 us
  transfers between devices with their start and end apart: 1, of which 1 were waited for; matrix products, arithmetic and copies ran while one was open for 0% of the time, Pallas kernels for 1%

profile of v5, /device:TPU:24, one launch (start us, length us, event | category | flops | bytes accessed | tf_op | source)
XLA Modules:
  0.0 88.6 jit_solution(695024381534203948)
XLA Ops:
  0.6 2.2 %gate.1 = bf16[64,9,2,128]{3,2,1,0:T(2,128)(2,1)} custom-call(bf16[128,512]{1,0:T(8,128)(2,1)} %x1.1, bf16[128,512]{1,0:T(8,128)(2,1)} %x2.1, bf16[128,512]{1,0:T(8,128)(2,1)} %value.1, bf16[128,512]{1,0:T(8,128)(2,1)} %oh.1, f32[3,512]{1,0:T(4,128)} %weight.3), custom_call_target="tpu_custom_call" | custom-call | tf_op jit(solution)/shard_map/gate/pallas_call | solution.py:173
  2.9 0.0 copy-start.11
  2.9 0.0 copy-start.3
  2.9 0.0 copy-start.5
  2.9 0.0 copy-start.6
  2.9 0.0 copy-start.7
  2.9 0.0 copy-start.8
  2.9 0.0 copy-start.9
  3.0 18.9 %all-to-all-start = ((bf16[64,9,2,128]{3,2,1,0:T(2,128)(2,1)}), bf16[64,9,2,128]{3,2,1,0:T(2,128)(2,1)S(1)}, u32[]{:S(2)}, u32[]{:S(2)}) async-start(bf16[64,9,2,128]{3,2,1,0:T(2,128)(2,1)} %gate.1), calls=%async_computation | async-start | bytes 589824 | tf_op jit(solution)/shard_map/all_to_all | solution.py:440
  21.8 0.0 copy-start.4
  21.8 0.0 copy-done.11
  21.8 0.1 maximum_bitcast_fusion.rate
  21.9 0.0 copy-start.10
  21.9 0.0 copy-done.3
  21.9 0.0 copy-done.5
  21.9 0.0 copy-done.6
  21.9 0.0 copy-done.7
  21.9 0.0 copy-done.8
  21.9 0.0 copy-done.9
  22.0 0.6 copy-done.4
  22.5 0.1 copy-done.10
  22.6 1.1 %tables.1 = (bf16[256,512]{1,0:T(8,128)(2,1)S(1)}, bf16[256,512]{1,0:T(8,128)(2,1)S(1)}, bf16[128,128]{1,0:T(8,128)(2,1)S(1)}, bf16[128,128]{1,0:T(8,128)(2,1)S(...) custom-call(s32[1]{0:T(128)} %bitcast.place, f32[1,128]{1,0:T(1,128)S(1)} %maximum_bitcast_fusion.rate, ...), custom_call_target="tpu_custom_call" | custom-call | flops 4000000 | bytes 1000000 | tf_op jit(solution)/shard_map/tables/pallas_call | solution.py:109
  23.7 20.4 %all-to-all-done.got = bf16[64,9,2,128]{3,2,1,0:T(2,128)(2,1)S(1)} async-done(((bf16[64,9,2,128]{3,2,1,0:T(2,128)(2,1)}), bf16[64,9,2,128]{3,2,1,0:T(2,128)(2,1)S(1)}, u32[]{:S(2)}, u32[]{:S(2)}) %all-to-all-start) | async-done | bytes 294944 | tf_op jit(solution)/shard_map/all_to_all | solution.py:440
  44.1 1.4 %owner.1 = (f32[8,128]{1,0:T(8,128)S(1)}, f32[8,128]{1,0:T(8,128)S(1)}, bf16[512,128]{1,0:T(8,128)(2,1)S(1)}, bf16[512,128]{1,0:T(8,128)(2,1)S(1)}, bf16[512,128...) custom-call(s32[1]{0:T(128)} %bitcast.place, bf16[64,9,2,128]{3,2,1,0:T(2,128)(2,1)S(1)} %all-to-all-done.got, ...), custom_call_target="tpu_custom_call" | custom-call | tf_op jit(solution)/shard_map/owner/pallas_call | solution.py:290
  45.5 9.4 %all_to_all.21 = f32[8,1,128]{2,1,0:T(1,128)S(1)} all-to-all(f32[8,1,128]{2,1,0:T(1,128)S(1)} %bitcast.9), channel_id=1, replica_groups=mesh['seq'=64,'chan'=8] {'chan'}, dimensions={0} | all-to-all | bytes 8192 | tf_op jit(solution)/shard_map/all_to_all | solution.py:442
  54.9 1.0 %emit.1 = bf16[64,11,2,128]{3,2,1,0:T(2,128)(2,1)S(1)} custom-call(bf16[64,9,2,128]{3,2,1,0:T(2,128)(2,1)S(1)} %all-to-all-done.got, f32[8,128]{1,0:T(8,128)S(1)} %bitcast.8, f32[8,128]{1,0:T(8,128)S(1)} %get-tuple-element.27.coef, bf16[512,128]{1,0:T(8,128)(2,1)S(1)} %get-tuple-element.28.us, bf16[512,128]{1,0:T(8,128)(2,1)S(1)} %get-tuple-element.29.ug, ...), custom_call_target="tpu_custom_call" | custom-call | tf_op jit(solution)/shard_map/emit/pallas_call | solution.py:369
  55.9 0.0 copy-start
  55.9 0.0 copy-start.1
  55.9 0.0 copy-start.2
  55.9 31.4 %all_to_all.22.back = bf16[64,11,2,128]{3,2,1,0:T(2,128)(2,1)S(1)} all-to-all(bf16[64,11,2,128]{3,2,1,0:T(2,128)(2,1)S(1)} %emit.1), channel_id=1, replica_groups=mesh['seq'=64,'chan'=8] {'seq'}, dimensions={0} | all-to-all | bytes 720896 | tf_op jit(solution)/shard_map/all_to_all | solution.py:444
  87.3 0.0 copy-done
  87.3 0.0 copy-done.1
  87.3 0.0 copy-done.2
  87.3 1.3 %finish.1 = (bf16[128,512]{1,0:T(8,128)(2,1)}, bf16[128,512]{1,0:T(8,128)(2,1)}, bf16[128,512]{1,0:T(8,128)(2,1)}, f32[64,512]{1,0:T(8,128)}, f32[1,64]{1,0:T(1,128)}) custom-call(bf16[64,11,2,128]{3,2,1,0:T(2,128)(2,1)S(1)} %all_to_all.22.back, bf16[128,512]{1,0:T(8,128)(2,1)S(1)} %copy-done, bf16[128,512]{1,0:T(8,128)(2,1)S(1)} %copy-done.1, ...), custom_call_target="tpu_custom_call" | custom-call | tf_op jit(solution)/shard_map/finish/pallas_call | solution.py:419
Async XLA Ops:
  2.9 19.0 %copy-start.11 = (f32[64]{0:T(128)S(1)}, f32[64]{0:T(128)}, u32[]{:S(2)}) copy-start(f32[64]{0:T(128)} %param.19) | copy-start | bytes 772
  2.9 19.0 %copy-start.3 = (f32[64,512]{1,0:T(8,128)S(1)}, f32[64,512]{1,0:T(8,128)}, u32[]{:S(2)}) copy-start(f32[64,512]{1,0:T(8,128)} %coef.1) | copy-start | bytes 393220
  2.9 19.0 %copy-start.5 = (f32[128,128]{1,0:T(8,128)S(1)}, f32[128,128]{1,0:T(8,128)}, u32[]{:S(2)}) copy-start(f32[128,128]{1,0:T(8,128)} %constant.22.clone.wave) | copy-start | bytes 196612
  2.9 19.0 %copy-start.6 = (f32[128,128]{1,0:T(8,128)S(1)}, f32[128,128]{1,0:T(8,128)}, u32[]{:S(2)}) copy-start(f32[128,128]{1,0:T(8,128)} %constant.21.clone.imag_b) | copy-start | bytes 196612
  2.9 19.0 %copy-start.7 = (f32[128,128]{1,0:T(8,128)S(1)}, f32[128,128]{1,0:T(8,128)}, u32[]{:S(2)}) copy-start(f32[128,128]{1,0:T(8,128)} %constant.20.clone.real_b) | copy-start | bytes 196612
  2.9 19.0 %copy-start.8 = (f32[128,128]{1,0:T(8,128)S(1)}, f32[128,128]{1,0:T(8,128)}, u32[]{:S(2)}) copy-start(f32[128,128]{1,0:T(8,128)} %constant.19.clone.sin_a) | copy-start | bytes 196612
  2.9 19.0 %copy-start.9 = (f32[128,128]{1,0:T(8,128)S(1)}, f32[128,128]{1,0:T(8,128)}, u32[]{:S(2)}) copy-start(f32[128,128]{1,0:T(8,128)} %constant.18.clone.cos_a) | copy-start | bytes 196612
  3.0 41.1 %all-to-all-start = ((bf16[64,9,2,128]{3,2,1,0:T(2,128)(2,1)}), bf16[64,9,2,128]{3,2,1,0:T(2,128)(2,1)S(1)}, u32[]{:S(2)}, u32[]{:S(2)}) async-start(bf16[64,9,2,128]{3,2,1,0:T(2,128)(2,1)} %gate.1), calls=%async_computation | async-start | bytes 589824 | tf_op jit(solution)/shard_map/all_to_all | solution.py:440
  21.8 0.7 copy-start.4
  21.9 0.7 copy-start.10
  55.9 31.4 %copy-start = (bf16[128,512]{1,0:T(8,128)(2,1)S(1)}, bf16[128,512]{1,0:T(8,128)(2,1)}, u32[]{:S(2)}) copy-start(bf16[128,512]{1,0:T(8,128)(2,1)} %x1.1) | copy-start | bytes 393220
  55.9 31.4 %copy-start.1 = (bf16[128,512]{1,0:T(8,128)(2,1)S(1)}, bf16[128,512]{1,0:T(8,128)(2,1)}, u32[]{:S(2)}) copy-start(bf16[128,512]{1,0:T(8,128)(2,1)} %x2.1) | copy-start | bytes 393220
  55.9 31.4 %copy-start.2 = (bf16[128,512]{1,0:T(8,128)(2,1)S(1)}, bf16[128,512]{1,0:T(8,128)(2,1)}, u32[]{:S(2)}) copy-start(bf16[128,512]{1,0:T(8,128)(2,1)} %value.1) | copy-start | bytes 393220

commit v6 on v5

--- a/solution.py
+++ b/solution.py
@@ -1,4 +1,3 @@
-import functools
 import math
 
 import jax
@@ -282,31 +281,6 @@
     part_out[...] = jnp.broadcast_to(part + pltpu.roll(part, ORDER, 1), part_out.shape)
 
 
-def owner(place, got, tables, peers):
-    chunks = got.shape[0]
-    rows = chunks * OWN
-    tx, tg, mf, me, wd, small = tables
-    flat = jax.ShapeDtypeStruct((rows, LANES), bf16)
-    return pl.pallas_call(
-        owner_kernel,
-        out_shape=(
-            jax.ShapeDtypeStruct((peers, LANES), f32),
-            jax.ShapeDtypeStruct((OWN, LANES), f32),
-            flat,
-            flat,
-            flat,
-            jax.ShapeDtypeStruct((rows, LANES), f32),
-        ),
-        in_specs=[SMEM] + [VMEM] * 5,
-        out_specs=tuple([VMEM] * 6),
-        scratch_shapes=[pltpu.VMEM((rows, LANES), f32)] * 2
-        + [pltpu.VMEM((rows, 4 * LANES), f32)] * 2
-        + [pltpu.VMEM((rows, LANES), f32)] * 4,
-        compiler_params=pltpu.CompilerParams(vmem_limit_bytes=24 << 20),
-        name="owner",
-    )(place, got, tx, tg, wd, small)
-
-
 def emit_kernel(got, parts, coef, us, ug, xb, head, mf, me, small, out, xs, gs, yc, yg):
     chunks = got.shape[0]
     rows = chunks * OWN
@@ -362,22 +336,52 @@
     return hit.astype(bf16)
 
 
-def emit(got, parts, made, tables):
+def owner_emit_kernel(
+    place, got, tx, tg, mf, me, wd, small, out, part, coef, us, ug, xb, head, gs, rs, ex, eg, sr, si, gr, gi, xs, yc, yg
+):
+    owner_kernel(place, got, tx, tg, wd, small, part, coef, us, ug, xb, head, gs, rs, ex, eg, sr, si, gr, gi)
+    emit_kernel(got, part, coef, us, ug, xb, head, mf, me, small, out, xs, gs, yc, yg)
+
+
+def owner_emit(place, got, tables):
     chunks = got.shape[0]
     rows = chunks * OWN
-    tx, tg, mf, me, wd, small = tables
+    wide = pltpu.VMEM((rows, LANES), f32)
+    flat = pltpu.VMEM((rows, LANES), bf16)
+    tall = pltpu.VMEM((rows, 4 * LANES), f32)
     return pl.pallas_call(
-        emit_kernel,
+        owner_emit_kernel,
         out_shape=jax.ShapeDtypeStruct((chunks, BACK // 2, 2, ROWS), bf16),
-        in_specs=[VMEM] * 10,
+        in_specs=[SMEM] + [VMEM] * 7,
         out_specs=VMEM,
-        scratch_shapes=[pltpu.VMEM((rows, LANES), f32)] * 4,
+        scratch_shapes=[pltpu.VMEM((1, LANES), f32), pltpu.VMEM((OWN, LANES), f32)]
+        + [flat] * 3
+        + [wide] * 3
+        + [tall] * 2
+        + [wide] * 7,
         compiler_params=pltpu.CompilerParams(vmem_limit_bytes=24 << 20),
-        name="emit",
-    )(got, parts, *made, mf, me, small)
-
-
-def finish_kernel(peers, back, x1, x2, value, weight, y, gx1, gvalue, gcoef, grate):
+        name="owner",
+    )(place, got, *tables)
+
+
+def rate_kernel(back, parts):
+    flat = back.reshape(back.shape[0], BACK, ROWS)
+    rates = jnp.sum(jnp.sum(flat[:, 2 * OWN + 4 :].astype(f32), axis=0), axis=0, keepdims=True)
+    parts[...] = jnp.broadcast_to(rates, parts.shape)
+
+
+def rate_parts(back, peers):
+    return pl.pallas_call(
+        rate_kernel,
+        out_shape=jax.ShapeDtypeStruct((peers, LANES), f32),
+        in_specs=[VMEM],
+        out_specs=VMEM,
+        compiler_params=pltpu.CompilerParams(vmem_limit_bytes=8 << 20),
+        name="rates",
+    )(back)
+
+
+def finish_kernel(back, x1, x2, value, weight, y, gx1, gvalue, gcoef):
     shards = back.shape[0]
     wide = shards * OWN
     every = back.reshape(shards, BACK, ROWS)
@@ -387,8 +391,6 @@
     both = every[:, 2 * OWN : 2 * OWN + 4].astype(f32)
     both = jnp.concatenate([both, pltpu.roll(both, ORDER, 2)], axis=1).reshape(wide, LANES)
     rest = every[:, 2 * OWN + 4 :].astype(f32)
-    rates = jnp.sum(jnp.sum(rest, axis=0), axis=0, keepdims=True)
-    grate[...] = rates[:, :ORDER] * (LENGTH * wide * peers) ** -0.5
     lane = lax.broadcasted_iota(jnp.int32, (shards, OWN, LANES), 2)
     row = lax.broadcasted_iota(jnp.int32, (shards, OWN, LANES), 1)
     ends = jnp.where(lane[:, :1] < ORDER, pltpu.roll(rest[:, 1:], ORDER, 2), rest[:, :1])
@@ -414,20 +416,20 @@
     gvalue[...] = (w[0:1] * grad_mixed + w[1:2] * one + w[2:3] * two).astype(bf16)
 
 
-def finish(back, x1, x2, value, weight, peers):
+def finish(back, x1, x2, value, weight):
     shape = jax.ShapeDtypeStruct(x1.shape, bf16)
     return pl.pallas_call(
-        functools.partial(finish_kernel, peers),
+        finish_kernel,
         out_shape=(
             shape,
             shape,
             shape,
             jax.ShapeDtypeStruct((ORDER, x1.shape[1]), f32),
-            jax.ShapeDtypeStruct((1, ORDER), f32),
         ),
         in_specs=[VMEM] * 5,
-        out_specs=tuple([VMEM] * 5),
+        out_specs=tuple([VMEM] * 4),
         compiler_params=pltpu.CompilerParams(vmem_limit_bytes=16 << 20),
+        cost_estimate=pl.CostEstimate(flops=4_000_000, bytes_accessed=4_000_000, transcendentals=0),
         name="finish",
     )(back, x1, x2, value, weight)
 
@@ -438,12 +440,13 @@
     tables = make_tables(place, rate, coef, short_weight)
     sent = gate(x1, x2, value, out_grad, short_weight)
     got = lax.all_to_all(sent, "seq", split_axis=0, concat_axis=0, tiled=True)
-    part, *made = owner(place, got, tables, peers)
-    parts = lax.all_to_all(part, "chan", split_axis=0, concat_axis=0, tiled=True)
-    done = emit(got, parts, made, tables)
+    done = owner_emit(place, got, tables)
     back = lax.all_to_all(done, "seq", split_axis=0, concat_axis=0, tiled=True)
-    y, gx1, gvalue, gcoef, grate = finish(back, x1, x2, value, short_weight, peers)
-    return (y, gx1, gvalue, gcoef, grate.reshape(ORDER))
+    parts = rate_parts(back, peers)
+    parts = lax.all_to_all(parts, "chan", split_axis=0, concat_axis=0, tiled=True)
+    y, gx1, gvalue, gcoef = finish(back, x1, x2, value, short_weight)
+    grate = jnp.sum(parts[:, :ORDER], axis=0) * (LENGTH * x1.shape[1] * peers) ** -0.5
+    return (y, gx1, gvalue, gcoef, grate)
 
 
 def solution(mesh):

time: 88.9 us -> 89.1 us (level); the launches traced: 88.6 us -> 87.8 us
  blocking collectives: 40.7 us -> 30.7 us
  starting transfers between devices: 18.9 us -> 23.2 us
  waiting for transfers between devices: 20.4 us -> 24.3 us
    all_to_all x1 -> x0, blocking collectives: 9.38 us -> none  [per_device(): lax.all_to_all(part, 'chan', split_axis=0, concat_axis=0, tiled=True)]
    all_to_all x0 -> x1, starting transfers between devices: none -> 4.3 us  [per_device(): lax.all_to_all(parts, 'chan', split_axis=0, concat_axis=0, tiled=True)]
    all_to_all x0 -> x1, waiting for transfers between devices: none -> 3.93 us  [per_device(): lax.all_to_all(parts, 'chan', split_axis=0, concat_axis=0, tiled=True)]
  transfers between devices with their start and end apart: 1 -> 2, of which waited for: 1 -> 2; matrix products, arithmetic and copies ran while one was open for 0% -> 0% of each run, Pallas kernels for 1% -> 3%
where the time goes in v6:
time: 89.1 us; the launch traced here: 87.8 us
  blocking collectives  30.7 us (34%)
  waiting for transfers between devices  24.3 us (27%)
  starting transfers between devices  23.2 us (26%)
  Pallas kernels  7.58 us (9%)
    all_to_all x1, blocking collectives, per_device(): back = lax.all_to_all(done, 'seq', split_axis=0, concat_axis=0, tiled=True)  30.7 us
    all_to_all x1, waiting for transfers between devices, per_device(): got = lax.all_to_all(sent, 'seq', split_axis=0, concat_axis=0, tiled=True)  20.4 us
    all_to_all x1, starting transfers between devices, per_device(): got = lax.all_to_all(sent, 'seq', split_axis=0, concat_axis=0, tiled=True)  18.9 us
    all_to_all x1, starting transfers between devices, per_device(): lax.all_to_all(parts, 'chan', split_axis=0, concat_axis=0, tiled=True)  4.3 us
    all_to_all x1, waiting for transfers between devices, per_device(): lax.all_to_all(parts, 'chan', split_axis=0, concat_axis=0, tiled=True)  3.93 us
    pallas_call x1, Pallas kernels, owner_emit(): pl.pallas_call(owner_emit_kernel, out_shape=jax.ShapeDtypeStruct((chunks,...  2.29 us
    pallas_call x1, Pallas kernels, gate(): pl.pallas_call(gate_kernel, out_shape=jax.ShapeDtypeStruct((shards, WORDS...  2.22 us
  transfers between devices with their start and end apart: 2, of which 2 were waited for; matrix products, arithmetic and copies ran while one was open for 0% of the time, Pallas kernels for 3%

profile of v6, /device:TPU:24, one launch (start us, length us, event | category | flops | bytes accessed | tf_op | source)
XLA Modules:
  0.0 87.8 jit_solution(17354458167494053538)
XLA Ops:
  0.6 2.2 %gate.1 = bf16[64,9,2,128]{3,2,1,0:T(2,128)(2,1)} custom-call(bf16[128,512]{1,0:T(8,128)(2,1)} %x1.1, bf16[128,512]{1,0:T(8,128)(2,1)} %x2.1, bf16[128,512]{1,0:T(8,128)(2,1)} %value.1, bf16[128,512]{1,0:T(8,128)(2,1)} %oh.1, f32[3,512]{1,0:T(4,128)} %weight.3), custom_call_target="tpu_custom_call" | custom-call | tf_op jit(solution)/shard_map/gate/pallas_call | solution.py:172
  2.9 0.0 copy-start.11
  2.9 0.0 copy-start.3
  2.9 0.0 copy-start.5
  2.9 0.0 copy-start.6
  2.9 0.0 copy-start.7
  2.9 0.0 copy-start.8
  2.9 0.0 copy-start.9
  2.9 18.9 %all-to-all-start = ((bf16[64,9,2,128]{3,2,1,0:T(2,128)(2,1)}), bf16[64,9,2,128]{3,2,1,0:T(2,128)(2,1)S(1)}, u32[]{:S(2)}, u32[]{:S(2)}) async-start(bf16[64,9,2,128]{3,2,1,0:T(2,128)(2,1)} %gate.1), calls=%async_computation | async-start | bytes 589824 | tf_op jit(solution)/shard_map/all_to_all | solution.py:442
  21.8 0.0 copy-start.4
  21.8 0.0 copy-done.11
  21.8 0.1 maximum_bitcast_fusion.rate
  21.9 0.0 copy-start.10
  21.9 0.0 copy-done.3
  21.9 0.0 copy-done.5
  21.9 0.0 copy-done.6
  21.9 0.0 copy-done.7
  21.9 0.0 copy-done.8
  21.9 0.0 copy-done.9
  21.9 0.6 copy-done.4
  22.5 0.1 copy-done.10
  22.6 1.1 %tables.1 = (bf16[256,512]{1,0:T(8,128)(2,1)S(1)}, bf16[256,512]{1,0:T(8,128)(2,1)S(1)}, bf16[128,128]{1,0:T(8,128)(2,1)S(1)}, bf16[128,128]{1,0:T(8,128)(2,1)S(...) custom-call(s32[1]{0:T(128)} %bitcast.place, f32[1,128]{1,0:T(1,128)S(1)} %maximum_bitcast_fusion.rate, ...), custom_call_target="tpu_custom_call" | custom-call | flops 4000000 | bytes 1000000 | tf_op jit(solution)/shard_map/tables/pallas_call | solution.py:108
  23.7 20.4 %all-to-all-done.got = bf16[64,9,2,128]{3,2,1,0:T(2,128)(2,1)S(1)} async-done(((bf16[64,9,2,128]{3,2,1,0:T(2,128)(2,1)}), bf16[64,9,2,128]{3,2,1,0:T(2,128)(2,1)S(1)}, u32[]{:S(2)}, u32[]{:S(2)}) %all-to-all-start) | async-done | bytes 294944 | tf_op jit(solution)/shard_map/all_to_all | solution.py:442
  44.0 2.3 %owner.1 = bf16[64,11,2,128]{3,2,1,0:T(2,128)(2,1)S(1)} custom-call(s32[1]{0:T(128)} %bitcast.place, bf16[64,9,2,128]{3,2,1,0:T(2,128)(2,1)S(1)} %all-to-all-done.got, bf16[256,512]{1,0:T(8,128)(2,1)S(1)} %get-tuple-element.15.tx, bf16[256,512]{1,0:T(8,128)(2,1)S(1)} %get-tuple-element.16.tg, bf16[128,128]{1,0:T(8,128)(2,1)S(1)} %get-tuple-element.17.mf, ...), custom_call_target="tpu_custom_call" | custom-call | tf_op jit(solution)/shard_map/owner/pallas_call | solution.py:352
  46.3 0.0 copy-start.2
  46.4 30.7 %all_to_all.22.back = bf16[64,11,2,128]{3,2,1,0:T(2,128)(2,1)S(1)} all-to-all(bf16[64,11,2,128]{3,2,1,0:T(2,128)(2,1)S(1)} %owner.1), channel_id=1, replica_groups=mesh['seq'=64,'chan'=8] {'seq'}, dimensions={0} | all-to-all | bytes 720896 | tf_op jit(solution)/shard_map/all_to_all | solution.py:444
  77.1 0.0 copy-start
  77.1 0.0 copy-start.1
  77.1 0.7 rates.1
  77.7 4.3 %all-to-all-start.2 = ((f32[8,1,128]{2,1,0:T(1,128)}), f32[8,1,128]{2,1,0:T(1,128)S(1)}, u32[]{:S(2)}, u32[]{:S(2)}) async-start(f32[8,1,128]{2,1,0:T(1,128)} %bitcast.3), calls=%async_computation.2 | async-start | bytes 8192 | tf_op jit(solution)/shard_map/all_to_all | solution.py:446
  82.0 0.0 copy-done.2
  82.0 0.0 copy-done
  82.0 0.0 copy-done.1
  82.1 1.3 %finish.1 = (bf16[128,512]{1,0:T(8,128)(2,1)}, bf16[128,512]{1,0:T(8,128)(2,1)}, bf16[128,512]{1,0:T(8,128)(2,1)}, f32[64,512]{1,0:T(8,128)}) custom-call(bf16[64,11,2,128]{3,2,1,0:T(2,128)(2,1)S(1)} %all_to_all.22.back, bf16[128,512]{1,0:T(8,128)(2,1)S(1)} %copy-done, bf16[128,512]{1,0:T(8,128)(2,1)S(1)} %copy-done.1, bf16[128,512]{1,0:T(8,128)(2,1)S(1)} %copy-done.2, ...), custom_call_target="tpu_custom_call" | custom-call | flops 4000000 | bytes 4000000 | tf_op jit(solution)/shard_map/finish/pallas_call | solution.py:421
  83.4 3.9 %all-to-all-done.2 = f32[8,1,128]{2,1,0:T(1,128)S(1)} async-done(((f32[8,1,128]{2,1,0:T(1,128)}), f32[8,1,128]{2,1,0:T(1,128)S(1)}, u32[]{:S(2)}, u32[]{:S(2)}) %all-to-all-start.2) | async-done | bytes 4128 | tf_op jit(solution)/shard_map/all_to_all | solution.py:446
  87.3 0.5 broadcast_multiply_fusion
  (1 shorter events, 0.0 us)
Async XLA Ops:
  2.9 19.0 %copy-start.11 = (f32[64]{0:T(128)S(1)}, f32[64]{0:T(128)}, u32[]{:S(2)}) copy-start(f32[64]{0:T(128)} %param.19) | copy-start | bytes 772
  2.9 19.0 %copy-start.3 = (f32[64,512]{1,0:T(8,128)S(1)}, f32[64,512]{1,0:T(8,128)}, u32[]{:S(2)}) copy-start(f32[64,512]{1,0:T(8,128)} %coef.1) | copy-start | bytes 393220
  2.9 19.0 %copy-start.5 = (f32[128,128]{1,0:T(8,128)S(1)}, f32[128,128]{1,0:T(8,128)}, u32[]{:S(2)}) copy-start(f32[128,128]{1,0:T(8,128)} %constant.26.clone.wave) | copy-start | bytes 196612
  2.9 19.0 %copy-start.6 = (f32[128,128]{1,0:T(8,128)S(1)}, f32[128,128]{1,0:T(8,128)}, u32[]{:S(2)}) copy-start(f32[128,128]{1,0:T(8,128)} %constant.25.clone.imag_b) | copy-start | bytes 196612
  2.9 19.0 %copy-start.7 = (f32[128,128]{1,0:T(8,128)S(1)}, f32[128,128]{1,0:T(8,128)}, u32[]{:S(2)}) copy-start(f32[128,128]{1,0:T(8,128)} %constant.24.clone.real_b) | copy-start | bytes 196612
  2.9 19.0 %copy-start.8 = (f32[128,128]{1,0:T(8,128)S(1)}, f32[128,128]{1,0:T(8,128)}, u32[]{:S(2)}) copy-start(f32[128,128]{1,0:T(8,128)} %constant.23.clone.sin_a) | copy-start | bytes 196612
  2.9 19.0 %copy-start.9 = (f32[128,128]{1,0:T(8,128)S(1)}, f32[128,128]{1,0:T(8,128)}, u32[]{:S(2)}) copy-start(f32[128,128]{1,0:T(8,128)} %constant.22.clone.cos_a) | copy-start | bytes 196612
  2.9 41.1 %all-to-all-start = ((bf16[64,9,2,128]{3,2,1,0:T(2,128)(2,1)}), bf16[64,9,2,128]{3,2,1,0:T(2,128)(2,1)S(1)}, u32[]{:S(2)}, u32[]{:S(2)}) async-start(bf16[64,9,2,128]{3,2,1,0:T(2,128)(2,1)} %gate.1), calls=%async_computation | async-start | bytes 589824 | tf_op jit(solution)/shard_map/all_to_all | solution.py:442
  21.8 0.7 copy-start.4
  21.9 0.7 copy-start.10
  46.3 35.7 %copy-start.2 = (bf16[128,512]{1,0:T(8,128)(2,1)S(1)}, bf16[128,512]{1,0:T(8,128)(2,1)}, u32[]{:S(2)}) copy-start(bf16[128,512]{1,0:T(8,128)(2,1)} %value.1) | copy-start | bytes 393220
  77.1 5.0 %copy-start = (bf16[128,512]{1,0:T(8,128)(2,1)S(1)}, bf16[128,512]{1,0:T(8,128)(2,1)}, u32[]{:S(2)}) copy-start(bf16[128,512]{1,0:T(8,128)(2,1)} %x1.1) | copy-start | bytes 393220
  77.1 5.0 %copy-start.1 = (bf16[128,512]{1,0:T(8,128)(2,1)S(1)}, bf16[128,512]{1,0:T(8,128)(2,1)}, u32[]{:S(2)}) copy-start(bf16[128,512]{1,0:T(8,128)(2,1)} %x2.1) | copy-start | bytes 393220
  77.7 9.6 %all-to-all-start.2 = ((f32[8,1,128]{2,1,0:T(1,128)}), f32[8,1,128]{2,1,0:T(1,128)S(1)}, u32[]{:S(2)}, u32[]{:S(2)}) async-start(f32[8,1,128]{2,1,0:T(1,128)} %bitcast.3), calls=%async_computation.2 | async-start | bytes 8192 | tf_op jit(solution)/shard_map/all_to_all | solution.py:446

commit v7 on v6

--- a/solution.py
+++ b/solution.py
@@ -367,7 +367,8 @@
 def rate_kernel(back, parts):
     flat = back.reshape(back.shape[0], BACK, ROWS)
     rates = jnp.sum(jnp.sum(flat[:, 2 * OWN + 4 :].astype(f32), axis=0), axis=0, keepdims=True)
-    parts[...] = jnp.broadcast_to(rates, parts.shape)
+    scale = (LENGTH * back.shape[0] * OWN * parts.shape[0]) ** -0.5
+    parts[...] = jnp.broadcast_to(rates * scale, parts.shape)
 
 
 def rate_parts(back, peers):
@@ -445,7 +446,7 @@
     parts = rate_parts(back, peers)
     parts = lax.all_to_all(parts, "chan", split_axis=0, concat_axis=0, tiled=True)
     y, gx1, gvalue, gcoef = finish(back, x1, x2, value, short_weight)
-    grate = jnp.sum(parts[:, :ORDER], axis=0) * (LENGTH * x1.shape[1] * peers) ** -0.5
+    grate = jnp.sum(parts[:, :ORDER], axis=0)
     return (y, gx1, gvalue, gcoef, grate)
 
 

time: 89.1 us -> 89.1 us (level)
  no operation moved by 1% of the time
where the time goes in v7:
time: 89.1 us; the launch traced here: 87.8 us
  blocking collectives  30.7 us (34%)
  waiting for transfers between devices  24.3 us (27%)
  starting transfers between devices  23.2 us (26%)
  Pallas kernels  7.58 us (9%)
    all_to_all x1, blocking collectives, per_device(): back = lax.all_to_all(done, 'seq', split_axis=0, concat_axis=0, tiled=True)  30.7 us
    all_to_all x1, waiting for transfers between devices, per_device(): got = lax.all_to_all(sent, 'seq', split_axis=0, concat_axis=0, tiled=True)  20.4 us
    all_to_all x1, starting transfers between devices, per_device(): got = lax.all_to_all(sent, 'seq', split_axis=0, concat_axis=0, tiled=True)  18.9 us
    all_to_all x1, starting transfers between devices, per_device(): lax.all_to_all(parts, 'chan', split_axis=0, concat_axis=0, tiled=True)  4.3 us
    all_to_all x1, waiting for transfers between devices, per_device(): lax.all_to_all(parts, 'chan', split_axis=0, concat_axis=0, tiled=True)  3.93 us
    pallas_call x1, Pallas kernels, owner_emit(): pl.pallas_call(owner_emit_kernel, out_shape=jax.ShapeDtypeStruct((chunks,...  2.29 us
    pallas_call x1, Pallas kernels, gate(): pl.pallas_call(gate_kernel, out_shape=jax.ShapeDtypeStruct((shards, WORDS...  2.22 us
  transfers between devices with their start and end apart: 2, of which 2 were waited for; matrix products, arithmetic and copies ran while one was open for 0% of the time, Pallas kernels for 3%

profile of v7, /device:TPU:24, one launch (start us, length us, event | category | flops | bytes accessed | tf_op | source)
XLA Modules:
  0.0 87.8 jit_solution(5116800616852668485)
XLA Ops:
  0.6 2.2 %gate.1 = bf16[64,9,2,128]{3,2,1,0:T(2,128)(2,1)} custom-call(bf16[128,512]{1,0:T(8,128)(2,1)} %x1.1, bf16[128,512]{1,0:T(8,128)(2,1)} %x2.1, bf16[128,512]{1,0:T(8,128)(2,1)} %value.1, bf16[128,512]{1,0:T(8,128)(2,1)} %oh.1, f32[3,512]{1,0:T(4,128)} %weight.3), custom_call_target="tpu_custom_call" | custom-call | tf_op jit(solution)/shard_map/gate/pallas_call | solution.py:172
  2.9 0.0 copy-start.11
  2.9 0.0 copy-start.3
  2.9 0.0 copy-start.5
  2.9 0.0 copy-start.6
  2.9 0.0 copy-start.7
  2.9 0.0 copy-start.8
  2.9 0.0 copy-start.9
  2.9 18.9 %all-to-all-start = ((bf16[64,9,2,128]{3,2,1,0:T(2,128)(2,1)}), bf16[64,9,2,128]{3,2,1,0:T(2,128)(2,1)S(1)}, u32[]{:S(2)}, u32[]{:S(2)}) async-start(bf16[64,9,2,128]{3,2,1,0:T(2,128)(2,1)} %gate.1), calls=%async_computation | async-start | bytes 589824 | tf_op jit(solution)/shard_map/all_to_all | solution.py:443
  21.8 0.0 copy-start.4
  21.8 0.0 copy-done.11
  21.8 0.1 maximum_bitcast_fusion.rate
  21.9 0.0 copy-start.10
  21.9 0.0 copy-done.3
  21.9 0.0 copy-done.5
  21.9 0.0 copy-done.6
  21.9 0.0 copy-done.7
  21.9 0.0 copy-done.8
  21.9 0.0 copy-done.9
  21.9 0.6 copy-done.4
  22.5 0.1 copy-done.10
  22.6 1.1 %tables.1 = (bf16[256,512]{1,0:T(8,128)(2,1)S(1)}, bf16[256,512]{1,0:T(8,128)(2,1)S(1)}, bf16[128,128]{1,0:T(8,128)(2,1)S(1)}, bf16[128,128]{1,0:T(8,128)(2,1)S(...) custom-call(s32[1]{0:T(128)} %bitcast.place, f32[1,128]{1,0:T(1,128)S(1)} %maximum_bitcast_fusion.rate, ...), custom_call_target="tpu_custom_call" | custom-call | flops 4000000 | bytes 1000000 | tf_op jit(solution)/shard_map/tables/pallas_call | solution.py:108
  23.7 20.4 %all-to-all-done.got = bf16[64,9,2,128]{3,2,1,0:T(2,128)(2,1)S(1)} async-done(((bf16[64,9,2,128]{3,2,1,0:T(2,128)(2,1)}), bf16[64,9,2,128]{3,2,1,0:T(2,128)(2,1)S(1)}, u32[]{:S(2)}, u32[]{:S(2)}) %all-to-all-start) | async-done | bytes 294944 | tf_op jit(solution)/shard_map/all_to_all | solution.py:443
  44.0 2.3 %owner.1 = bf16[64,11,2,128]{3,2,1,0:T(2,128)(2,1)S(1)} custom-call(s32[1]{0:T(128)} %bitcast.place, bf16[64,9,2,128]{3,2,1,0:T(2,128)(2,1)S(1)} %all-to-all-done.got, bf16[256,512]{1,0:T(8,128)(2,1)S(1)} %get-tuple-element.15.tx, bf16[256,512]{1,0:T(8,128)(2,1)S(1)} %get-tuple-element.16.tg, bf16[128,128]{1,0:T(8,128)(2,1)S(1)} %get-tuple-element.17.mf, ...), custom_call_target="tpu_custom_call" | custom-call | tf_op jit(solution)/shard_map/owner/pallas_call | solution.py:352
  46.3 0.0 copy-start.2
  46.4 30.7 %all_to_all.22.back = bf16[64,11,2,128]{3,2,1,0:T(2,128)(2,1)S(1)} all-to-all(bf16[64,11,2,128]{3,2,1,0:T(2,128)(2,1)S(1)} %owner.1), channel_id=1, replica_groups=mesh['seq'=64,'chan'=8] {'seq'}, dimensions={0} | all-to-all | bytes 720896 | tf_op jit(solution)/shard_map/all_to_all | solution.py:445
  77.1 0.0 copy-start
  77.1 0.0 copy-start.1
  77.1 0.7 rates.1
  77.7 4.3 %all-to-all-start.2 = ((f32[8,1,128]{2,1,0:T(1,128)}), f32[8,1,128]{2,1,0:T(1,128)S(1)}, u32[]{:S(2)}, u32[]{:S(2)}) async-start(f32[8,1,128]{2,1,0:T(1,128)} %bitcast.3), calls=%async_computation.2 | async-start | bytes 8192 | tf_op jit(solution)/shard_map/all_to_all | solution.py:447
  82.0 0.0 copy-done.2
  82.0 0.0 copy-done
  82.0 0.0 copy-done.1
  82.1 1.3 %finish.1 = (bf16[128,512]{1,0:T(8,128)(2,1)}, bf16[128,512]{1,0:T(8,128)(2,1)}, bf16[128,512]{1,0:T(8,128)(2,1)}, f32[64,512]{1,0:T(8,128)}) custom-call(bf16[64,11,2,128]{3,2,1,0:T(2,128)(2,1)S(1)} %all_to_all.22.back, bf16[128,512]{1,0:T(8,128)(2,1)S(1)} %copy-done, bf16[128,512]{1,0:T(8,128)(2,1)S(1)} %copy-done.1, bf16[128,512]{1,0:T(8,128)(2,1)S(1)} %copy-done.2, ...), custom_call_target="tpu_custom_call" | custom-call | flops 4000000 | bytes 4000000 | tf_op jit(solution)/shard_map/finish/pallas_call | solution.py:422
  83.4 3.9 %all-to-all-done.2 = f32[8,1,128]{2,1,0:T(1,128)S(1)} async-done(((f32[8,1,128]{2,1,0:T(1,128)}), f32[8,1,128]{2,1,0:T(1,128)S(1)}, u32[]{:S(2)}, u32[]{:S(2)}) %all-to-all-start.2) | async-done | bytes 4128 | tf_op jit(solution)/shard_map/all_to_all | solution.py:447
  87.3 0.5 slice_reduce_fusion
Async XLA Ops:
  2.9 19.0 %copy-start.11 = (f32[64]{0:T(128)S(1)}, f32[64]{0:T(128)}, u32[]{:S(2)}) copy-start(f32[64]{0:T(128)} %param.19) | copy-start | bytes 772
  2.9 19.0 %copy-start.3 = (f32[64,512]{1,0:T(8,128)S(1)}, f32[64,512]{1,0:T(8,128)}, u32[]{:S(2)}) copy-start(f32[64,512]{1,0:T(8,128)} %coef.1) | copy-start | bytes 393220
  2.9 19.0 %copy-start.5 = (f32[128,128]{1,0:T(8,128)S(1)}, f32[128,128]{1,0:T(8,128)}, u32[]{:S(2)}) copy-start(f32[128,128]{1,0:T(8,128)} %constant.24.clone.wave) | copy-start | bytes 196612
  2.9 19.0 %copy-start.6 = (f32[128,128]{1,0:T(8,128)S(1)}, f32[128,128]{1,0:T(8,128)}, u32[]{:S(2)}) copy-start(f32[128,128]{1,0:T(8,128)} %constant.23.clone.imag_b) | copy-start | bytes 196612
  2.9 19.0 %copy-start.7 = (f32[128,128]{1,0:T(8,128)S(1)}, f32[128,128]{1,0:T(8,128)}, u32[]{:S(2)}) copy-start(f32[128,128]{1,0:T(8,128)} %constant.22.clone.real_b) | copy-start | bytes 196612
  2.9 19.0 %copy-start.8 = (f32[128,128]{1,0:T(8,128)S(1)}, f32[128,128]{1,0:T(8,128)}, u32[]{:S(2)}) copy-start(f32[128,128]{1,0:T(8,128)} %constant.21.clone.sin_a) | copy-start | bytes 196612
  2.9 19.0 %copy-start.9 = (f32[128,128]{1,0:T(8,128)S(1)}, f32[128,128]{1,0:T(8,128)}, u32[]{:S(2)}) copy-start(f32[128,128]{1,0:T(8,128)} %constant.20.clone.cos_a) | copy-start | bytes 196612
  2.9 41.1 %all-to-all-start = ((bf16[64,9,2,128]{3,2,1,0:T(2,128)(2,1)}), bf16[64,9,2,128]{3,2,1,0:T(2,128)(2,1)S(1)}, u32[]{:S(2)}, u32[]{:S(2)}) async-start(bf16[64,9,2,128]{3,2,1,0:T(2,128)(2,1)} %gate.1), calls=%async_computation | async-start | bytes 589824 | tf_op jit(solution)/shard_map/all_to_all | solution.py:443
  21.8 0.7 copy-start.4
  21.9 0.7 copy-start.10
  46.3 35.7 %copy-start.2 = (bf16[128,512]{1,0:T(8,128)(2,1)S(1)}, bf16[128,512]{1,0:T(8,128)(2,1)}, u32[]{:S(2)}) copy-start(bf16[128,512]{1,0:T(8,128)(2,1)} %value.1) | copy-start | bytes 393220
  77.1 5.0 %copy-start = (bf16[128,512]{1,0:T(8,128)(2,1)S(1)}, bf16[128,512]{1,0:T(8,128)(2,1)}, u32[]{:S(2)}) copy-start(bf16[128,512]{1,0:T(8,128)(2,1)} %x1.1) | copy-start | bytes 393220
  77.1 5.0 %copy-start.1 = (bf16[128,512]{1,0:T(8,128)(2,1)S(1)}, bf16[128,512]{1,0:T(8,128)(2,1)}, u32[]{:S(2)}) copy-start(bf16[128,512]{1,0:T(8,128)(2,1)} %x2.1) | copy-start | bytes 393220
  77.7 9.6 %all-to-all-start.2 = ((f32[8,1,128]{2,1,0:T(1,128)}), f32[8,1,128]{2,1,0:T(1,128)S(1)}, u32[]{:S(2)}, u32[]{:S(2)}) async-start(f32[8,1,128]{2,1,0:T(1,128)} %bitcast.3), calls=%async_computation.2 | async-start | bytes 8192 | tf_op jit(solution)/shard_map/all_to_all | solution.py:447

commit v8 on v6

--- a/solution.py
+++ b/solution.py
@@ -364,24 +364,40 @@
     )(place, got, *tables)
 
 
-def rate_kernel(back, parts):
+def rate_kernel(back, early, parts):
     flat = back.reshape(back.shape[0], BACK, ROWS)
     rates = jnp.sum(jnp.sum(flat[:, 2 * OWN + 4 :].astype(f32), axis=0), axis=0, keepdims=True)
     parts[...] = jnp.broadcast_to(rates, parts.shape)
 
 
-def rate_parts(back, peers):
+def rate_parts(back, early, peers):
     return pl.pallas_call(
         rate_kernel,
         out_shape=jax.ShapeDtypeStruct((peers, LANES), f32),
-        in_specs=[VMEM],
+        in_specs=[VMEM, pl.BlockSpec(memory_space=pl.ANY)],
         out_specs=VMEM,
         compiler_params=pltpu.CompilerParams(vmem_limit_bytes=8 << 20),
         name="rates",
-    )(back)
-
-
-def finish_kernel(back, x1, x2, value, weight, y, gx1, gvalue, gcoef):
+    )(back, early)
+
+
+def mix_kernel(value, weight, early):
+    early[...] = mix(value[...].astype(f32), jnp.zeros((2, value.shape[1]), f32), weight[...])
+
+
+def mix_early(value, weight):
+    return pl.pallas_call(
+        mix_kernel,
+        out_shape=jax.ShapeDtypeStruct(value.shape, f32),
+        in_specs=[VMEM] * 2,
+        out_specs=VMEM,
+        compiler_params=pltpu.CompilerParams(vmem_limit_bytes=12 << 20),
+        cost_estimate=pl.CostEstimate(flops=1_000_000, bytes_accessed=2_000_000, transcendentals=0),
+        name="mix",
+    )(value, weight)
+
+
+def finish_kernel(back, x1, x2, early, weight, y, gx1, gvalue, gcoef):
     shards = back.shape[0]
     wide = shards * OWN
     every = back.reshape(shards, BACK, ROWS)
@@ -402,7 +418,14 @@
     first = x1[...].astype(f32)
     w = weight[...]
     y[...] = (x2[...].astype(f32) * conv).astype(bf16)
-    mixed = mix(value[...].astype(f32), turned[ORDER + 2 : ORDER + 4], w)
+    prior = turned[ORDER + 2 : ORDER + 4]
+    position = lax.broadcasted_iota(jnp.int32, early.shape, 0)
+    mixed = early[...]
+    mixed = jnp.where(
+        position == 0,
+        mixed + w[1:2] * prior[1:2] + w[2:3] * prior[0:1],
+        jnp.where(position == 1, mixed + w[2:3] * prior[1:2], mixed),
+    )
     gx1[...] = (grad * mixed).astype(bf16)
     grad_mixed = grad * first
     after = turned[ORDER : ORDER + 2]
@@ -416,7 +439,7 @@
     gvalue[...] = (w[0:1] * grad_mixed + w[1:2] * one + w[2:3] * two).astype(bf16)
 
 
-def finish(back, x1, x2, value, weight):
+def finish(back, x1, x2, early, weight):
     shape = jax.ShapeDtypeStruct(x1.shape, bf16)
     return pl.pallas_call(
         finish_kernel,
@@ -431,7 +454,7 @@
         compiler_params=pltpu.CompilerParams(vmem_limit_bytes=16 << 20),
         cost_estimate=pl.CostEstimate(flops=4_000_000, bytes_accessed=4_000_000, transcendentals=0),
         name="finish",
-    )(back, x1, x2, value, weight)
+    )(back, x1, x2, early, weight)
 
 
 def per_device(x1, x2, value, out_grad, short_weight, coef, rate):
@@ -441,10 +464,12 @@
     sent = gate(x1, x2, value, out_grad, short_weight)
     got = lax.all_to_all(sent, "seq", split_axis=0, concat_axis=0, tiled=True)
     done = owner_emit(place, got, tables)
+    late, done = lax.optimization_barrier((value, done))
+    early = mix_early(late, short_weight)
     back = lax.all_to_all(done, "seq", split_axis=0, concat_axis=0, tiled=True)
-    parts = rate_parts(back, peers)
+    parts = rate_parts(back, early, peers)
     parts = lax.all_to_all(parts, "chan", split_axis=0, concat_axis=0, tiled=True)
-    y, gx1, gvalue, gcoef = finish(back, x1, x2, value, short_weight)
+    y, gx1, gvalue, gcoef = finish(back, x1, x2, early, short_weight)
     grate = jnp.sum(parts[:, :ORDER], axis=0) * (LENGTH * x1.shape[1] * peers) ** -0.5
     return (y, gx1, gvalue, gcoef, grate)
 

time: 89.1 us -> 90.1 us (1.011)
  blocking collectives: 30.7 us -> 0 us
  waiting for transfers between devices: 24.3 us -> 48.5 us
  starting transfers between devices: 23.2 us -> 29.8 us
    all_to_all x1 -> x0, blocking collectives: 30.7 us -> none  [per_device(): back = lax.all_to_all(done, 'seq', split_axis=0, concat_axis=0, tiled=True)]
    all_to_all x0 -> x1, waiting for transfers between devices: none -> 24.1 us  [per_device(): back = lax.all_to_all(done, 'seq', split_axis=0, concat_axis=0, tiled=True)]
    all_to_all x0 -> x1, starting transfers between devices: none -> 6.7 us  [per_device(): back = lax.all_to_all(done, 'seq', split_axis=0, concat_axis=0, tiled=True)]
  transfers between devices with their start and end apart: 2 -> 3, of which waited for: 2 -> 3; matrix products, arithmetic and copies ran while one was open for 0% -> 0% of each run, Pallas kernels for 3% -> 3%
where the time goes in v8:
time: 90.1 us; the launch traced here: 88.8 us
  waiting for transfers between devices  48.5 us (54%)
  starting transfers between devices  29.8 us (33%)
  Pallas kernels  8.34 us (9%)
    all_to_all x1, waiting for transfers between devices, per_device(): back = lax.all_to_all(done, 'seq', split_axis=0, concat_axis=0, tiled=True)  24.1 us
    all_to_all x1, waiting for transfers between devices, per_device(): got = lax.all_to_all(sent, 'seq', split_axis=0, concat_axis=0, tiled=True)  20.4 us
    all_to_all x1, starting transfers between devices, per_device(): got = lax.all_to_all(sent, 'seq', split_axis=0, concat_axis=0, tiled=True)  18.9 us
    all_to_all x1, starting transfers between devices, per_device(): back = lax.all_to_all(done, 'seq', split_axis=0, concat_axis=0, tiled=True)  6.7 us
    all_to_all x1, starting transfers between devices, per_device(): lax.all_to_all(parts, 'chan', split_axis=0, concat_axis=0, tiled=True)  4.3 us
    all_to_all x1, waiting for transfers between devices, per_device(): lax.all_to_all(parts, 'chan', split_axis=0, concat_axis=0, tiled=True)  4.03 us
    pallas_call x1, Pallas kernels, owner_emit(): pl.pallas_call(owner_emit_kernel, out_shape=jax.ShapeDtypeStruct((chunks,...  3.03 us
    pallas_call x1, Pallas kernels, gate(): pl.pallas_call(gate_kernel, out_shape=jax.ShapeDtypeStruct((shards, WORDS...  2.22 us
  transfers between devices with their start and end apart: 3, of which 3 were waited for; matrix products, arithmetic and copies ran while one was open for 0% of the time, Pallas kernels for 3%

profile of v8, /device:TPU:24, one launch (start us, length us, event | category | flops | bytes accessed | tf_op | source)
XLA Modules:
  0.0 88.8 jit_solution(8971986767866021085)
XLA Ops:
  0.6 2.2 %gate.1 = bf16[64,9,2,128]{3,2,1,0:T(2,128)(2,1)} custom-call(bf16[128,512]{1,0:T(8,128)(2,1)} %x1.1, bf16[128,512]{1,0:T(8,128)(2,1)} %x2.1, bf16[128,512]{1,0:T(8,128)(2,1)} %value, bf16[128,512]{1,0:T(8,128)(2,1)} %oh.1, f32[3,512]{1,0:T(4,128)} %weight.5), custom_call_target="tpu_custom_call" | custom-call | tf_op jit(solution)/shard_map/gate/pallas_call | solution.py:172
  2.9 0.0 copy-start.11
  2.9 0.0 copy-start.4
  2.9 0.0 copy-start.5
  2.9 0.0 copy-start.6
  2.9 0.0 copy-start.7
  2.9 0.0 copy-start.8
  2.9 0.0 copy-start.9
  3.0 18.9 %all-to-all-start = ((bf16[64,9,2,128]{3,2,1,0:T(2,128)(2,1)}), bf16[64,9,2,128]{3,2,1,0:T(2,128)(2,1)S(1)}, u32[]{:S(2)}, u32[]{:S(2)}) async-start(bf16[64,9,2,128]{3,2,1,0:T(2,128)(2,1)} %gate.1), calls=%async_computation | async-start | bytes 589824 | tf_op jit(solution)/shard_map/all_to_all | solution.py:465
  21.8 0.0 copy-start.3
  21.8 0.0 copy-done.11
  21.8 0.1 maximum_bitcast_fusion.rate
  21.9 0.0 copy-start.10
  21.9 0.0 copy-done.4
  21.9 0.0 copy-done.5
  21.9 0.0 copy-done.6
  21.9 0.0 copy-done.7
  21.9 0.0 copy-done.8
  21.9 0.0 copy-done.9
  22.0 0.6 copy-done.3
  22.5 0.1 copy-done.10
  22.6 1.1 %tables.1 = (bf16[256,512]{1,0:T(8,128)(2,1)S(1)}, bf16[256,512]{1,0:T(8,128)(2,1)S(1)}, bf16[128,128]{1,0:T(8,128)(2,1)S(1)}, bf16[128,128]{1,0:T(8,128)(2,1)S(...) custom-call(s32[1]{0:T(128)} %bitcast.place, f32[1,128]{1,0:T(1,128)S(1)} %maximum_bitcast_fusion.rate, ...), custom_call_target="tpu_custom_call" | custom-call | flops 4000000 | bytes 1000000 | tf_op jit(solution)/shard_map/tables/pallas_call | solution.py:108
  23.7 20.4 %all-to-all-done.got = bf16[64,9,2,128]{3,2,1,0:T(2,128)(2,1)S(1)} async-done(((bf16[64,9,2,128]{3,2,1,0:T(2,128)(2,1)}), bf16[64,9,2,128]{3,2,1,0:T(2,128)(2,1)S(1)}, u32[]{:S(2)}, u32[]{:S(2)}) %all-to-all-start) | async-done | bytes 294944 | tf_op jit(solution)/shard_map/all_to_all | solution.py:465
  44.1 3.0 %owner.1 = bf16[64,11,2,128]{3,2,1,0:T(2,128)(2,1)} custom-call(s32[1]{0:T(128)} %bitcast.place, bf16[64,9,2,128]{3,2,1,0:T(2,128)(2,1)S(1)} %all-to-all-done.got, bf16[256,512]{1,0:T(8,128)(2,1)S(1)} %get-tuple-element.17.tx, bf16[256,512]{1,0:T(8,128)(2,1)S(1)} %get-tuple-element.18.tg, bf16[128,128]{1,0:T(8,128)(2,1)S(1)} %get-tuple-element.19.mf, ...), custom_call_target="tpu_custom_call" | custom-call | tf_op jit(solution)/shard_map/owner/pallas_call | solution.py:352
  47.1 0.0 copy-start
  47.1 6.7 %all-to-all-start.1 = ((bf16[64,11,2,128]{3,2,1,0:T(2,128)(2,1)}), bf16[64,11,2,128]{3,2,1,0:T(2,128)(2,1)S(1)}, u32[]{:S(2)}, u32[]{:S(2)}) async-start(bf16[64,11,2,128]{3,2,1,0:T(2,128)(2,1)} %owner.1), calls=%async_computation.1 | async-start | bytes 720896 | tf_op jit(solution)/shard_map/all_to_all | solution.py:469
  53.8 0.0 copy-done
  53.8 0.1 mix.1.early
  53.9 0.0 copy-start.1
  53.9 0.0 copy-start.2
  53.9 24.1 %all-to-all-done.1.back = bf16[64,11,2,128]{3,2,1,0:T(2,128)(2,1)S(1)} async-done(((bf16[64,11,2,128]{3,2,1,0:T(2,128)(2,1)}), bf16[64,11,2,128]{3,2,1,0:T(2,128)(2,1)S(1)}, u32[]{:S(2)}, u32[]{:S(2)}) %all-to-all-start.1) | async-done | bytes 360480 | tf_op jit(solution)/shard_map/all_to_all | solution.py:469
  78.0 0.7 rates.1
  78.7 4.3 %all-to-all-start.2 = ((f32[8,1,128]{2,1,0:T(1,128)}), f32[8,1,128]{2,1,0:T(1,128)S(1)}, u32[]{:S(2)}, u32[]{:S(2)}) async-start(f32[8,1,128]{2,1,0:T(1,128)} %bitcast.3), calls=%async_computation.2 | async-start | bytes 8192 | tf_op jit(solution)/shard_map/all_to_all | solution.py:471
  83.0 0.0 copy-done.1
  83.0 0.0 copy-done.2
  83.0 1.2 %finish.1 = (bf16[128,512]{1,0:T(8,128)(2,1)}, bf16[128,512]{1,0:T(8,128)(2,1)}, bf16[128,512]{1,0:T(8,128)(2,1)}, f32[64,512]{1,0:T(8,128)}) custom-call(bf16[64,11,2,128]{3,2,1,0:T(2,128)(2,1)S(1)} %all-to-all-done.1.back, bf16[128,512]{1,0:T(8,128)(2,1)S(1)} %copy-done.1, bf16[128,512]{1,0:T(8,128)(2,1)S(1)} %copy-done.2, f32[128,512]{1,0:T(8,128)S(1)} %mix.1.early, ...), custom_call_target="tpu_custom_call" | custom-call | flops 4000000 | bytes 4000000 | tf_op jit(solution)/shard_map/finish/pallas_call | solution.py:444
  84.2 4.0 %all-to-all-done.2 = f32[8,1,128]{2,1,0:T(1,128)S(1)} async-done(((f32[8,1,128]{2,1,0:T(1,128)}), f32[8,1,128]{2,1,0:T(1,128)S(1)}, u32[]{:S(2)}, u32[]{:S(2)}) %all-to-all-start.2) | async-done | bytes 4128 | tf_op jit(solution)/shard_map/all_to_all | solution.py:471
  88.2 0.5 broadcast_multiply_fusion
  (1 shorter events, 0.0 us)
Async XLA Ops:
  2.9 19.0 %copy-start.11 = (f32[64]{0:T(128)S(1)}, f32[64]{0:T(128)}, u32[]{:S(2)}) copy-start(f32[64]{0:T(128)} %param.19) | copy-start | bytes 772
  2.9 19.0 %copy-start.4 = (f32[64,512]{1,0:T(8,128)S(1)}, f32[64,512]{1,0:T(8,128)}, u32[]{:S(2)}) copy-start(f32[64,512]{1,0:T(8,128)} %coef.1) | copy-start | bytes 393220
  2.9 19.0 %copy-start.5 = (f32[128,128]{1,0:T(8,128)S(1)}, f32[128,128]{1,0:T(8,128)}, u32[]{:S(2)}) copy-start(f32[128,128]{1,0:T(8,128)} %constant.26.clone.wave) | copy-start | bytes 196612
  2.9 19.0 %copy-start.6 = (f32[128,128]{1,0:T(8,128)S(1)}, f32[128,128]{1,0:T(8,128)}, u32[]{:S(2)}) copy-start(f32[128,128]{1,0:T(8,128)} %constant.25.clone.imag_b) | copy-start | bytes 196612
  2.9 19.0 %copy-start.7 = (f32[128,128]{1,0:T(8,128)S(1)}, f32[128,128]{1,0:T(8,128)}, u32[]{:S(2)}) copy-start(f32[128,128]{1,0:T(8,128)} %constant.24.clone.real_b) | copy-start | bytes 196612
  2.9 19.0 %copy-start.8 = (f32[128,128]{1,0:T(8,128)S(1)}, f32[128,128]{1,0:T(8,128)}, u32[]{:S(2)}) copy-start(f32[128,128]{1,0:T(8,128)} %constant.23.clone.sin_a) | copy-start | bytes 196612
  2.9 19.0 %copy-start.9 = (f32[128,128]{1,0:T(8,128)S(1)}, f32[128,128]{1,0:T(8,128)}, u32[]{:S(2)}) copy-start(f32[128,128]{1,0:T(8,128)} %constant.22.clone.cos_a) | copy-start | bytes 196612
  3.0 41.1 %all-to-all-start = ((bf16[64,9,2,128]{3,2,1,0:T(2,128)(2,1)}), bf16[64,9,2,128]{3,2,1,0:T(2,128)(2,1)S(1)}, u32[]{:S(2)}, u32[]{:S(2)}) async-start(bf16[64,9,2,128]{3,2,1,0:T(2,128)(2,1)} %gate.1), calls=%async_computation | async-start | bytes 589824 | tf_op jit(solution)/shard_map/all_to_all | solution.py:465
  21.8 0.7 copy-start.3
  21.9 0.7 copy-start.10
  47.1 6.7 %copy-start = (bf16[128,512]{1,0:T(8,128)(2,1)S(1)}, bf16[128,512]{1,0:T(8,128)(2,1)}, u32[]{:S(2)}) copy-start(bf16[128,512]{1,0:T(8,128)(2,1)} %value) | copy-start | bytes 393220
  47.1 30.9 %all-to-all-start.1 = ((bf16[64,11,2,128]{3,2,1,0:T(2,128)(2,1)}), bf16[64,11,2,128]{3,2,1,0:T(2,128)(2,1)S(1)}, u32[]{:S(2)}, u32[]{:S(2)}) async-start(bf16[64,11,2,128]{3,2,1,0:T(2,128)(2,1)} %owner.1), calls=%async_computation.1 | async-start | bytes 720896 | tf_op jit(solution)/shard_map/all_to_all | solution.py:469
  53.9 29.1 %copy-start.1 = (bf16[128,512]{1,0:T(8,128)(2,1)S(1)}, bf16[128,512]{1,0:T(8,128)(2,1)}, u32[]{:S(2)}) copy-start(bf16[128,512]{1,0:T(8,128)(2,1)} %x1.1) | copy-start | bytes 393220
  53.9 29.1 %copy-start.2 = (bf16[128,512]{1,0:T(8,128)(2,1)S(1)}, bf16[128,512]{1,0:T(8,128)(2,1)}, u32[]{:S(2)}) copy-start(bf16[128,512]{1,0:T(8,128)(2,1)} %x2.1) | copy-start | bytes 393220
  78.7 9.6 %all-to-all-start.2 = ((f32[8,1,128]{2,1,0:T(1,128)}), f32[8,1,128]{2,1,0:T(1,128)S(1)}, u32[]{:S(2)}, u32[]{:S(2)}) async-start(f32[8,1,128]{2,1,0:T(1,128)} %bitcast.3), calls=%async_computation.2 | async-start | bytes 8192 | tf_op jit(solution)/shard_map/all_to_all | solution.py:471

commit v9 on v6

--- a/solution.py
+++ b/solution.py
@@ -289,7 +289,6 @@
         return array.reshape(chunks, OWN, LANES)
 
     xs[...] = xb[...].astype(f32)
-    gs[...] = got.reshape(chunks, WORDS, ROWS)[:, : 2 * OWN].astype(f32)[:, OWN:].reshape(rows, ROWS)
     yc[...] = lax.dot_general(us[...], mf[...], NT, preferred_element_type=f32)
     yg[...] = lax.dot_general(ug[...], me[...], NT, preferred_element_type=f32)
     here = lax.broadcasted_iota(jnp.int32, (ROWS, ROWS), 0)

time: 89.1 us -> 89.1 us (level)
  no operation moved by 1% of the time
where the time goes in v9:
time: 89.1 us; the launch traced here: 87.8 us
  blocking collectives  30.7 us (34%)
  waiting for transfers between devices  24.3 us (27%)
  starting transfers between devices  23.1 us (26%)
  Pallas kernels  7.52 us (8%)
    all_to_all x1, blocking collectives, per_device(): back = lax.all_to_all(done, 'seq', split_axis=0, concat_axis=0, tiled=True)  30.7 us
    all_to_all x1, waiting for transfers between devices, per_device(): got = lax.all_to_all(sent, 'seq', split_axis=0, concat_axis=0, tiled=True)  20.4 us
    all_to_all x1, starting transfers between devices, per_device(): got = lax.all_to_all(sent, 'seq', split_axis=0, concat_axis=0, tiled=True)  18.9 us
    all_to_all x1, starting transfers between devices, per_device(): lax.all_to_all(parts, 'chan', split_axis=0, concat_axis=0, tiled=True)  4.3 us
    all_to_all x1, waiting for transfers between devices, per_device(): lax.all_to_all(parts, 'chan', split_axis=0, concat_axis=0, tiled=True)  3.93 us
    pallas_call x1, Pallas kernels, owner_emit(): pl.pallas_call(owner_emit_kernel, out_shape=jax.ShapeDtypeStruct((chunks,...  2.22 us
    pallas_call x1, Pallas kernels, gate(): pl.pallas_call(gate_kernel, out_shape=jax.ShapeDtypeStruct((shards, WORDS...  2.22 us
  transfers between devices with their start and end apart: 2, of which 2 were waited for; matrix products, arithmetic and copies ran while one was open for 0% of the time, Pallas kernels for 3%

profile of v9, /device:TPU:24, one launch (start us, length us, event | category | flops | bytes accessed | tf_op | source)
XLA Modules:
  0.0 87.8 jit_solution(15585526575799257297)
XLA Ops:
  0.6 2.2 %gate.1 = bf16[64,9,2,128]{3,2,1,0:T(2,128)(2,1)} custom-call(bf16[128,512]{1,0:T(8,128)(2,1)} %x1.1, bf16[128,512]{1,0:T(8,128)(2,1)} %x2.1, bf16[128,512]{1,0:T(8,128)(2,1)} %value.1, bf16[128,512]{1,0:T(8,128)(2,1)} %oh.1, f32[3,512]{1,0:T(4,128)} %weight.3), custom_call_target="tpu_custom_call" | custom-call | tf_op jit(solution)/shard_map/gate/pallas_call | solution.py:172
  2.9 0.0 copy-start.11
  2.9 0.0 copy-start.3
  2.9 0.0 copy-start.5
  2.9 0.0 copy-start.6
  2.9 0.0 copy-start.7
  2.9 0.0 copy-start.8
  2.9 0.0 copy-start.9
  2.9 18.9 %all-to-all-start = ((bf16[64,9,2,128]{3,2,1,0:T(2,128)(2,1)}), bf16[64,9,2,128]{3,2,1,0:T(2,128)(2,1)S(1)}, u32[]{:S(2)}, u32[]{:S(2)}) async-start(bf16[64,9,2,128]{3,2,1,0:T(2,128)(2,1)} %gate.1), calls=%async_computation | async-start | bytes 589824 | tf_op jit(solution)/shard_map/all_to_all | solution.py:441
  21.8 0.0 copy-start.4
  21.8 0.0 copy-done.11
  21.8 0.1 maximum_bitcast_fusion.rate
  21.9 0.0 copy-start.10
  21.9 0.0 copy-done.3
  21.9 0.0 copy-done.5
  21.9 0.0 copy-done.6
  21.9 0.0 copy-done.7
  21.9 0.0 copy-done.8
  21.9 0.0 copy-done.9
  21.9 0.6 copy-done.4
  22.5 0.1 copy-done.10
  22.6 1.1 %tables.1 = (bf16[256,512]{1,0:T(8,128)(2,1)S(1)}, bf16[256,512]{1,0:T(8,128)(2,1)S(1)}, bf16[128,128]{1,0:T(8,128)(2,1)S(1)}, bf16[128,128]{1,0:T(8,128)(2,1)S(...) custom-call(s32[1]{0:T(128)} %bitcast.place, f32[1,128]{1,0:T(1,128)S(1)} %maximum_bitcast_fusion.rate, ...), custom_call_target="tpu_custom_call" | custom-call | flops 4000000 | bytes 1000000 | tf_op jit(solution)/shard_map/tables/pallas_call | solution.py:108
  23.7 20.4 %all-to-all-done.got = bf16[64,9,2,128]{3,2,1,0:T(2,128)(2,1)S(1)} async-done(((bf16[64,9,2,128]{3,2,1,0:T(2,128)(2,1)}), bf16[64,9,2,128]{3,2,1,0:T(2,128)(2,1)S(1)}, u32[]{:S(2)}, u32[]{:S(2)}) %all-to-all-start) | async-done | bytes 294944 | tf_op jit(solution)/shard_map/all_to_all | solution.py:441
  44.0 2.2 %owner.1 = bf16[64,11,2,128]{3,2,1,0:T(2,128)(2,1)S(1)} custom-call(s32[1]{0:T(128)} %bitcast.place, bf16[64,9,2,128]{3,2,1,0:T(2,128)(2,1)S(1)} %all-to-all-done.got, bf16[256,512]{1,0:T(8,128)(2,1)S(1)} %get-tuple-element.15.tx, bf16[256,512]{1,0:T(8,128)(2,1)S(1)} %get-tuple-element.16.tg, bf16[128,128]{1,0:T(8,128)(2,1)S(1)} %get-tuple-element.17.mf, ...), custom_call_target="tpu_custom_call" | custom-call | tf_op jit(solution)/shard_map/owner/pallas_call | solution.py:351
  46.3 0.0 copy-start.2
  46.3 30.7 %all_to_all.22.back = bf16[64,11,2,128]{3,2,1,0:T(2,128)(2,1)S(1)} all-to-all(bf16[64,11,2,128]{3,2,1,0:T(2,128)(2,1)S(1)} %owner.1), channel_id=1, replica_groups=mesh['seq'=64,'chan'=8] {'seq'}, dimensions={0} | all-to-all | bytes 720896 | tf_op jit(solution)/shard_map/all_to_all | solution.py:443
  77.0 0.0 copy-start
  77.0 0.0 copy-start.1
  77.0 0.7 rates.1
  77.7 4.3 %all-to-all-start.2 = ((f32[8,1,128]{2,1,0:T(1,128)}), f32[8,1,128]{2,1,0:T(1,128)S(1)}, u32[]{:S(2)}, u32[]{:S(2)}) async-start(f32[8,1,128]{2,1,0:T(1,128)} %bitcast.3), calls=%async_computation.2 | async-start | bytes 8192 | tf_op jit(solution)/shard_map/all_to_all | solution.py:445
  82.0 0.0 copy-done.2
  82.0 0.0 copy-done
  82.0 0.0 copy-done.1
  82.0 1.3 %finish.1 = (bf16[128,512]{1,0:T(8,128)(2,1)}, bf16[128,512]{1,0:T(8,128)(2,1)}, bf16[128,512]{1,0:T(8,128)(2,1)}, f32[64,512]{1,0:T(8,128)}) custom-call(bf16[64,11,2,128]{3,2,1,0:T(2,128)(2,1)S(1)} %all_to_all.22.back, bf16[128,512]{1,0:T(8,128)(2,1)S(1)} %copy-done, bf16[128,512]{1,0:T(8,128)(2,1)S(1)} %copy-done.1, bf16[128,512]{1,0:T(8,128)(2,1)S(1)} %copy-done.2, ...), custom_call_target="tpu_custom_call" | custom-call | flops 4000000 | bytes 4000000 | tf_op jit(solution)/shard_map/finish/pallas_call | solution.py:420
  83.3 3.9 %all-to-all-done.2 = f32[8,1,128]{2,1,0:T(1,128)S(1)} async-done(((f32[8,1,128]{2,1,0:T(1,128)}), f32[8,1,128]{2,1,0:T(1,128)S(1)}, u32[]{:S(2)}, u32[]{:S(2)}) %all-to-all-start.2) | async-done | bytes 4128 | tf_op jit(solution)/shard_map/all_to_all | solution.py:445
  87.2 0.5 broadcast_multiply_fusion
  (1 shorter events, 0.0 us)
Async XLA Ops:
  2.9 19.0 %copy-start.11 = (f32[64]{0:T(128)S(1)}, f32[64]{0:T(128)}, u32[]{:S(2)}) copy-start(f32[64]{0:T(128)} %param.19) | copy-start | bytes 772
  2.9 19.0 %copy-start.3 = (f32[64,512]{1,0:T(8,128)S(1)}, f32[64,512]{1,0:T(8,128)}, u32[]{:S(2)}) copy-start(f32[64,512]{1,0:T(8,128)} %coef.1) | copy-start | bytes 393220
  2.9 19.0 %copy-start.5 = (f32[128,128]{1,0:T(8,128)S(1)}, f32[128,128]{1,0:T(8,128)}, u32[]{:S(2)}) copy-start(f32[128,128]{1,0:T(8,128)} %constant.26.clone.wave) | copy-start | bytes 196612
  2.9 19.0 %copy-start.6 = (f32[128,128]{1,0:T(8,128)S(1)}, f32[128,128]{1,0:T(8,128)}, u32[]{:S(2)}) copy-start(f32[128,128]{1,0:T(8,128)} %constant.25.clone.imag_b) | copy-start | bytes 196612
  2.9 19.0 %copy-start.7 = (f32[128,128]{1,0:T(8,128)S(1)}, f32[128,128]{1,0:T(8,128)}, u32[]{:S(2)}) copy-start(f32[128,128]{1,0:T(8,128)} %constant.24.clone.real_b) | copy-start | bytes 196612
  2.9 19.0 %copy-start.8 = (f32[128,128]{1,0:T(8,128)S(1)}, f32[128,128]{1,0:T(8,128)}, u32[]{:S(2)}) copy-start(f32[128,128]{1,0:T(8,128)} %constant.23.clone.sin_a) | copy-start | bytes 196612
  2.9 19.0 %copy-start.9 = (f32[128,128]{1,0:T(8,128)S(1)}, f32[128,128]{1,0:T(8,128)}, u32[]{:S(2)}) copy-start(f32[128,128]{1,0:T(8,128)} %constant.22.clone.cos_a) | copy-start | bytes 196612
  2.9 41.1 %all-to-all-start = ((bf16[64,9,2,128]{3,2,1,0:T(2,128)(2,1)}), bf16[64,9,2,128]{3,2,1,0:T(2,128)(2,1)S(1)}, u32[]{:S(2)}, u32[]{:S(2)}) async-start(bf16[64,9,2,128]{3,2,1,0:T(2,128)(2,1)} %gate.1), calls=%async_computation | async-start | bytes 589824 | tf_op jit(solution)/shard_map/all_to_all | solution.py:441
  21.8 0.7 copy-start.4
  21.9 0.7 copy-start.10
  46.3 35.7 %copy-start.2 = (bf16[128,512]{1,0:T(8,128)(2,1)S(1)}, bf16[128,512]{1,0:T(8,128)(2,1)}, u32[]{:S(2)}) copy-start(bf16[128,512]{1,0:T(8,128)(2,1)} %value.1) | copy-start | bytes 393220
  77.0 5.0 %copy-start = (bf16[128,512]{1,0:T(8,128)(2,1)S(1)}, bf16[128,512]{1,0:T(8,128)(2,1)}, u32[]{:S(2)}) copy-start(bf16[128,512]{1,0:T(8,128)(2,1)} %x1.1) | copy-start | bytes 393220
  77.0 5.0 %copy-start.1 = (bf16[128,512]{1,0:T(8,128)(2,1)S(1)}, bf16[128,512]{1,0:T(8,128)(2,1)}, u32[]{:S(2)}) copy-start(bf16[128,512]{1,0:T(8,128)(2,1)} %x2.1) | copy-start | bytes 393220
  77.7 9.6 %all-to-all-start.2 = ((f32[8,1,128]{2,1,0:T(1,128)}), f32[8,1,128]{2,1,0:T(1,128)S(1)}, u32[]{:S(2)}, u32[]{:S(2)}) async-start(f32[8,1,128]{2,1,0:T(1,128)} %bitcast.3), calls=%async_computation.2 | async-start | bytes 8192 | tf_op jit(solution)/shard_map/all_to_all | solution.py:445
